TPU v7x, 256 devices: a whole 4x4x8 slice. The times are simulated.
256 devices in a mesh: lon: 64 (over x, y_lo, z), lat: 4 (over y_hi, core).
Axes of the slice: x: 4, y: 4 (y_hi: 2, y_lo: 2; y = y_hi * 2 + y_lo), z: 8, core: 2. Of those that a mesh axis runs over, the one named last changes fastest.
Arguments:
- features: bfloat16 [4, 24, 768, 512], P(None, 'lat', 'lon'), may hold values from -6 to 6
- norm_gain: float32 [512], replicated, may hold values from 0.1 to 1.9
- qkv_weight: bfloat16 [512, 1536], replicated, may hold values from -0.25 to 0.25
- proj_weight: bfloat16 [512, 512], replicated, may hold values from -0.25 to 0.25
- bias_table: float32 [8, 759], replicated, may hold values from -4 to 4
- merge_gain: float32 [2048], replicated, may hold values from 0.1 to 1.9
- merge_weight: bfloat16 [2048, 1024], replicated, may hold values from -0.125 to 0.125
- merged_cot: bfloat16 [4, 12, 384, 1024], P(None, 'lat', 'lon'), may hold values from -6 to 6
Outputs:
- merged: bfloat16 [4, 12, 384, 1024], P(None, 'lat', 'lon')
- features_grad: bfloat16 [4, 24, 768, 512], P(None, 'lat', 'lon')
- qkv_grad: float32 [512, 1536], P('lon', 'lat')
- proj_grad: float32 [512, 512], P('lon', 'lat')
- merge_grad: float32 [2048, 1024], P('lon', 'lat')
- norm_gain_grad: float32 [512], replicated
- merge_gain_grad: float32 [2048], replicated
- bias_grad: float32 [8, 759], replicated
All inputs are finite; a program needn't handle non-finite values.
Results may differ from a plain program's by a relative error of at most 0.025.
Values may be sent and summed in bfloat16 or wider, within the bound.
No kernel may reach another device: no remote copies, remote signals or barrier semaphores. Data moves between devices by JAX's collectives and lax.ppermute only.
A program may use at most 128 MiB of HBM per device.

v0:
```python
import functools

import jax
import jax.numpy as jnp
import numpy as np
from jax import lax
from jax.experimental import pallas as pl
from jax.experimental.pallas import tpu as pltpu
from jax.sharding import Mesh
from jax.sharding import PartitionSpec as P

EPSILON = 1e-05
MASKED = -1000000000.0
HEADS, LEV, ROWS, COLS = 8, 4, 6, 12
WIN = 144
TOK = 288
HALF_LON, HALF_LAT = 6, 3
SPAN = 384
TABLE = 759
AXES = ("x", "yl", "z", "yh", "c")
LON, LAT = ("x", "yl", "z"), ("yh", "c")
CORE, NEAR, FAR = ("c",), ("x", "yl"), ("z", "yh")
BF, F32 = jnp.bfloat16, jnp.float32


def token(w, l, r, c):
    return w * WIN + l * 72 + r * 12 + c


def level_of(w, l):
    return (2 * w + l + 1) % LEV


def plans():
    own = np.zeros((TOK, TOK)); west = np.zeros((TOK, 144)); south = np.zeros((TOK, 144))
    back = np.zeros((TOK, TOK))
    quad_own = np.zeros((4 * 96, TOK)); quad_prev = np.zeros((4 * 96, 48)); quad_next = np.zeros((4 * 96, 48))
    edge = np.zeros((96, TOK))
    for w in range(2):
        for l in range(2):
            lev, s = level_of(w, l), 2 * w + l
            for r in range(ROWS):
                for c in range(COLS):
                    t = token(w, l, r, c)
                    i, j = r + HALF_LAT, c + HALF_LON
                    if i >= ROWS:
                        south[t, ((i - ROWS) * COLS + c) * LEV + lev] = 1
                    elif j >= COLS:
                        west[t, (i * HALF_LON + j - COLS) * LEV + lev] = 1
                    else:
                        own[t, (i * COLS + j) * LEV + lev] = 1
                    back[(r * COLS + c) * LEV + lev, t] = 1
                    dj, pc = c % 2, c // 2
                    if r % 2:
                        di, pr = 0, (r + 1) // 2
                    else:
                        di, pr = 1, r // 2
                    quad_own[(dj * 2 + di) * 96 + pr * 24 + s * 6 + pc, t] = 1
                    if r == 0:
                        edge[s * 12 + c, t] = 1
                    if r == ROWS - 1:
                        edge[48 + s * 12 + c, t] = 1
            for c in range(COLS):
                dj, pc = c % 2, c // 2
                quad_prev[(dj * 2 + 0) * 96 + 0 * 24 + s * 6 + pc, s * 12 + c] = 1
                quad_next[(dj * 2 + 1) * 96 + 3 * 24 + s * 6 + pc, s * 12 + c] = 1
    cot_own = np.zeros((96, 72)); cot_west = np.zeros((96, 36)); cot_south = np.zeros((96, 48))
    coarse = np.zeros((72, 96))
    for pr in range(4):
        for s in range(LEV):
            lev = (s + 1) % LEV
            for pc in range(6):
                p = pr * 24 + s * 6 + pc
                i, j = pr + 1, pc + 3
                if i >= 3:
                    cot_south[p, ((i - 3) * 6 + pc) * LEV + lev] = 1
                elif j >= 6:
                    cot_west[p, (i * 3 + j - 6) * LEV + lev] = 1
                else:
                    cot_own[p, (i * 6 + j) * LEV + lev] = 1
                if pr < 3:
                    coarse[(pr * 6 + pc) * LEV + lev, p] = 1
    place = np.zeros(WIN, np.int64)
    for l in range(2):
        for r in range(ROWS):
            for c in range(COLS):
                place[l * 72 + r * 12 + c] = l * 253 + r * 23 + c
    spread = np.zeros((SPAN, 256))
    spread[379 - place, np.arange(WIN)] = 1
    level = np.arange(WIN) // 72
    north = (np.arange(WIN) % 72) // 12 >= HALF_LAT
    return dict(
        own=own, west=west, south=south, back=back, quad_own=quad_own, quad_prev=quad_prev,
        quad_next=quad_next, quad_t=quad_own.T, edge=edge, cot_own=cot_own, cot_west=cot_west,
        cot_south=cot_south, coarse=coarse, spread=spread, spread_t=spread.T,
        apart_level=(level[:, None] != level[None]) * 1.0,
        apart_north=(north[:, None] != north[None]) * 1.0,
    ), [int(v) for v in place]


PLAN, PLACE = plans()


def plan(name):
    return jnp.asarray(PLAN[name], BF)


def mm(a, b):
    return jnp.dot(a, b, preferred_element_type=F32)


def mm_nt(a, b):
    return lax.dot_general(a, b, (((1,), (1,)), ((), ())), preferred_element_type=F32)


def mm_tn(a, b):
    return lax.dot_general(a, b, (((0,), (0,)), ((), ())), preferred_element_type=F32)


def vmem(count):
    return [pl.BlockSpec(memory_space=pltpu.VMEM)] * count


PARAMS = pltpu.CompilerParams(vmem_limit_bytes=56 * 1024 * 1024)


def bias_kernel(last_ref, table_ref, spread_ref, level_ref, north_ref, bias_ref, mask_ref, rows_ref, left_ref, right_ref):
    table = table_ref[...]
    for q in range(WIN):
        rows_ref[8 * q : 8 * q + 8, :] = pltpu.roll(table, (768 - PLACE[q]) % 768, 1)[:, :SPAN]
    rows = rows_ref[...]
    high = rows.astype(BF)
    rest = rows - high.astype(F32)
    middle = rest.astype(BF)
    low = (rest - middle.astype(F32)).astype(BF)
    spread = spread_ref[...]
    wide = mm(high, spread) + mm(middle, spread) + mm(low, spread)
    left_ref[...] = wide[:, :128]
    right_ref[...] = wide[:, 128:]
    for h in range(HEADS):
        bias_ref[h, :, :128] = left_ref[pl.ds(h, WIN, stride=8), :]
        bias_ref[h, :, 128:] = right_ref[pl.ds(h, WIN, stride=8), :][:, :16]
    north = jnp.where(last_ref[0] == 1, north_ref[...].astype(F32), 0.0)
    mask_ref[0] = north * MASKED
    mask_ref[1] = jnp.maximum(north, level_ref[...].astype(F32)) * MASKED


def bias_of(table, last):
    shapes = [jax.ShapeDtypeStruct((HEADS, WIN, WIN), F32), jax.ShapeDtypeStruct((2, WIN, WIN), F32)]
    return pl.pallas_call(
        bias_kernel,
        out_shape=shapes,
        in_specs=[pl.BlockSpec(memory_space=pltpu.SMEM)] + vmem(4),
        out_specs=vmem(2),
        scratch_shapes=[pltpu.VMEM((8 * WIN, SPAN), F32)] + [pltpu.VMEM((8 * WIN, 128), F32)] * 2,
        compiler_params=PARAMS,
    )(last, jnp.pad(table, ((0, 0), (0, 768 - TABLE))), plan("spread"), plan("apart_level"), plan("apart_north"))


def norm_parts(values, width):
    mean = sum(jnp.sum(v, axis=1, keepdims=True) for v in values) * (1.0 / width)
    center = [v - mean for v in values]
    spread = sum(jnp.sum(v * v, axis=1, keepdims=True) for v in center) * (1.0 / width)
    scale = lax.rsqrt(spread + EPSILON)
    return [v * scale for v in center], scale


def norm_back(hats, scale, cots, gains, width):
    inner = [c * g for c, g in zip(cots, gains)]
    first = sum(jnp.sum(v, axis=1, keepdims=True) for v in inner) * (1.0 / width)
    second = sum(jnp.sum(v * h, axis=1, keepdims=True) for v, h in zip(inner, hats)) * (1.0 / width)
    return [scale * (v - first - h * second) for v, h in zip(inner, hats)]


def lower_half():
    return lax.broadcasted_iota(jnp.int32, (WIN, 128), 1) < 64


def attend_kernel(
    own_ref, west_ref, south_ref, plan_own, plan_west, plan_south, plan_edge, gain_ref, wqkv_ref, wproj_ref,
    bias_ref, mask_ref, x_ref, qkv_ref, p_ref, mixed_ref, block_ref, edge_ref,
):
    x = mm(plan_own[...], own_ref[...]) + mm(plan_west[...], west_ref[...]) + mm(plan_south[...], south_ref[...])
    x_ref[...] = x.astype(BF)
    (hat,), _ = norm_parts([x], 512)
    normed = (hat * gain_ref[...]).astype(BF)
    qkv_ref[...] = mm(normed, wqkv_ref[...]).astype(BF)
    lower = lower_half()
    for w in range(2):
        rows = slice(w * WIN, (w + 1) * WIN)
        for pair in range(4):
            lanes = slice(pair * 128, pair * 128 + 128)
            query = qkv_ref[rows, lanes]
            key = qkv_ref[rows, 512 + pair * 128 : 640 + pair * 128]
            value = qkv_ref[rows, 1024 + pair * 128 : 1152 + pair * 128]
            outs = []
            for half in range(2):
                h = 2 * pair + half
                keep = lower if half == 0 else jnp.logical_not(lower)
                part = jnp.where(keep, query * 0.125, 0.0).astype(BF)
                scores = mm_nt(part, key) + bias_ref[h] + mask_ref[w]
                top = jnp.max(scores, axis=1, keepdims=True)
                grown = jnp.exp(scores - top)
                weights = (grown / jnp.sum(grown, axis=1, keepdims=True)).astype(BF)
                p_ref[w * HEADS + h] = weights
                outs.append(mm(weights, value))
            mixed_ref[rows, lanes] = jnp.where(lower, outs[0], outs[1]).astype(BF)
    attended = mm(mixed_ref[...], wproj_ref[...]).astype(BF)
    block = (x + attended.astype(F32)).astype(BF)
    block_ref[...] = block
    edge_ref[...] = mm(plan_edge[...], block).astype(BF)


def attend(own, west, south, gain, wqkv, wproj, bias, mask):
    shapes = [(TOK, 512), (TOK, 1536), (2 * HEADS, WIN, WIN), (TOK, 512), (TOK, 512), (96, 512)]
    return pl.pallas_call(
        attend_kernel,
        out_shape=[jax.ShapeDtypeStruct(s, BF) for s in shapes],
        in_specs=vmem(12),
        out_specs=vmem(6),
        compiler_params=PARAMS,
    )(own, west, south, plan("own"), plan("west"), plan("south"), plan("edge"), gain, wqkv, wproj, bias, mask)


def merge_kernel(
    block_ref, prev_ref, next_ref, cot_ref, cot_west_ref, cot_south_ref, quad_own, quad_prev, quad_next, quad_t,
    plan_cot, plan_cot_west, plan_cot_south, coarse, gain_ref, wmerge_ref,
    merged_ref, back_ref, gain_grad_ref, parts_ref,
):
    stacked = mm(quad_own[...], block_ref[...]) + mm(quad_prev[...], prev_ref[...]) + mm(quad_next[...], next_ref[...])
    values = [stacked[96 * k : 96 * k + 96] for k in range(4)]
    hats, scale = norm_parts(values, 2048)
    gains = [gain_ref[:, 512 * k : 512 * k + 512] for k in range(4)]
    normed = [(h * g).astype(BF) for h, g in zip(hats, gains)]
    merged = sum(mm(normed[k], wmerge_ref[512 * k : 512 * k + 512, :]) for k in range(4)).astype(BF)
    merged_ref[...] = mm(coarse[...], merged).astype(BF)
    cot = (
        mm(plan_cot[...], cot_ref[...]) + mm(plan_cot_west[...], cot_west_ref[...])
        + mm(plan_cot_south[...], cot_south_ref[...])
    )
    cot_all = cot.astype(BF)
    counted = lax.broadcasted_iota(jnp.int32, (96, 1024), 0) < 72
    cot_own = jnp.where(counted, cot, 0.0).astype(BF)
    cots = [mm_nt(cot_all, wmerge_ref[512 * k : 512 * k + 512, :]).astype(BF).astype(F32) for k in range(4)]
    for k in range(4):
        gain_grad_ref[:, 512 * k : 512 * k + 512] = jnp.sum((cots[k] * hats[k])[:72], axis=0, keepdims=True)
    pulled = norm_back(hats, scale, cots, gains, 2048)
    back_ref[...] = mm(quad_t[...], jnp.concatenate(pulled, axis=0).astype(BF)).astype(BF)
    for k in range(4):
        for lat in range(4):
            grad = mm_tn(normed[k], cot_own[:, 256 * lat : 256 * lat + 256])
            for t in range(2):
                piece = grad[:, 128 * t : 128 * t + 128].reshape(2, 8, 32, 128).astype(BF)
                parts_ref[lat % 2, 2 * k : 2 * k + 2, :, lat // 2, 32 * t : 32 * t + 32, :] = piece


def merge(block, prev, following, cot, cot_west, cot_south, gain, wmerge):
    shapes = [
        jax.ShapeDtypeStruct((72, 1024), BF), jax.ShapeDtypeStruct((TOK, 512), BF),
        jax.ShapeDtypeStruct((1, 2048), F32), jax.ShapeDtypeStruct((2, 8, 8, 2, 64, 128), BF),
    ]
    names = ("quad_own", "quad_prev", "quad_next", "quad_t", "cot_own", "cot_west", "cot_south", "coarse")
    return pl.pallas_call(
        merge_kernel,
        out_shape=shapes,
        in_specs=vmem(16),
        out_specs=vmem(4),
        compiler_params=PARAMS,
    )(block, prev, following, cot, cot_west, cot_south, *[plan(n) for n in names], gain, wmerge)


def back_kernel(
    cot_ref, x_ref, qkv_ref, p_ref, mixed_ref, wqkv_ref, wproj_ref, gain_ref, spread_t, back_plan,
    grad_ref, gain_grad_ref, bias_grad_ref, parts_ref, dqkv_ref, left_ref, right_ref, wide_ref,
):
    cot = cot_ref[...]
    mixed_cot = mm_nt(cot, wproj_ref[...]).astype(BF)
    lower = lower_half()
    for w in range(2):
        rows = slice(w * WIN, (w + 1) * WIN)
        for pair in range(4):
            lanes = slice(pair * 128, pair * 128 + 128)
            query = qkv_ref[rows, lanes]
            key = qkv_ref[rows, 512 + pair * 128 : 640 + pair * 128]
            value = qkv_ref[rows, 1024 + pair * 128 : 1152 + pair * 128]
            out_cot = mixed_cot[rows, lanes]
            found = []
            for half in range(2):
                h = 2 * pair + half
                keep = lower if half == 0 else jnp.logical_not(lower)
                part = jnp.where(keep, out_cot, 0.0).astype(BF)
                weights = p_ref[w * HEADS + h]
                weight_cot = mm_nt(part, value).astype(BF).astype(F32)
                wide = weights.astype(F32)
                product = wide * weight_cot
                score_cot = product - wide * jnp.sum(product, axis=1, keepdims=True)
                places = pl.ds(h, WIN, stride=8)
                right = jnp.concatenate([score_cot[:, 128:], jnp.zeros((WIN, 112), F32)], axis=1)
                if w == 0:
                    left_ref[places, :] = score_cot[:, :128]
                    right_ref[places, :] = right
                else:
                    left_ref[places, :] = left_ref[places, :] + score_cot[:, :128]
                    right_ref[places, :] = right_ref[places, :] + right
                scaled = (score_cot * 0.125).astype(BF)
                found.append((mm(scaled, key), mm_tn(scaled, query), mm_tn(weights, out_cot)))
            for n in range(3):
                both = jnp.where(lower, found[0][n], found[1][n]).astype(BF)
                dqkv_ref[rows, 512 * n + pair * 128 : 512 * n + pair * 128 + 128] = both
    dqkv = dqkv_ref[...]
    x = x_ref[...].astype(F32)
    (hat,), scale = norm_parts([x], 512)
    gain = gain_ref[...]
    normed = (hat * gain).astype(BF)
    normed_cot = mm_nt(dqkv, wqkv_ref[...]).astype(BF).astype(F32)
    gain_grad_ref[...] = jnp.sum(normed_cot * hat, axis=0, keepdims=True)
    (pulled,) = norm_back([hat], scale, [normed_cot], [gain], 512)
    total = (cot.astype(F32) + pulled.astype(BF).astype(F32)).astype(BF)
    grad_ref[...] = mm(back_plan[...], total).astype(BF)
    mixed = mixed_ref[...]
    for lat in range(4):
        grad = mm_tn(normed, dqkv[:, 384 * lat : 384 * lat + 384])
        proj = mm_tn(mixed, cot[:, 128 * lat : 128 * lat + 128])
        tiles = [grad[:, 128 * t : 128 * t + 128].reshape(8, 8, 8, 128) for t in range(3)] + [proj.reshape(8, 8, 8, 128)]
        for t in range(2):
            piece = jnp.concatenate([tiles[2 * t], tiles[2 * t + 1]], axis=2).astype(BF)
            parts_ref[lat % 2, :, :, lat // 2, 16 * t : 16 * t + 16, :] = piece
    wide_ref[...] = mm(left_ref[...].astype(BF), spread_t[:128, :]) + mm(right_ref[...].astype(BF), spread_t[128:, :])
    blank = jnp.zeros((8, 512 - SPAN), F32)
    levels = []
    for l in range(2):
        outer = None
        for r in reversed(range(ROWS)):
            inner = None
            for c in reversed(range(COLS)):
                q = 8 * (l * 72 + r * 12 + c)
                here = jnp.concatenate([wide_ref[q : q + 8, :], blank], axis=1)
                inner = here if inner is None else pltpu.roll(inner, 1, 1) + here
            outer = inner if outer is None else pltpu.roll(outer, 23, 1) + inner
        levels.append(jnp.concatenate([outer, jnp.zeros((8, 256), F32)], axis=1))
    bias_grad_ref[...] = levels[0] + pltpu.roll(levels[1], 253, 1)


def attend_back(cot, x, qkv, p, mixed, wqkv, wproj, gain):
    shapes = [
        jax.ShapeDtypeStruct((TOK, 512), BF), jax.ShapeDtypeStruct((1, 512), F32),
        jax.ShapeDtypeStruct((8, 768), F32), jax.ShapeDtypeStruct((2, 8, 8, 2, 32, 128), BF),
    ]
    return pl.pallas_call(
        back_kernel,
        out_shape=shapes,
        in_specs=vmem(10),
        out_specs=vmem(4),
        scratch_shapes=[pltpu.VMEM((TOK, 1536), BF), pltpu.VMEM((8 * WIN, 128), F32), pltpu.VMEM((8 * WIN, 128), F32), pltpu.VMEM((8 * WIN, SPAN), F32)],
        compiler_params=PARAMS,
    )(cot, x, qkv, p, mixed, wqkv, wproj, gain, plan("spread_t"), plan("back"))


def total_of(axes):
    total = 1
    for axis in axes:
        total *= lax.axis_size(axis)
    return total


def moved(block, axes, distance):
    count = total_of(axes)
    return lax.ppermute(block, axes, [((i - distance) % count, i) for i in range(count)])


def exchange(parts, small, axes):
    count = parts.shape[0]
    rows = jnp.broadcast_to(small.astype(BF)[None], (count,) + small.shape)
    sent = jnp.concatenate([parts.astype(BF).reshape(count, -1, 128), rows], axis=1)
    got = lax.all_to_all(sent, axes, 0, 0, tiled=True)
    total = jnp.sum(got.astype(F32), axis=0)
    body = total[: sent.shape[1] - small.shape[0]]
    return body.reshape(parts.shape[1:]), total[sent.shape[1] - small.shape[0] :]


def reduce_all(early, late, vectors):
    parts = jnp.concatenate([late, early], axis=4).reshape(2, 8, 16, 96, 128)
    small = jnp.concatenate([v.reshape(-1, 128) for v in vectors], axis=0)
    small = jnp.pad(small, ((0, 80 - small.shape[0]), (0, 0)))
    for axes in (CORE, NEAR, FAR):
        parts, small = exchange(parts, small, axes)

    def whole(block, rows, tiles_wide):
        return block.reshape(tiles_wide, rows, 128).transpose(1, 0, 2).reshape(rows, tiles_wide * 128)

    return whole(parts[:24], 8, 3), parts[24:32], whole(parts[32:], 32, 2), small


def on_device(features, norm_gain, qkv_weight, proj_weight, bias_table, merge_gain, merge_weight, merged_cot):
    last = (lax.axis_index(LAT) == total_of(LAT) - 1).astype(jnp.int32).reshape(1)
    gain, wide_gain = norm_gain.reshape(1, 512), merge_gain.reshape(1, 2048)
    own = features.transpose(1, 2, 0, 3).reshape(6, 48, 512)
    cot = merged_cot.transpose(1, 2, 0, 3).reshape(3, 24, 1024)
    west = moved(own[:, :24], LON, -1)
    cot_west = moved(cot[:, :12], LON, -1)
    south = moved(jnp.concatenate([own[:3, 24:], west[:3]], axis=1), LAT, -1)
    cot_south = moved(jnp.concatenate([cot[:2, 12:], cot_west[:2]], axis=1), LAT, -1)
    bias, mask = bias_of(bias_table, last)
    x, qkv, p, mixed, block, edge = attend(
        own.reshape(TOK, 512), west.reshape(144, 512), south.reshape(144, 512), gain, qkv_weight, proj_weight, bias, mask
    )
    following = moved(edge[:48], LAT, -1)
    prev = moved(edge[48:], LAT, 1)
    merged, attn_cot, merge_gain_part, early = merge(
        block, prev, following, cot.reshape(72, 1024), cot_west.reshape(36, 1024), cot_south.reshape(48, 1024),
        wide_gain, merge_weight,
    )
    grad, norm_gain_part, bias_part, late = attend_back(
        attn_cot, x, qkv, p, mixed, qkv_weight, proj_weight, gain
    )

    def home(field, rows_back, width_back):
        north = moved(field[field.shape[0] - rows_back :], LAT, 1)
        field = jnp.concatenate([north, field[: field.shape[0] - rows_back]], axis=0)
        east = moved(field[:, field.shape[1] - width_back :], LON, 1)
        return jnp.concatenate([east, field[:, : field.shape[1] - width_back]], axis=1)

    merged = home(merged.reshape(3, 24, 1024), 1, 12).reshape(3, 6, 4, 1024).transpose(2, 0, 1, 3)
    features_grad = home(grad.reshape(6, 48, 512), 3, 24).reshape(6, 12, 4, 512).transpose(2, 0, 1, 3)
    qkv_grad, proj_grad, merge_grad, small = reduce_all(early, late, (norm_gain_part, merge_gain_part, bias_part))
    return (
        merged,
        features_grad,
        qkv_grad,
        proj_grad,
        merge_grad,
        small[:4].reshape(-1),
        small[4:20].reshape(-1),
        small[20:68].reshape(8, 768)[:, :TABLE],
    )


def solution(mesh):
    fine = Mesh(mesh.devices.reshape(4, 2, 8, 2, 2), AXES)
    field = P(None, LAT, LON, None)
    return jax.shard_map(
        on_device,
        mesh=fine,
        in_specs=(field, P(), P(), P(), P(), P(), P(), field),
        out_specs=(field, field, P(LON, LAT), P(LON, LAT), P(LON, LAT), P(), P(), P()),
        check_vma=False,
    )
```

profile of v0, /device:TPU:8, one launch (start us, length us, event | category | flops | bytes accessed | tf_op | source)
XLA Modules:
  0.0 175.0 jit_solution(5298355505977263153)
XLA Ops:
  0.6 1.1 reshape.99
  1.7 5.8 %collective-permute-start = (bf16[6,24,512]{2,1,0:T(8,128)(2,1)S(1)}, bf16[6,24,512]{2,1,0:T(8,128)(2,1)S(1)}, u32[]{:S(2)}, u32[]{:S(2)}) collective-permute-start(bf16[6,24,512]{2,1,0:T(8,128)(2,1)S(1)} %slice.136), channel_id=1, source_target_pairs={{4,0},{8,4},{12,8},{16,12},{20,16},{24,20},{28,24},{32,28},{36,32}... | collective-permute-start | bytes 442376 | tf_op jit(solution)/shard_map/ppermute | solution.py:368
  7.6 0.9 reshape.105
  8.5 1.1 collective-permute-start.4
  9.6 2.1 %collective-permute-done = bf16[6,24,512]{2,1,0:T(8,128)(2,1)S(1)} collective-permute-done((bf16[6,24,512]{2,1,0:T(8,128)(2,1)S(1)}, bf16[6,24,512]{2,1,0:T(8,128)(2,1)S(1)}, u32[]{:S(2)}, u32[]{:S(2)}) %collective-permute-start) | collective-permute-done | bytes 147488 | tf_op jit(solution)/shard_map/ppermute | solution.py:368
  11.9 1.8 reshape_reshape.9.own_ref
  13.7 1.3 pad.9.table_ref
  15.0 3.6 %shard_map.296 = (f32[8,144,144]{2,1,0:T(8,128)}, f32[2,144,144]{2,1,0:T(8,128)}) custom-call(s32[1]{0:T(128)} %bitcast.4.last_ref, f32[8,768]{1,0:T(8,128)} %pad.9.table_ref, bf16[384,256]{1,0:T(8,128)(2,1)} %constant.50.clone.spread_ref, bf16[144,144]{1,0:T(8,128)(2,1)} %constant.51.clone.level_ref, bf16[144,144]{1,0:T(8,128)(2,1)} %constant.52.clone.north_ref), custom_call_target="tpu_custom_call" | custom-call | tf_op jit(solution)/shard_map/pallas_call | solution.py:150
  18.7 2.7 %collective-permute-start.5 = (bf16[2,24,1024]{2,1,0:T(8,128)(2,1)S(1)}, bf16[2,24,1024]{2,1,0:T(8,128)(2,1)S(1)}, u32[]{:S(2)}, u32[]{:S(2)}) collective-permute-start(bf16[2,24,1024]{2,1,0:T(8,128)(2,1)S(1)} %pad_maximum_fusion.7), channel_id=1, source_target_pairs={{1,0},{2,1},{3,2},{0,3},{5,4},{6,5},{7,6},{4,7},{9,8},{10,9},{11,1... | collective-permute-start | bytes 294920 | tf_op jit(solution)/shard_map/ppermute | solution.py:368
  22.0 6.3 %shard_map.297 = (bf16[288,512]{1,0:T(8,128)(2,1)}, bf16[288,1536]{1,0:T(8,128)(2,1)}, bf16[16,144,144]{2,1,0:T(8,128)(2,1)}, bf16[288,512]{1,0:T(8,128)(2,1)}, ...) custom-call(bf16[288,512]{1,0:T(8,128)(2,1)} %reshape_reshape.9.own_ref, bf16[144,512]{1,0:T(8,128)(2,1)} %bitcast.49, ...), custom_call_target="tpu_custom_call" | custom-call | tf_op jit(solution)/shard_map/pallas_call | solution.py:216
  28.3 0.8 fusion.10
  31.1 3.4 %collective-permute-done.2.prev_ref = bf16[48,512]{1,0:T(8,128)(2,1)S(1)} collective-permute-done((bf16[48,512]{1,0:T(8,128)(2,1)S(1)}, bf16[48,512]{1,0:T(8,128)(2,1)S(1)}, u32[]{:S(2)}, u32[]{:S(2)}) %collective-permute-start.2) | collective-permute-done | bytes 49184 | tf_op jit(solution)/shard_map/ppermute | solution.py:368
  35.1 9.5 %shard_map.298 = (bf16[72,1024]{1,0:T(8,128)(2,1)}, bf16[288,512]{1,0:T(8,128)(2,1)}, f32[1,2048]{1,0:T(1,128)}, bf16[2,8,8,2,64,128]{5,4,3,2,1,0:T(8,128)(2,1)}) custom-call(bf16[288,512]{1,0:T(8,128)(2,1)} %get-tuple-element.26.block_ref, bf16[48,512]{1,0:T(8,128)(2,1)} %copy-done.7, bf16[48,512]{1,0:T(8,128)(2,1)} %copy-done.6, ...), custom_call_target="tpu_custom_call" | custom-call | tf_op jit(solution)/shard_map/pallas_call | solution.py:263
  44.6 13.1 %shard_map.299 = (bf16[288,512]{1,0:T(8,128)(2,1)}, f32[1,512]{1,0:T(1,128)}, f32[8,768]{1,0:T(8,128)}, bf16[2,8,8,2,32,128]{5,4,3,2,1,0:T(8,128)(2,1)}) custom-call(bf16[288,512]{1,0:T(8,128)(2,1)} %get-tuple-element.29.cot_ref, bf16[288,512]{1,0:T(8,128)(2,1)} %get-tuple-element.30.x_ref, bf16[288,1536]{1,0:T(8,128)(2,1)} %get-tuple-element.31.qkv_ref, ...), custom_call_target="tpu_custom_call" | custom-call | tf_op jit(solution)/shard_map/pallas_call | solution.py:349
  58.5 0.7 convert.25
  59.3 5.0 %pad_maximum_fusion.1 = bf16[2,8,8,2,96,128]{5,4,3,2,1,0:T(8,128)(2,1)S(1)} fusion(bf16[2,8,8,2,64,128]{5,4,3,2,1,0:T(8,128)(2,1)} %get-tuple-element.36, bf16[2,8,8,2,32,128]{5,4,3,2,1,0:T(8,128)(2,1)} %get-tuple-element.35), kind=kLoop, calls=%fused_computation.1 | loop fusion | flops 12582912 | bytes 12582912 | tf_op jit(solution)/shard_map/concatenate | solution.py:382
  64.3 6.7 %pad_maximum_fusion = bf16[2,12368,128]{2,1,0:T(8,128)(2,1)S(1)} fusion(bf16[2,80,128]{2,1,0:T(8,128)(2,1)S(1)} %broadcast_in_dim.6, bf16[2,12288,128]{2,1,0:T(8,128)(2,1)S(1)} %bitcast.38), kind=kLoop, calls=%fused_computation | loop fusion | flops 12664832 | bytes 12664832 | tf_op jit(solution)/shard_map/concatenate | solution.py:374
  71.0 10.0 %all_to_all.15 = bf16[2,12368,128]{2,1,0:T(8,128)(2,1)} all-to-all(bf16[2,12368,128]{2,1,0:T(8,128)(2,1)S(1)} %pad_maximum_fusion), channel_id=1, replica_groups=mesh['x'=4,'yl'=2,'z'=8,'yh'=2,'c'=2] {'c'}, dimensions={0} | all-to-all | bytes 12664832 | tf_op jit(solution)/shard_map/all_to_all | solution.py:375
  81.0 8.0 %reduce = bf16[12368,128]{1,0:T(8,128)(2,1)S(1)} reduce(bf16[2,12368,128]{2,1,0:T(8,128)(2,1)} %all_to_all.15, bf16[]{:T(256)} %constant.49.clone.1), dimensions={0}, to_apply=%region_0.1.clone | reduce | flops 1583104 | bytes 9498626 | tf_op jit(solution)/shard_map/reduce_sum | solution.py:376
  89.5 45.9 %all_to_all.16 = bf16[8,1616,128]{2,1,0:T(8,128)(2,1)S(1)} all-to-all(bf16[8,1616,128]{2,1,0:T(8,128)(2,1)S(1)} %pad_maximum_fusion.2), channel_id=1, replica_groups=mesh['x'=4,'yl'=2,'z'=8,'yh'=2,'c'=2] {'x','yl'}, dimensions={0} | all-to-all | bytes 6619136 | tf_op jit(solution)/shard_map/all_to_all | solution.py:375
  135.4 1.3 reduce.1
  136.7 0.8 slice.149
  137.5 1.0 slice.148
  138.6 0.9 pad_maximum_fusion.3
  139.5 7.1 %all-to-all-start.2 = ((bf16[16,176,128]{2,1,0:T(8,128)(2,1)}), bf16[16,176,128]{2,1,0:T(8,128)(2,1)S(1)}, u32[]{:S(2)}, u32[]{:S(2)}) async-start(bf16[16,176,128]{2,1,0:T(8,128)(2,1)} %pad_maximum_fusion.3), calls=%async_computation.2 | async-start | bytes 1441792 | tf_op jit(solution)/shard_map/all_to_all | solution.py:375
  146.7 3.6 %collective-permute-start.8 = (bf16[3,48,512]{2,1,0:T(8,128)(2,1)S(1)}, bf16[3,48,512]{2,1,0:T(8,128)(2,1)S(1)}, u32[]{:S(2)}, u32[]{:S(2)}) collective-permute-start(bf16[3,48,512]{2,1,0:T(8,128)(2,1)S(1)} %bitcast.53), channel_id=1, source_target_pairs={{3,0},{0,1},{1,2},{2,3},{7,4},{4,5},{5,6},{6,7},{11,8},{8,9},{9,10... | collective-permute-start | bytes 442376 | tf_op jit(solution)/shard_map/ppermute | solution.py:368
  150.3 1.4 collective-permute-done.6
  151.7 2.4 %collective-permute-start.7 = (bf16[3,12,1024]{2,1,0:T(8,128)(2,1)S(1)}, bf16[3,12,1024]{2,1,0:T(8,128)(2,1)S(1)}, u32[]{:S(2)}, u32[]{:S(2)}) collective-permute-start(bf16[3,12,1024]{2,1,0:T(8,128)(2,1)S(1)} %fusion.3), channel_id=1, source_target_pairs={{252,0},{0,4},{4,8},{8,12},{12,16},{16,20},{20,24},{24,28},{28,32}... | collective-permute-start | bytes 221192 | tf_op jit(solution)/shard_map/ppermute | solution.py:368
  154.2 1.7 collective-permute-start.9
  155.8 12.9 %collective-permute-done.7 = bf16[3,12,1024]{2,1,0:T(8,128)(2,1)S(1)} collective-permute-done((bf16[3,12,1024]{2,1,0:T(8,128)(2,1)S(1)}, bf16[3,12,1024]{2,1,0:T(8,128)(2,1)S(1)}, u32[]{:S(2)}, u32[]{:S(2)}) %collective-permute-start.7) | collective-permute-done | bytes 73760 | tf_op jit(solution)/shard_map/ppermute | solution.py:368
  169.5 1.0 collective-permute-done.9
  170.5 0.8 reshape.110
  (65 shorter events, 9.5 us)
Async XLA Ops:
  0.6 29.1 %copy-start = (bf16[4,3,6,1024]{3,0,2,1:T(4,128)(2,1)S(1)}, bf16[4,3,6,1024]{3,0,2,1:T(4,128)(2,1)}, u32[]{:S(2)}) copy-start(bf16[4,3,6,1024]{3,0,2,1:T(4,128)(2,1)} %param.32) | copy-start | bytes 442372
  1.7 10.0 %collective-permute-start = (bf16[6,24,512]{2,1,0:T(8,128)(2,1)S(1)}, bf16[6,24,512]{2,1,0:T(8,128)(2,1)S(1)}, u32[]{:S(2)}, u32[]{:S(2)}) collective-permute-start(bf16[6,24,512]{2,1,0:T(8,128)(2,1)S(1)} %slice.136), channel_id=1, source_target_pairs={{4,0},{8,4},{12,8},{16,12},{20,16},{24,20},{28,24},{32,28},{36,32}... | collective-permute-start | bytes 442376 | tf_op jit(solution)/shard_map/ppermute | solution.py:368
  8.5 10.1 %collective-permute-start.4 = (bf16[3,12,1024]{2,1,0:T(8,128)(2,1)S(1)}, bf16[3,12,1024]{2,1,0:T(8,128)(2,1)S(1)}, u32[]{:S(2)}, u32[]{:S(2)}) collective-permute-start(bf16[3,12,1024]{2,1,0:T(8,128)(2,1)S(1)} %slice.139), channel_id=1, source_target_pairs={{4,0},{8,4},{12,8},{16,12},{20,16},{24,20},{28,24},{32,28},{36,32}... | collective-permute-start | bytes 221192 | tf_op jit(solution)/shard_map/ppermute | solution.py:368
  11.7 9.6 %copy-start.1 = (bf16[6,24,512]{2,1,0:T(8,128)(2,1)}, bf16[6,24,512]{2,1,0:T(8,128)(2,1)S(1)}, u32[]{:S(2)}) copy-start(bf16[6,24,512]{2,1,0:T(8,128)(2,1)S(1)} %collective-permute-done) | copy-start | bytes 442372
  11.7 9.6 %collective-permute-start.1 = (bf16[3,48,512]{2,1,0:T(8,128)(2,1)S(1)}, bf16[3,48,512]{2,1,0:T(8,128)(2,1)S(1)}, u32[]{:S(2)}, u32[]{:S(2)}) collective-permute-start(bf16[3,48,512]{2,1,0:T(8,128)(2,1)S(1)} %pad_maximum_fusion.6), channel_id=1, source_target_pairs={{1,0},{2,1},{3,2},{0,3},{5,4},{6,5},{7,6},{4,7},{9,8},{10,9},{11,1... | collective-permute-start | bytes 442376 | tf_op jit(solution)/shard_map/ppermute | solution.py:368
  18.7 12.4 %collective-permute-start.5 = (bf16[2,24,1024]{2,1,0:T(8,128)(2,1)S(1)}, bf16[2,24,1024]{2,1,0:T(8,128)(2,1)S(1)}, u32[]{:S(2)}, u32[]{:S(2)}) collective-permute-start(bf16[2,24,1024]{2,1,0:T(8,128)(2,1)S(1)} %pad_maximum_fusion.7), channel_id=1, source_target_pairs={{1,0},{2,1},{3,2},{0,3},{5,4},{6,5},{7,6},{4,7},{9,8},{10,9},{11,1... | collective-permute-start | bytes 294920 | tf_op jit(solution)/shard_map/ppermute | solution.py:368
  21.4 0.7 copy-start.3
  29.1 1.9 %collective-permute-start.3 = (bf16[48,512]{1,0:T(8,128)(2,1)S(1)}, bf16[48,512]{1,0:T(8,128)(2,1)S(1)}, u32[]{:S(2)}, u32[]{:S(2)}) collective-permute-start(bf16[48,512]{1,0:T(8,128)(2,1)S(1)} %get-tuple-element.42), channel_id=1, source_target_pairs={{1,0},{2,1},{3,2},{0,3},{5,4},{6,5},{7,6},{4,7},{9,8},{10,9},{11,1... | collective-permute-start | bytes 147464 | tf_op jit(solution)/shard_map/ppermute | solution.py:368
  29.2 5.3 %collective-permute-start.2 = (bf16[48,512]{1,0:T(8,128)(2,1)S(1)}, bf16[48,512]{1,0:T(8,128)(2,1)S(1)}, u32[]{:S(2)}, u32[]{:S(2)}) collective-permute-start(bf16[48,512]{1,0:T(8,128)(2,1)S(1)} %get-tuple-element.43), channel_id=1, source_target_pairs={{3,0},{0,1},{1,2},{2,3},{7,4},{4,5},{5,6},{6,7},{11,8},{8,9},{9,10... | collective-permute-start | bytes 147464 | tf_op jit(solution)/shard_map/ppermute | solution.py:368
  31.0 3.4 %copy-start.5 = (bf16[2,24,1024]{2,1,0:T(8,128)(2,1)}, bf16[2,24,1024]{2,1,0:T(8,128)(2,1)S(1)}, u32[]{:S(2)}) copy-start(bf16[2,24,1024]{2,1,0:T(8,128)(2,1)S(1)} %collective-permute-done.5) | copy-start | bytes 294916
  31.0 3.4 %copy-start.6 = (bf16[48,512]{1,0:T(8,128)(2,1)}, bf16[48,512]{1,0:T(8,128)(2,1)S(1)}, u32[]{:S(2)}) copy-start(bf16[48,512]{1,0:T(8,128)(2,1)S(1)} %collective-permute-done.3.next_ref) | copy-start | bytes 147460
  34.5 0.6 copy-start.7
  44.6 13.8 %copy-start.8 = (f32[1,2048]{1,0:T(1,128)S(1)}, f32[1,2048]{1,0:T(1,128)}, u32[]{:S(2)}) copy-start(f32[1,2048]{1,0:T(1,128)} %get-tuple-element.38) | copy-start | bytes 24580
  135.4 11.2 %copy-start.4 = (bf16[72,1024]{1,0:T(8,128)(2,1)S(1)}, bf16[72,1024]{1,0:T(8,128)(2,1)}, u32[]{:S(2)}) copy-start(bf16[72,1024]{1,0:T(8,128)(2,1)} %get-tuple-element.28) | copy-start | bytes 442372
  136.7 10.0 %copy-start.2 = (bf16[288,512]{1,0:T(8,128)(2,1)S(1)}, bf16[288,512]{1,0:T(8,128)(2,1)}, u32[]{:S(2)}) copy-start(bf16[288,512]{1,0:T(8,128)(2,1)} %get-tuple-element.34) | copy-start | bytes 884740
  139.5 31.8 %all-to-all-start.2 = ((bf16[16,176,128]{2,1,0:T(8,128)(2,1)}), bf16[16,176,128]{2,1,0:T(8,128)(2,1)S(1)}, u32[]{:S(2)}, u32[]{:S(2)}) async-start(bf16[16,176,128]{2,1,0:T(8,128)(2,1)} %pad_maximum_fusion.3), calls=%async_computation.2 | async-start | bytes 1441792 | tf_op jit(solution)/shard_map/all_to_all | solution.py:375
  146.6 5.1 %collective-permute-start.6 = (bf16[1,24,1024]{2,1,0:T(8,128)(2,1)S(1)}, bf16[1,24,1024]{2,1,0:T(8,128)(2,1)S(1)}, u32[]{:S(2)}, u32[]{:S(2)}) collective-permute-start(bf16[1,24,1024]{2,1,0:T(8,128)(2,1)S(1)} %slice_bitcast_fusion), channel_id=1, source_target_pairs={{3,0},{0,1},{1,2},{2,3},{7,4},{4,5},{5,6},{6,7},{11,8},{8,9},{9,10... | collective-permute-start | bytes 147464 | tf_op jit(solution)/shard_map/ppermute | solution.py:368
  146.7 7.4 %collective-permute-start.8 = (bf16[3,48,512]{2,1,0:T(8,128)(2,1)S(1)}, bf16[3,48,512]{2,1,0:T(8,128)(2,1)S(1)}, u32[]{:S(2)}, u32[]{:S(2)}) collective-permute-start(bf16[3,48,512]{2,1,0:T(8,128)(2,1)S(1)} %bitcast.53), channel_id=1, source_target_pairs={{3,0},{0,1},{1,2},{2,3},{7,4},{4,5},{5,6},{6,7},{11,8},{8,9},{9,10... | collective-permute-start | bytes 442376 | tf_op jit(solution)/shard_map/ppermute | solution.py:368
  151.7 17.1 %collective-permute-start.7 = (bf16[3,12,1024]{2,1,0:T(8,128)(2,1)S(1)}, bf16[3,12,1024]{2,1,0:T(8,128)(2,1)S(1)}, u32[]{:S(2)}, u32[]{:S(2)}) collective-permute-start(bf16[3,12,1024]{2,1,0:T(8,128)(2,1)S(1)} %fusion.3), channel_id=1, source_target_pairs={{252,0},{0,4},{4,8},{8,12},{12,16},{16,20},{20,24},{24,28},{28,32}... | collective-permute-start | bytes 221192 | tf_op jit(solution)/shard_map/ppermute | solution.py:368
  154.2 16.3 %collective-permute-start.9 = (bf16[6,24,512]{2,1,0:T(8,128)(2,1)S(1)}, bf16[6,24,512]{2,1,0:T(8,128)(2,1)S(1)}, u32[]{:S(2)}, u32[]{:S(2)}) collective-permute-start(bf16[6,24,512]{2,1,0:T(8,128)(2,1)S(1)} %fusion.1), channel_id=1, source_target_pairs={{252,0},{0,4},{4,8},{8,12},{12,16},{16,20},{20,24},{24,28},{28,32}... | collective-permute-start | bytes 442376 | tf_op jit(solution)/shard_map/ppermute | solution.py:368
where the time goes:
time: 177 us; the launch traced here: 175 us
  blocking collectives  55.9 us (32%)
  Pallas kernels  32.5 us (18%)
  starting transfers between devices  25.2 us (14%)
  other arithmetic  23.9 us (14%)
  waiting for transfers between devices  20.8 us (12%)
  local copies, waits for them, and re-layouts  16 us (9%)
    all_to_all x2, blocking collectives, exchange(): got = lax.all_to_all(sent, axes, 0, 0, tiled=True)  55.9 us
    ppermute x10, waiting for transfers between devices, moved(): lax.ppermute(block, axes, [((i - distance) % count, i) for i in range(cou...  20.8 us
    ppermute x10, starting transfers between devices, moved(): lax.ppermute(block, axes, [((i - distance) % count, i) for i in range(cou...  18.1 us
    pallas_call x1, Pallas kernels, attend_back(): pl.pallas_call(back_kernel, out_shape=shapes, in_specs=vmem(10), out_spec...  13.1 us
    pallas_call x1, Pallas kernels, merge(): pl.pallas_call(merge_kernel, out_shape=shapes, in_specs=vmem(16), out_spe...  9.53 us
    reduce_sum x3, other arithmetic, exchange(): total = jnp.sum(got.astype(F32), axis=0)  9.45 us
    concatenate x3, other arithmetic, exchange(): jnp.concatenate([parts.astype(BF).reshape(count, -1, 128), rows], axis=1)  7.85 us
    all_to_all x1, starting transfers between devices, exchange(): got = lax.all_to_all(sent, axes, 0, 0, tiled=True)  7.07 us
  transfers between devices with their start and end apart: 11, of which 5 were waited for; matrix products, arithmetic and copies ran while one was open for 5% of the time, Pallas kernels for 6%

commit v1 on v0

--- a/solution.py
+++ b/solution.py
@@ -19,7 +19,7 @@
 TABLE = 759
 AXES = ("x", "yl", "z", "yh", "c")
 LON, LAT = ("x", "yl", "z"), ("yh", "c")
-CORE, NEAR, FAR = ("c",), ("x", "yl"), ("z", "yh")
+NEAR, FAR, CLOSE = ("x", "yl"), ("z", "yh"), ("x", "yl", "c")
 BF, F32 = jnp.bfloat16, jnp.float32
 
 
@@ -32,7 +32,7 @@
 
 
 def plans():
-    own = np.zeros((TOK, TOK)); west = np.zeros((TOK, 144)); south = np.zeros((TOK, 144))
+    own = np.zeros((TOK, TOK)); west = np.zeros((TOK, 144)); south = np.zeros((TOK, 72)); corner = np.zeros((TOK, 72))
     back = np.zeros((TOK, TOK))
     quad_own = np.zeros((4 * 96, TOK)); quad_prev = np.zeros((4 * 96, 48)); quad_next = np.zeros((4 * 96, 48))
     edge = np.zeros((96, TOK))
@@ -43,8 +43,10 @@
                 for c in range(COLS):
                     t = token(w, l, r, c)
                     i, j = r + HALF_LAT, c + HALF_LON
-                    if i >= ROWS:
-                        south[t, ((i - ROWS) * COLS + c) * LEV + lev] = 1
+                    if i >= ROWS and j >= COLS:
+                        corner[t, ((i - ROWS) * HALF_LON + j - COLS) * LEV + lev] = 1
+                    elif i >= ROWS:
+                        south[t, ((i - ROWS) * HALF_LON + c) * LEV + lev] = 1
                     elif j >= COLS:
                         west[t, (i * HALF_LON + j - COLS) * LEV + lev] = 1
                     else:
@@ -64,7 +66,7 @@
                 dj, pc = c % 2, c // 2
                 quad_prev[(dj * 2 + 0) * 96 + 0 * 24 + s * 6 + pc, s * 12 + c] = 1
                 quad_next[(dj * 2 + 1) * 96 + 3 * 24 + s * 6 + pc, s * 12 + c] = 1
-    cot_own = np.zeros((96, 72)); cot_west = np.zeros((96, 36)); cot_south = np.zeros((96, 48))
+    cot_own = np.zeros((96, 72)); cot_west = np.zeros((96, 24)); cot_south = np.zeros((96, 24)); cot_corner = np.zeros((96, 24))
     coarse = np.zeros((72, 96))
     for pr in range(4):
         for s in range(LEV):
@@ -72,10 +74,12 @@
             for pc in range(6):
                 p = pr * 24 + s * 6 + pc
                 i, j = pr + 1, pc + 3
-                if i >= 3:
-                    cot_south[p, ((i - 3) * 6 + pc) * LEV + lev] = 1
+                if i >= 3 and j >= 6:
+                    cot_corner[p, ((i - 3) * 3 + j - 6) * LEV + lev] = 1
+                elif i >= 3:
+                    cot_south[p, ((i - 3) * 3 + pc) * LEV + lev] = 1
                 elif j >= 6:
-                    cot_west[p, (i * 3 + j - 6) * LEV + lev] = 1
+                    cot_west[p, ((i - 1) * 3 + j - 6) * LEV + lev] = 1
                 else:
                     cot_own[p, (i * 6 + j) * LEV + lev] = 1
                 if pr < 3:
@@ -90,9 +94,9 @@
     level = np.arange(WIN) // 72
     north = (np.arange(WIN) % 72) // 12 >= HALF_LAT
     return dict(
-        own=own, west=west, south=south, back=back, quad_own=quad_own, quad_prev=quad_prev,
+        own=own, west=west, south=south, corner=corner, back=back, quad_own=quad_own, quad_prev=quad_prev,
         quad_next=quad_next, quad_t=quad_own.T, edge=edge, cot_own=cot_own, cot_west=cot_west,
-        cot_south=cot_south, coarse=coarse, spread=spread, spread_t=spread.T,
+        cot_south=cot_south, cot_corner=cot_corner, coarse=coarse, spread=spread, spread_t=spread.T,
         apart_level=(level[:, None] != level[None]) * 1.0,
         apart_north=(north[:, None] != north[None]) * 1.0,
     ), [int(v) for v in place]
@@ -119,6 +123,10 @@
 
 def vmem(count):
     return [pl.BlockSpec(memory_space=pltpu.VMEM)] * count
+
+
+def cost(flops, moved_bytes):
+    return pl.CostEstimate(flops=flops, bytes_accessed=moved_bytes, transcendentals=0)
 
 
 PARAMS = pltpu.CompilerParams(vmem_limit_bytes=56 * 1024 * 1024)
@@ -154,6 +162,7 @@
         out_specs=vmem(2),
         scratch_shapes=[pltpu.VMEM((8 * WIN, SPAN), F32)] + [pltpu.VMEM((8 * WIN, 128), F32)] * 2,
         compiler_params=PARAMS,
+        cost_estimate=cost(2_000_000_000, 4_000_000),
     )(last, jnp.pad(table, ((0, 0), (0, 768 - TABLE))), plan("spread"), plan("apart_level"), plan("apart_north"))
 
 
@@ -177,10 +186,13 @@
 
 
 def attend_kernel(
-    own_ref, west_ref, south_ref, plan_own, plan_west, plan_south, plan_edge, gain_ref, wqkv_ref, wproj_ref,
-    bias_ref, mask_ref, x_ref, qkv_ref, p_ref, mixed_ref, block_ref, edge_ref,
+    own_ref, west_ref, south_ref, corner_ref, plan_own, plan_west, plan_south, plan_corner, plan_edge, gain_ref, wqkv_ref, wproj_ref,
+    bias_ref, mask_ref, x_ref, qkv_ref, p_ref, mixed_ref, block_ref, first_ref, last_ref,
 ):
-    x = mm(plan_own[...], own_ref[...]) + mm(plan_west[...], west_ref[...]) + mm(plan_south[...], south_ref[...])
+    x = (
+        mm(plan_own[...], own_ref[...]) + mm(plan_west[...], west_ref[...])
+        + mm(plan_south[...], south_ref[...]) + mm(plan_corner[...], corner_ref[...])
+    )
     x_ref[...] = x.astype(BF)
     (hat,), _ = norm_parts([x], 512)
     normed = (hat * gain_ref[...]).astype(BF)
@@ -208,70 +220,104 @@
     attended = mm(mixed_ref[...], wproj_ref[...]).astype(BF)
     block = (x + attended.astype(F32)).astype(BF)
     block_ref[...] = block
-    edge_ref[...] = mm(plan_edge[...], block).astype(BF)
-
-
-def attend(own, west, south, gain, wqkv, wproj, bias, mask):
-    shapes = [(TOK, 512), (TOK, 1536), (2 * HEADS, WIN, WIN), (TOK, 512), (TOK, 512), (96, 512)]
+    edge = mm(plan_edge[...], block).astype(BF)
+    first_ref[...] = edge[:48]
+    last_ref[...] = edge[48:]
+
+
+def attend(own, west, south, corner, gain, wqkv, wproj, bias, mask):
+    shapes = [(TOK, 512), (TOK, 1536), (2 * HEADS, WIN, WIN), (TOK, 512), (TOK, 512), (48, 512), (48, 512)]
     return pl.pallas_call(
         attend_kernel,
         out_shape=[jax.ShapeDtypeStruct(s, BF) for s in shapes],
-        in_specs=vmem(12),
-        out_specs=vmem(6),
-        compiler_params=PARAMS,
-    )(own, west, south, plan("own"), plan("west"), plan("south"), plan("edge"), gain, wqkv, wproj, bias, mask)
-
-
-def merge_kernel(
-    block_ref, prev_ref, next_ref, cot_ref, cot_west_ref, cot_south_ref, quad_own, quad_prev, quad_next, quad_t,
-    plan_cot, plan_cot_west, plan_cot_south, coarse, gain_ref, wmerge_ref,
-    merged_ref, back_ref, gain_grad_ref, parts_ref,
+        in_specs=vmem(14),
+        out_specs=vmem(7),
+        compiler_params=PARAMS,
+        cost_estimate=cost(4_000_000_000, 8_000_000),
+    )(own, west, south, corner, plan("own"), plan("west"), plan("south"), plan("corner"), plan("edge"), gain, wqkv, wproj, bias, mask)
+
+
+def stack_kernel(
+    block_ref, prev_ref, next_ref, cot_ref, cot_west_ref, cot_south_ref, cot_corner_ref, quad_own, quad_prev, quad_next,
+    plan_cot, plan_cot_west, plan_cot_south, plan_cot_corner, gain_ref, pair_ref, hats_ref, scale_ref, all_cot_ref,
 ):
     stacked = mm(quad_own[...], block_ref[...]) + mm(quad_prev[...], prev_ref[...]) + mm(quad_next[...], next_ref[...])
     values = [stacked[96 * k : 96 * k + 96] for k in range(4)]
     hats, scale = norm_parts(values, 2048)
+    scale_ref[...] = jnp.broadcast_to(scale, (96, 128))
+    normed = []
+    for k in range(4):
+        hats_ref[k] = hats[k]
+        normed.append((hats[k] * gain_ref[:, 512 * k : 512 * k + 512]).astype(BF))
+    cot = (
+        mm(plan_cot[...], cot_ref[...]) + mm(plan_cot_west[...], cot_west_ref[...])
+        + mm(plan_cot_south[...], cot_south_ref[...]) + mm(plan_cot_corner[...], cot_corner_ref[...])
+    )
+    all_cot_ref[...] = cot.astype(BF)
+    counted = lax.broadcasted_iota(jnp.int32, (80, 1024), 0) < 72
+    cot_own = jnp.where(counted, cot[:80], 0.0).astype(BF)
+    for c in range(2):
+        halves = [cot_own[:, 512 * yh + 256 * c : 512 * yh + 256 * c + 256] for yh in range(2)]
+        for xy in range(8):
+            peer = 2 * xy + c
+            pair_ref[peer, :, :256] = normed[xy // 2][:80, 256 * (xy % 2) : 256 * (xy % 2) + 256]
+            pair_ref[peer, :, 256:512] = halves[0]
+            pair_ref[peer, :, 512:] = halves[1]
+
+
+def stack(block, prev, following, cot, cot_west, cot_south, cot_corner, gain):
+    shapes = [
+        jax.ShapeDtypeStruct((16, 80, 768), BF), jax.ShapeDtypeStruct((4, 96, 512), F32),
+        jax.ShapeDtypeStruct((96, 128), F32), jax.ShapeDtypeStruct((96, 1024), BF),
+    ]
+    names = ("quad_own", "quad_prev", "quad_next", "cot_own", "cot_west", "cot_south", "cot_corner")
+    return pl.pallas_call(
+        stack_kernel,
+        out_shape=shapes,
+        in_specs=vmem(15),
+        out_specs=vmem(4),
+        compiler_params=PARAMS,
+        cost_estimate=cost(2_000_000_000, 8_000_000),
+    )(block, prev, following, cot, cot_west, cot_south, cot_corner, *[plan(n) for n in names], gain)
+
+
+def merge_kernel(
+    hats_ref, scale_ref, all_cot_ref, quad_t, coarse, gain_ref, wmerge_ref, merged_ref, back_ref, gain_grad_ref,
+):
     gains = [gain_ref[:, 512 * k : 512 * k + 512] for k in range(4)]
+    hats = [hats_ref[k] for k in range(4)]
+    scale = scale_ref[:, :1]
+    cot_all = all_cot_ref[...]
+    cots = [mm_nt(cot_all, wmerge_ref[512 * k : 512 * k + 512, :]).astype(BF).astype(F32) for k in range(4)]
+    pulled = norm_back(hats, scale, cots, gains, 2048)
+    back_ref[...] = mm(quad_t[...], jnp.concatenate(pulled, axis=0).astype(BF)).astype(BF)
     normed = [(h * g).astype(BF) for h, g in zip(hats, gains)]
     merged = sum(mm(normed[k], wmerge_ref[512 * k : 512 * k + 512, :]) for k in range(4)).astype(BF)
     merged_ref[...] = mm(coarse[...], merged).astype(BF)
-    cot = (
-        mm(plan_cot[...], cot_ref[...]) + mm(plan_cot_west[...], cot_west_ref[...])
-        + mm(plan_cot_south[...], cot_south_ref[...])
-    )
-    cot_all = cot.astype(BF)
-    counted = lax.broadcasted_iota(jnp.int32, (96, 1024), 0) < 72
-    cot_own = jnp.where(counted, cot, 0.0).astype(BF)
-    cots = [mm_nt(cot_all, wmerge_ref[512 * k : 512 * k + 512, :]).astype(BF).astype(F32) for k in range(4)]
     for k in range(4):
-        gain_grad_ref[:, 512 * k : 512 * k + 512] = jnp.sum((cots[k] * hats[k])[:72], axis=0, keepdims=True)
-    pulled = norm_back(hats, scale, cots, gains, 2048)
-    back_ref[...] = mm(quad_t[...], jnp.concatenate(pulled, axis=0).astype(BF)).astype(BF)
-    for k in range(4):
-        for lat in range(4):
-            grad = mm_tn(normed[k], cot_own[:, 256 * lat : 256 * lat + 256])
-            for t in range(2):
-                piece = grad[:, 128 * t : 128 * t + 128].reshape(2, 8, 32, 128).astype(BF)
-                parts_ref[lat % 2, 2 * k : 2 * k + 2, :, lat // 2, 32 * t : 32 * t + 32, :] = piece
-
-
-def merge(block, prev, following, cot, cot_west, cot_south, gain, wmerge):
+        summed = jnp.sum((cots[k] * hats[k])[:72], axis=0, keepdims=True)
+        for i in range(4):
+            gain_grad_ref[4 * k + i : 4 * k + i + 1, :] = summed[:, 128 * i : 128 * i + 128]
+
+
+def merge(hats, scale, all_cot, gain, wmerge):
     shapes = [
         jax.ShapeDtypeStruct((72, 1024), BF), jax.ShapeDtypeStruct((TOK, 512), BF),
-        jax.ShapeDtypeStruct((1, 2048), F32), jax.ShapeDtypeStruct((2, 8, 8, 2, 64, 128), BF),
+        jax.ShapeDtypeStruct((16, 128), F32),
     ]
-    names = ("quad_own", "quad_prev", "quad_next", "quad_t", "cot_own", "cot_west", "cot_south", "coarse")
     return pl.pallas_call(
         merge_kernel,
         out_shape=shapes,
-        in_specs=vmem(16),
-        out_specs=vmem(4),
-        compiler_params=PARAMS,
-    )(block, prev, following, cot, cot_west, cot_south, *[plan(n) for n in names], gain, wmerge)
+        in_specs=vmem(7),
+        out_specs=vmem(3),
+        compiler_params=PARAMS,
+        cost_estimate=cost(4_000_000_000, 16_000_000),
+    )(hats, scale, all_cot, plan("quad_t"), plan("coarse"), gain, wmerge)
 
 
 def back_kernel(
-    cot_ref, x_ref, qkv_ref, p_ref, mixed_ref, wqkv_ref, wproj_ref, gain_ref, spread_t, back_plan,
-    grad_ref, gain_grad_ref, bias_grad_ref, parts_ref, dqkv_ref, left_ref, right_ref, wide_ref,
+    core_ref, cot_ref, x_ref, qkv_ref, p_ref, mixed_ref, wqkv_ref, wproj_ref, gain_ref, merge_gain_ref, spread_t, back_plan,
+    grad_ref, small_ref, mine_ref, theirs_ref, dqkv_ref, left_ref, right_ref, wide_ref,
 ):
     cot = cot_ref[...]
     mixed_cot = mm_nt(cot, wproj_ref[...]).astype(BF)
@@ -313,18 +359,27 @@
     gain = gain_ref[...]
     normed = (hat * gain).astype(BF)
     normed_cot = mm_nt(dqkv, wqkv_ref[...]).astype(BF).astype(F32)
-    gain_grad_ref[...] = jnp.sum(normed_cot * hat, axis=0, keepdims=True)
+    gain_grad = jnp.sum(normed_cot * hat, axis=0, keepdims=True)
+    small_ref[48:64, :] = merge_gain_ref[...]
+    small_ref[64:80, :] = jnp.zeros((16, 128), F32)
+    for i in range(4):
+        small_ref[64 + i : 65 + i, :] = gain_grad[:, 128 * i : 128 * i + 128]
     (pulled,) = norm_back([hat], scale, [normed_cot], [gain], 512)
     total = (cot.astype(F32) + pulled.astype(BF).astype(F32)).astype(BF)
     grad_ref[...] = mm(back_plan[...], total).astype(BF)
     mixed = mixed_ref[...]
-    for lat in range(4):
-        grad = mm_tn(normed, dqkv[:, 384 * lat : 384 * lat + 384])
-        proj = mm_tn(mixed, cot[:, 128 * lat : 128 * lat + 128])
-        tiles = [grad[:, 128 * t : 128 * t + 128].reshape(8, 8, 8, 128) for t in range(3)] + [proj.reshape(8, 8, 8, 128)]
-        for t in range(2):
-            piece = jnp.concatenate([tiles[2 * t], tiles[2 * t + 1]], axis=2).astype(BF)
-            parts_ref[lat % 2, :, :, lat // 2, 16 * t : 16 * t + 16, :] = piece
+    core = core_ref[0]
+    for yh in range(2):
+        for out_ref, owner in ((theirs_ref, 1 - core), (mine_ref, core)):
+            first = pl.multiple_of(768 * yh + 384 * owner, 128)
+            grad = mm_tn(normed, dqkv_ref[:, pl.ds(first, 384)])
+            proj = mm_tn(mixed, cot_ref[:, pl.ds(pl.multiple_of(256 * yh + 128 * owner, 128), 128)])
+            tiles = [grad[:, 128 * t : 128 * t + 128] for t in range(3)] + [proj]
+            for xy in range(8):
+                chunk = [v[64 * xy : 64 * xy + 64].reshape(8, 8, 128) for v in tiles]
+                for t in range(2):
+                    piece = jnp.concatenate([chunk[2 * t], chunk[2 * t + 1]], axis=1).astype(BF)
+                    out_ref[xy, :, yh, 16 * t : 16 * t + 16, :] = piece
     wide_ref[...] = mm(left_ref[...].astype(BF), spread_t[:128, :]) + mm(right_ref[...].astype(BF), spread_t[128:, :])
     blank = jnp.zeros((8, 512 - SPAN), F32)
     levels = []
@@ -338,22 +393,24 @@
                 inner = here if inner is None else pltpu.roll(inner, 1, 1) + here
             outer = inner if outer is None else pltpu.roll(outer, 23, 1) + inner
         levels.append(jnp.concatenate([outer, jnp.zeros((8, 256), F32)], axis=1))
-    bias_grad_ref[...] = levels[0] + pltpu.roll(levels[1], 253, 1)
-
-
-def attend_back(cot, x, qkv, p, mixed, wqkv, wproj, gain):
+    bias_grad = levels[0] + pltpu.roll(levels[1], 253, 1)
+    for i in range(6):
+        small_ref[8 * i : 8 * i + 8, :] = bias_grad[:, 128 * i : 128 * i + 128]
+
+
+def attend_back(core, cot, x, qkv, p, mixed, wqkv, wproj, gain, merge_gain):
     shapes = [
-        jax.ShapeDtypeStruct((TOK, 512), BF), jax.ShapeDtypeStruct((1, 512), F32),
-        jax.ShapeDtypeStruct((8, 768), F32), jax.ShapeDtypeStruct((2, 8, 8, 2, 32, 128), BF),
-    ]
+        jax.ShapeDtypeStruct((TOK, 512), BF), jax.ShapeDtypeStruct((80, 128), F32),
+    ] + [jax.ShapeDtypeStruct((8, 8, 2, 32, 128), BF)] * 2
     return pl.pallas_call(
         back_kernel,
         out_shape=shapes,
-        in_specs=vmem(10),
+        in_specs=[pl.BlockSpec(memory_space=pltpu.SMEM)] + vmem(11),
         out_specs=vmem(4),
         scratch_shapes=[pltpu.VMEM((TOK, 1536), BF), pltpu.VMEM((8 * WIN, 128), F32), pltpu.VMEM((8 * WIN, 128), F32), pltpu.VMEM((8 * WIN, SPAN), F32)],
         compiler_params=PARAMS,
-    )(cot, x, qkv, p, mixed, wqkv, wproj, gain, plan("spread_t"), plan("back"))
+        cost_estimate=cost(8_000_000_000, 16_000_000),
+    )(core, cot, x, qkv, p, mixed, wqkv, wproj, gain, merge_gain, plan("spread_t"), plan("back"))
 
 
 def total_of(axes):
@@ -368,27 +425,106 @@
     return lax.ppermute(block, axes, [((i - distance) % count, i) for i in range(count)])
 
 
-def exchange(parts, small, axes):
-    count = parts.shape[0]
-    rows = jnp.broadcast_to(small.astype(BF)[None], (count,) + small.shape)
-    sent = jnp.concatenate([parts.astype(BF).reshape(count, -1, 128), rows], axis=1)
-    got = lax.all_to_all(sent, axes, 0, 0, tiled=True)
-    total = jnp.sum(got.astype(F32), axis=0)
-    body = total[: sent.shape[1] - small.shape[0]]
-    return body.reshape(parts.shape[1:]), total[sent.shape[1] - small.shape[0] :]
-
-
-def reduce_all(early, late, vectors):
-    parts = jnp.concatenate([late, early], axis=4).reshape(2, 8, 16, 96, 128)
-    small = jnp.concatenate([v.reshape(-1, 128) for v in vectors], axis=0)
-    small = jnp.pad(small, ((0, 80 - small.shape[0]), (0, 0)))
-    for axes in (CORE, NEAR, FAR):
-        parts, small = exchange(parts, small, axes)
-
-    def whole(block, rows, tiles_wide):
-        return block.reshape(tiles_wide, rows, 128).transpose(1, 0, 2).reshape(rows, tiles_wide * 128)
-
-    return whole(parts[:24], 8, 3), parts[24:32], whole(parts[32:], 32, 2), small
+def pack_kernel(mine_ref, theirs_ref, small_ref, small_theirs_ref, out_ref):
+    out_ref[:, :512, :] = (mine_ref[...].astype(F32) + theirs_ref[...].astype(F32)).astype(BF)
+    small = (small_ref[...] + small_theirs_ref[...]).astype(BF)
+    for i in range(8):
+        out_ref[i, 512:, :] = small
+
+
+def pack(mine, theirs, small, small_theirs):
+    return pl.pallas_call(
+        pack_kernel,
+        out_shape=jax.ShapeDtypeStruct((8, 592, 128), BF),
+        in_specs=vmem(4),
+        out_specs=vmem(1)[0],
+        compiler_params=PARAMS,
+    )(mine, theirs, small, small_theirs)
+
+
+def pair_kernel(early_ref, out_ref):
+    tokens = early_ref[...].reshape(1280, 768)
+    grad = mm_tn(tokens[:, :256], tokens[:, 256:])
+    for z in range(8):
+        for yh in range(2):
+            for t in range(2):
+                piece = grad[32 * z : 32 * z + 32, 256 * yh + 128 * t : 256 * yh + 128 * t + 128]
+                out_ref[2 * z + yh, 32 * t : 32 * t + 32, :] = piece.astype(BF)
+
+
+def pair_grad(early):
+    return pl.pallas_call(
+        pair_kernel,
+        out_shape=jax.ShapeDtypeStruct((16, 64, 128), BF),
+        in_specs=vmem(1),
+        out_specs=vmem(1)[0],
+        compiler_params=PARAMS,
+    )(early)
+
+
+def fold_kernel(early_ref, late_ref, out_ref):
+    out_ref[:, :64, :] = early_ref[...]
+    late = jnp.sum(late_ref[...].astype(F32), axis=0).astype(BF)
+    out_ref[:, 64:96, :] = late[:512].reshape(16, 32, 128)
+    for i in range(16):
+        out_ref[i, 96:, :] = late[512:]
+
+
+def fold(early, late):
+    return pl.pallas_call(
+        fold_kernel,
+        out_shape=jax.ShapeDtypeStruct((16, 176, 128), BF),
+        in_specs=vmem(2),
+        out_specs=vmem(1)[0],
+        compiler_params=PARAMS,
+    )(early, late)
+
+
+def unpack_kernel(got_ref, qkv_ref, proj_ref, merge_ref, norm_gain_ref, merge_gain_ref, bias_ref):
+    total = jnp.sum(got_ref[...].astype(F32), axis=0)
+    for t in range(2):
+        merge_ref[:, 128 * t : 128 * t + 128] = total[32 * t : 32 * t + 32]
+    for t in range(3):
+        qkv_ref[:, 128 * t : 128 * t + 128] = total[64 + 8 * t : 72 + 8 * t]
+    proj_ref[...] = total[88:96]
+    for t in range(6):
+        width = min(128, TABLE - 128 * t)
+        bias_ref[:, 128 * t : 128 * t + width] = total[96 + 8 * t : 104 + 8 * t, :width]
+    merge_gain_ref[...] = total[144:160]
+    norm_gain_ref[...] = total[160:168]
+
+
+def unpack(got):
+    shapes = [(8, 384), (8, 128), (32, 256), (8, 128), (16, 128), (8, TABLE)]
+    return pl.pallas_call(
+        unpack_kernel,
+        out_shape=[jax.ShapeDtypeStruct(s, F32) for s in shapes],
+        in_specs=vmem(1),
+        out_specs=vmem(6),
+        compiler_params=PARAMS,
+    )(got)
+
+
+def swapped(value, axis, bit):
+    count = lax.axis_size(axis)
+    return lax.ppermute(value, axis, [(i ^ bit, i) for i in range(count)])
+
+
+def diagonal(block, distance):
+    route = [(((i // 4 - distance) % 64) * 4 + (i % 4 - distance) % 4, i) for i in range(256)]
+    return lax.ppermute(block, AXES, route)
+
+
+def spread_over(parts, axes):
+    return lax.all_to_all(parts, axes, 0, 0, tiled=True)
+
+
+def home(field, rows, width):
+    north = moved(field[rows:, :width], LAT, 1)
+    east = moved(field[:rows, width:], LON, 1)
+    corner = diagonal(field[rows:, width:], 1)
+    top = jnp.concatenate([corner, north], axis=1)
+    return jnp.concatenate([top, jnp.concatenate([east, field[:rows, :width]], axis=1)], axis=0)
 
 
 def on_device(features, norm_gain, qkv_weight, proj_weight, bias_table, merge_gain, merge_weight, merged_cot):
@@ -397,41 +533,53 @@
     own = features.transpose(1, 2, 0, 3).reshape(6, 48, 512)
     cot = merged_cot.transpose(1, 2, 0, 3).reshape(3, 24, 1024)
     west = moved(own[:, :24], LON, -1)
-    cot_west = moved(cot[:, :12], LON, -1)
-    south = moved(jnp.concatenate([own[:3, 24:], west[:3]], axis=1), LAT, -1)
-    cot_south = moved(jnp.concatenate([cot[:2, 12:], cot_west[:2]], axis=1), LAT, -1)
+    south = moved(own[:3, 24:], LAT, -1)
+    corner = diagonal(own[:3, :24], -1)
     bias, mask = bias_of(bias_table, last)
-    x, qkv, p, mixed, block, edge = attend(
-        own.reshape(TOK, 512), west.reshape(144, 512), south.reshape(144, 512), gain, qkv_weight, proj_weight, bias, mask
-    )
-    following = moved(edge[:48], LAT, -1)
-    prev = moved(edge[48:], LAT, 1)
-    merged, attn_cot, merge_gain_part, early = merge(
-        block, prev, following, cot.reshape(72, 1024), cot_west.reshape(36, 1024), cot_south.reshape(48, 1024),
-        wide_gain, merge_weight,
-    )
-    grad, norm_gain_part, bias_part, late = attend_back(
-        attn_cot, x, qkv, p, mixed, qkv_weight, proj_weight, gain
-    )
-
-    def home(field, rows_back, width_back):
-        north = moved(field[field.shape[0] - rows_back :], LAT, 1)
-        field = jnp.concatenate([north, field[: field.shape[0] - rows_back]], axis=0)
-        east = moved(field[:, field.shape[1] - width_back :], LON, 1)
-        return jnp.concatenate([east, field[:, : field.shape[1] - width_back]], axis=1)
-
-    merged = home(merged.reshape(3, 24, 1024), 1, 12).reshape(3, 6, 4, 1024).transpose(2, 0, 1, 3)
-    features_grad = home(grad.reshape(6, 48, 512), 3, 24).reshape(6, 12, 4, 512).transpose(2, 0, 1, 3)
-    qkv_grad, proj_grad, merge_grad, small = reduce_all(early, late, (norm_gain_part, merge_gain_part, bias_part))
+    flat = own.reshape(TOK, 512)
+    flat, bias, mask, west, south, corner = lax.optimization_barrier((flat, bias, mask, west, south, corner))
+    x, qkv, p, mixed, block, first, final = attend(
+        flat, west.reshape(144, 512), south.reshape(72, 512), corner.reshape(72, 512),
+        gain, qkv_weight, proj_weight, bias, mask,
+    )
+    following = moved(first, LAT, -1)
+    prev = moved(final, LAT, 1)
+    cot, block = lax.optimization_barrier((cot, block))
+    cot_west = moved(cot[1:, :12], LON, -1)
+    cot_south = moved(cot[:2, 12:], LAT, -1)
+    cot_corner = diagonal(cot[:2, :12], -1)
+    core = lax.axis_index("c").astype(jnp.int32).reshape(1)
+    pair, hats, scale, all_cot = stack(
+        block, prev, following, cot.reshape(72, 1024), cot_west.reshape(24, 1024), cot_south.reshape(24, 1024),
+        cot_corner.reshape(24, 1024), wide_gain,
+    )
+    early = spread_over(pair, CLOSE)
+    merged, attn_cot, merge_gain_part = merge(hats, scale, all_cot, wide_gain, merge_weight)
+    merged = home(merged.reshape(3, 24, 1024), 2, 12)
+    grad, small, late, late_out = attend_back(
+        core, attn_cot, x, qkv, p, mixed, qkv_weight, proj_weight, gain, merge_gain_part
+    )
+
+    late_theirs, small_theirs = swapped(late_out, "c", 1), swapped(small, "c", 1)
+    late = pack(late.reshape(8, 512, 128), late_theirs.reshape(8, 512, 128), small, small_theirs)
+    late, early = lax.optimization_barrier((late, early))
+    late = spread_over(late, NEAR)
+    early = pair_grad(early)
+    grad = home(grad.reshape(6, 48, 512), 3, 24)
+    late, early, grad, merged = lax.optimization_barrier((late, early, grad, merged))
+    merged = merged.reshape(3, 6, 4, 1024).transpose(2, 0, 1, 3)
+    features_grad = grad.reshape(6, 12, 4, 512).transpose(2, 0, 1, 3)
+    got = spread_over(fold(early, late), FAR)
+    qkv_grad, proj_grad, merge_grad, norm_gain_grad, merge_gain_grad, bias_grad = unpack(got)
     return (
         merged,
         features_grad,
         qkv_grad,
         proj_grad,
         merge_grad,
-        small[:4].reshape(-1),
-        small[4:20].reshape(-1),
-        small[20:68].reshape(8, 768)[:, :TABLE],
+        norm_gain_grad[:4].reshape(-1),
+        merge_gain_grad.reshape(-1),
+        bias_grad,
     )
 
 

time: 177 us -> 136 us (0.77)
  blocking collectives: 55.9 us -> 0 us
  other arithmetic: 23.9 us -> 0.07 us
  waiting for transfers between devices: 20.8 us -> 36.9 us
  starting transfers between devices: 25.2 us -> 39.7 us
  Pallas kernels: 32.5 us -> 43.2 us
  local copies, waits for them, and re-layouts: 16 us -> 14 us
    all_to_all x2 -> x0, blocking collectives: 55.9 us -> none  [exchange(): got = lax.all_to_all(sent, axes, 0, 0, tiled=True)]
    all_to_all x1 -> x3, waiting for transfers between devices: 0.01 us -> 20.7 us  [spread_over(): return lax.all_to_all(parts, axes, 0, 0, tiled=True)]
    concatenate x11 -> x2, other arithmetic: 13 us -> 0.07 us  [home(): jnp.concatenate([top, jnp.concatenate([east, field[:rows, :width]], axis=...]
    all_to_all x1 -> x3, starting transfers between devices: 7.07 us -> 19 us  [spread_over(): return lax.all_to_all(parts, axes, 0, 0, tiled=True)]
    pallas_call x2 -> x7, Pallas kernels: 22.7 us -> 33.2 us  [the longest x1 13.5 us: attend_back(): pl.pallas_call(back_kernel, out_shape=shapes, in_specs=[pl.BlockSpec(memo...]
    reduce_sum x3 -> x0, other arithmetic: 9.45 us -> none  [exchange(): total = jnp.sum(got.astype(F32), axis=0)]
    ppermute x10, waiting for transfers between devices: 20.8 us -> 11.5 us  [moved(): lax.ppermute(block, axes, [((i - distance) % count, i) for i in range(cou...]
    ppermute x0 -> x6, starting transfers between devices: none -> 8.6 us  [the longest x4 8.09 us: diagonal(): return lax.ppermute(block, AXES, route)]
  transfers between devices with their start and end apart: 11 -> 19, of which waited for: 5 -> 9; matrix products, arithmetic and copies ran while one was open for 5% -> 6% of each run, Pallas kernels for 6% -> 21%
where the time goes in v1:
time: 136 us; the launch traced here: 135 us
  Pallas kernels  43.2 us (32%)
  starting transfers between devices  39.7 us (29%)
  waiting for transfers between devices  36.9 us (27%)
  local copies, waits for them, and re-layouts  14 us (10%)
    all_to_all x3, waiting for transfers between devices, spread_over(): return lax.all_to_all(parts, axes, 0, 0, tiled=True)  20.7 us
    all_to_all x3, starting transfers between devices, spread_over(): return lax.all_to_all(parts, axes, 0, 0, tiled=True)  19 us
    pallas_call x1, Pallas kernels, attend_back(): pl.pallas_call(back_kernel, out_shape=shapes, in_specs=[pl.BlockSpec(memo...  13.5 us
    ppermute x10, starting transfers between devices, moved(): lax.ppermute(block, axes, [((i - distance) % count, i) for i in range(cou...  12.1 us
    ppermute x10, waiting for transfers between devices, moved(): lax.ppermute(block, axes, [((i - distance) % count, i) for i in range(cou...  11.5 us
    ppermute x4, starting transfers between devices, diagonal(): return lax.ppermute(block, AXES, route)  8.09 us
    pallas_call x1, Pallas kernels, attend(): pl.pallas_call(attend_kernel, out_shape=[jax.ShapeDtypeStruct(s, BF) for...  6.3 us
    pallas_call x1, Pallas kernels, merge(): pl.pallas_call(merge_kernel, out_shape=shapes, in_specs=vmem(7), out_spec...  6.04 us
  transfers between devices with their start and end apart: 19, of which 9 were waited for; matrix products, arithmetic and copies ran while one was open for 6% of the time, Pallas kernels for 21%

profile of v1, /device:TPU:8, one launch (start us, length us, event | category | flops | bytes accessed | tf_op | source)
XLA Modules:
  0.0 134.6 jit_solution(13998338976010477984)
XLA Ops:
  0.6 1.0 reshape.85
  1.7 6.4 %collective-permute-start.2 = (bf16[3,24,512]{2,1,0:T(8,128)(2,1)S(1)}, bf16[3,24,512]{2,1,0:T(8,128)(2,1)S(1)}, u32[]{:S(2)}, u32[]{:S(2)}) collective-permute-start(bf16[3,24,512]{2,1,0:T(8,128)(2,1)S(1)} %get-tuple-element.92), channel_id=1, source_target_pairs={{5,0},{6,1},{7,2},{4,3},{9,4},{10,5},{11,6},{8,7},{13,8},{14,9},{1... | collective-permute-start | bytes 221192 | tf_op jit(solution)/shard_map/ppermute | solution.py:515
  8.1 1.7 %collective-permute-start.1 = (bf16[3,24,512]{2,1,0:T(8,128)(2,1)S(1)}, bf16[3,24,512]{2,1,0:T(8,128)(2,1)S(1)}, u32[]{:S(2)}, u32[]{:S(2)}) collective-permute-start(bf16[3,24,512]{2,1,0:T(8,128)(2,1)S(1)} %get-tuple-element.93), channel_id=1, source_target_pairs={{1,0},{2,1},{3,2},{0,3},{5,4},{6,5},{7,6},{4,7},{9,8},{10,9},{11,1... | collective-permute-start | bytes 221192 | tf_op jit(solution)/shard_map/ppermute | solution.py:425
  9.8 1.7 %collective-permute-start = (bf16[6,24,512]{2,1,0:T(8,128)(2,1)S(1)}, bf16[6,24,512]{2,1,0:T(8,128)(2,1)S(1)}, u32[]{:S(2)}, u32[]{:S(2)}) collective-permute-start(bf16[6,24,512]{2,1,0:T(8,128)(2,1)S(1)} %slice.60), channel_id=1, source_target_pairs={{4,0},{8,4},{12,8},{16,12},{20,16},{24,20},{28,24},{32,28},{36,32}... | collective-permute-start | bytes 442376 | tf_op jit(solution)/shard_map/ppermute | solution.py:425
  11.5 1.3 %pad.4.table_ref = f32[8,768]{1,0:T(8,128)} pad(f32[8,759]{1,0:T(8,128)} %param.31, f32[]{:T(128)} %constant.50.clone.1), padding=0_0x0_9 | pad | bytes 48868 | tf_op jit(solution)/shard_map/jit(_pad)/pad | solution.py:166
  12.9 3.6 %shard_map.314 = (f32[8,144,144]{2,1,0:T(8,128)}, f32[2,144,144]{2,1,0:T(8,128)}) custom-call(s32[1]{0:T(128)} %bitcast.3.last_ref, f32[8,768]{1,0:T(8,128)} %pad.4.table_ref, bf16[384,256]{1,0:T(8,128)(2,1)} %constant.51.clone.spread_ref, bf16[144,144]{1,0:T(8,128)(2,1)} %constant.52.clone.level_ref, bf16[144,144]{1,0:T(8,128)(2,1)} %constant.53.clone.north_ref), custom_call_target="tpu_custom_call" | custom-call | flops 2000000000 | bytes 4000000 | tf_op jit(solution)/shard_map/pallas_call | solution.py:158
  18.1 6.3 %shard_map.315 = (bf16[288,512]{1,0:T(8,128)(2,1)}, bf16[288,1536]{1,0:T(8,128)(2,1)}, bf16[16,144,144]{2,1,0:T(8,128)(2,1)}, bf16[288,512]{1,0:T(8,128)(2,1)}, ...) custom-call(bf16[288,512]{1,0:T(8,128)(2,1)} %reshape_reshape.3.own_ref, ...), custom_call_target="tpu_custom_call" | custom-call | flops 4000000000 | bytes 8000000 | tf_op jit(solution)/shard_map/pallas_call | solution.py:230
  24.6 1.7 %collective-permute-start.6 = (bf16[2,12,1024]{2,1,0:T(8,128)(2,1)S(1)}, bf16[2,12,1024]{2,1,0:T(8,128)(2,1)S(1)}, u32[]{:S(2)}, u32[]{:S(2)}) collective-permute-start(bf16[2,12,1024]{2,1,0:T(8,128)(2,1)S(1)} %get-tuple-element.99), channel_id=1, source_target_pairs={{1,0},{2,1},{3,2},{0,3},{5,4},{6,5},{7,6},{4,7},{9,8},{10,9},{11,1... | collective-permute-start | bytes 147464 | tf_op jit(solution)/shard_map/ppermute | solution.py:425
  26.7 3.2 %collective-permute-start.4 = (bf16[48,512]{1,0:T(8,128)(2,1)}, bf16[48,512]{1,0:T(8,128)(2,1)S(1)}, u32[]{:S(2)}, u32[]{:S(2)}) collective-permute-start(bf16[48,512]{1,0:T(8,128)(2,1)} %get-tuple-element.59), channel_id=1, source_target_pairs={{1,0},{2,1},{3,2},{0,3},{5,4},{6,5},{7,6},{4,7},{9,8},{10,9},{11,1... | collective-permute-start | bytes 147464 | tf_op jit(solution)/shard_map/ppermute | solution.py:425
  32.8 3.8 %shard_map.316 = (bf16[16,80,768]{2,1,0:T(8,128)(2,1)}, f32[4,96,512]{2,1,0:T(8,128)}, f32[96,128]{1,0:T(8,128)}, bf16[96,1024]{1,0:T(8,128)(2,1)}) custom-call(bf16[288,512]{1,0:T(8,128)(2,1)} %get-tuple-element.57.block_ref, bf16[48,512]{1,0:T(8,128)(2,1)} %copy-done.12, bf16[48,512]{1,0:T(8,128)(2,1)} %copy-done.13, bf16[72,1024]{1,0:T(8,128)(2,1)} %bitcast.23, ...), custom_call_target="tpu_custom_call" | custom-call | flops 2000000000 | bytes 8000000 | tf_op jit(solution)/shard_map/pallas_call | solution.py:274
  36.6 9.3 %all-to-all-start = ((bf16[16,80,768]{2,1,0:T(8,128)(2,1)}), bf16[16,80,768]{2,1,0:T(8,128)(2,1)S(1)}, u32[]{:S(2)}, u32[]{:S(2)}) async-start(bf16[16,80,768]{2,1,0:T(8,128)(2,1)} %get-tuple-element.73), calls=%async_computation | async-start | bytes 3932160 | tf_op jit(solution)/shard_map/all_to_all | solution.py:519
  45.9 6.0 %shard_map.317 = (bf16[72,1024]{1,0:T(8,128)(2,1)}, bf16[288,512]{1,0:T(8,128)(2,1)}, f32[16,128]{1,0:T(8,128)}) custom-call(f32[4,96,512]{2,1,0:T(8,128)} %get-tuple-element.61.hats_ref, f32[96,128]{1,0:T(8,128)} %get-tuple-element.62.scale_ref, bf16[96,1024]{1,0:T(8,128)(2,1)} %get-tuple-element.63.all_cot_ref, bf16[288,384]{1,0:T(8,128)(2,1)} %constant.66.clone.quad_t, ...), custom_call_target="tpu_custom_call" | custom-call | flops 4000000000 | bytes 16000000 | tf_op jit(solution)/shard_map/pallas_call | solution.py:308
  52.0 13.5 %shard_map.318 = (bf16[288,512]{1,0:T(8,128)(2,1)}, f32[80,128]{1,0:T(8,128)}, bf16[8,8,2,32,128]{4,3,2,1,0:T(8,128)(2,1)}, bf16[8,8,2,32,128]{4,3,2,1,0:T(8,128)(2,1)}) custom-call(s32[1]{0:T(128)} %bitcast.core_ref, bf16[288,512]{1,0:T(8,128)(2,1)} %get-tuple-element.64.cot_ref, bf16[288,512]{1,0:T(8,128)(2,1)} %get-tuple-element.65.x_ref, ...), custom_call_target="tpu_custom_call" | custom-call | flops 8000000000 | bytes 16000000 | tf_op jit(solution)/shard_map/pallas_call | solution.py:405
  66.0 2.4 %collective-permute-done.9.small_theirs_ref = f32[80,128]{1,0:T(8,128)S(1)} collective-permute-done((f32[80,128]{1,0:T(8,128)}, f32[80,128]{1,0:T(8,128)S(1)}, u32[]{:S(2)}, u32[]{:S(2)}) %collective-permute-start.9) | collective-permute-done | bytes 40992 | tf_op jit(solution)/shard_map/ppermute | solution.py:510
  69.4 2.8 %shard_map.319 = bf16[8,592,128]{2,1,0:T(8,128)(2,1)} custom-call(bf16[8,512,128]{2,1,0:T(8,128)(2,1)} %bitcast.21, bf16[8,512,128]{2,1,0:T(8,128)(2,1)} %bitcast.22, f32[80,128]{1,0:T(8,128)} %get-tuple-element.72.small_ref, f32[80,128]{1,0:T(8,128)} %copy-done.8), custom_call_target="tpu_custom_call" | custom-call | tf_op jit(solution)/shard_map/pallas_call | solution.py:436
  72.3 5.9 %all-to-all-start.1 = ((bf16[8,592,128]{2,1,0:T(8,128)(2,1)}), bf16[8,592,128]{2,1,0:T(8,128)(2,1)S(1)}, u32[]{:S(2)}, u32[]{:S(2)}) async-start(bf16[8,592,128]{2,1,0:T(8,128)(2,1)} %shard_map.319), calls=%async_computation.1 | async-start | bytes 2424832 | tf_op jit(solution)/shard_map/all_to_all | solution.py:519
  79.1 1.3 collective-permute-start.13
  80.3 1.4 %collective-permute-start.14 = (bf16[1,12,1024]{2,1,0:T(8,128)(2,1)S(1)}, bf16[1,12,1024]{2,1,0:T(8,128)(2,1)S(1)}, u32[]{:S(2)}, u32[]{:S(2)}) collective-permute-start(bf16[1,12,1024]{2,1,0:T(8,128)(2,1)S(1)} %get-tuple-element.95), channel_id=1, source_target_pairs={{3,0},{0,1},{1,2},{2,3},{7,4},{4,5},{5,6},{6,7},{11,8},{8,9},{9,10... | collective-permute-start | bytes 73736 | tf_op jit(solution)/shard_map/ppermute | solution.py:425
  83.4 1.2 collective-permute-done.13
  84.6 1.5 %collective-permute-start.11 = (bf16[3,24,512]{2,1,0:T(8,128)(2,1)S(1)}, bf16[3,24,512]{2,1,0:T(8,128)(2,1)S(1)}, u32[]{:S(2)}, u32[]{:S(2)}) collective-permute-start(bf16[3,24,512]{2,1,0:T(8,128)(2,1)S(1)} %get-tuple-element.91), channel_id=1, source_target_pairs={{3,0},{0,1},{1,2},{2,3},{7,4},{4,5},{5,6},{6,7},{11,8},{8,9},{9,10... | collective-permute-start | bytes 221192 | tf_op jit(solution)/shard_map/ppermute | solution.py:425
  86.1 1.6 %collective-permute-done.14 = bf16[1,12,1024]{2,1,0:T(8,128)(2,1)S(1)} collective-permute-done((bf16[1,12,1024]{2,1,0:T(8,128)(2,1)S(1)}, bf16[1,12,1024]{2,1,0:T(8,128)(2,1)S(1)}, u32[]{:S(2)}, u32[]{:S(2)}) %collective-permute-start.14) | collective-permute-done | bytes 24608 | tf_op jit(solution)/shard_map/ppermute | solution.py:425
  87.7 1.9 %collective-permute-done.15 = bf16[2,12,1024]{2,1,0:T(8,128)(2,1)S(1)} collective-permute-done((bf16[2,12,1024]{2,1,0:T(8,128)(2,1)S(1)}, bf16[2,12,1024]{2,1,0:T(8,128)(2,1)S(1)}, u32[]{:S(2)}, u32[]{:S(2)}) %collective-permute-start.15) | collective-permute-done | bytes 49184 | tf_op jit(solution)/shard_map/ppermute | solution.py:425
  89.6 1.1 collective-permute-done.10
  90.7 2.5 %collective-permute-done.12 = bf16[3,24,512]{2,1,0:T(8,128)(2,1)S(1)} collective-permute-done((bf16[3,24,512]{2,1,0:T(8,128)(2,1)S(1)}, bf16[3,24,512]{2,1,0:T(8,128)(2,1)S(1)}, u32[]{:S(2)}, u32[]{:S(2)}) %collective-permute-start.12) | collective-permute-done | bytes 73760 | tf_op jit(solution)/shard_map/ppermute | solution.py:425
  93.2 5.2 %collective-permute-done.11 = bf16[3,24,512]{2,1,0:T(8,128)(2,1)S(1)} collective-permute-done((bf16[3,24,512]{2,1,0:T(8,128)(2,1)S(1)}, bf16[3,24,512]{2,1,0:T(8,128)(2,1)S(1)}, u32[]{:S(2)}, u32[]{:S(2)}) %collective-permute-start.11) | collective-permute-done | bytes 73760 | tf_op jit(solution)/shard_map/ppermute | solution.py:425
  98.5 2.8 %shard_map.320.early_ref = bf16[16,64,128]{2,1,0:T(8,128)(2,1)} custom-call(bf16[16,80,768]{2,1,0:T(8,128)(2,1)} %copy-done), custom_call_target="tpu_custom_call" | custom-call | tf_op jit(solution)/shard_map/pallas_call | solution.py:456
  101.3 1.0 copy-done.1
  102.3 2.4 %shard_map.321 = bf16[16,176,128]{2,1,0:T(8,128)(2,1)} custom-call(bf16[16,64,128]{2,1,0:T(8,128)(2,1)} %shard_map.320.early_ref, bf16[8,592,128]{2,1,0:T(8,128)(2,1)} %copy-done.1), custom_call_target="tpu_custom_call" | custom-call | tf_op jit(solution)/shard_map/pallas_call | solution.py:474
  104.7 3.8 %all-to-all-start.2 = ((bf16[16,176,128]{2,1,0:T(8,128)(2,1)}), bf16[16,176,128]{2,1,0:T(8,128)(2,1)S(1)}, u32[]{:S(2)}, u32[]{:S(2)}) async-start(bf16[16,176,128]{2,1,0:T(8,128)(2,1)} %shard_map.321), calls=%async_computation.2 | async-start | bytes 1441792 | tf_op jit(solution)/shard_map/all_to_all | solution.py:519
  110.0 20.7 %all-to-all-done.2.got_ref = bf16[16,176,128]{2,1,0:T(8,128)(2,1)S(1)} async-done(((bf16[16,176,128]{2,1,0:T(8,128)(2,1)}), bf16[16,176,128]{2,1,0:T(8,128)(2,1)S(1)}, u32[]{:S(2)}, u32[]{:S(2)}) %all-to-all-start.2) | async-done | bytes 720928 | tf_op jit(solution)/shard_map/all_to_all | solution.py:519
  131.6 1.8 %shard_map.322 = (f32[8,384]{1,0:T(8,128)}, f32[8,128]{1,0:T(8,128)}, f32[32,256]{1,0:T(8,128)}, f32[8,128]{1,0:T(8,128)}, f32[16,128]{1,0:T(8,128)}, /*index=5*/f32[8,759]{1,0:T(8,128)}) custom-call(bf16[16,176,128]{2,1,0:T(8,128)(2,1)} %copy-done.2), custom_call_target="tpu_custom_call" | custom-call | tf_op jit(solution)/shard_map/pallas_call | solution.py:499
  133.4 1.3 slice_bitcast_fusion
  (61 shorter events, 11.4 us)
Async XLA Ops:
  1.7 15.7 %collective-permute-start.2 = (bf16[3,24,512]{2,1,0:T(8,128)(2,1)S(1)}, bf16[3,24,512]{2,1,0:T(8,128)(2,1)S(1)}, u32[]{:S(2)}, u32[]{:S(2)}) collective-permute-start(bf16[3,24,512]{2,1,0:T(8,128)(2,1)S(1)} %get-tuple-element.92), channel_id=1, source_target_pairs={{5,0},{6,1},{7,2},{4,3},{9,4},{10,5},{11,6},{8,7},{13,8},{14,9},{1... | collective-permute-start | bytes 221192 | tf_op jit(solution)/shard_map/ppermute | solution.py:515
  8.1 9.3 %collective-permute-start.1 = (bf16[3,24,512]{2,1,0:T(8,128)(2,1)S(1)}, bf16[3,24,512]{2,1,0:T(8,128)(2,1)S(1)}, u32[]{:S(2)}, u32[]{:S(2)}) collective-permute-start(bf16[3,24,512]{2,1,0:T(8,128)(2,1)S(1)} %get-tuple-element.93), channel_id=1, source_target_pairs={{1,0},{2,1},{3,2},{0,3},{5,4},{6,5},{7,6},{4,7},{9,8},{10,9},{11,1... | collective-permute-start | bytes 221192 | tf_op jit(solution)/shard_map/ppermute | solution.py:425
  9.8 7.6 %collective-permute-start = (bf16[6,24,512]{2,1,0:T(8,128)(2,1)S(1)}, bf16[6,24,512]{2,1,0:T(8,128)(2,1)S(1)}, u32[]{:S(2)}, u32[]{:S(2)}) collective-permute-start(bf16[6,24,512]{2,1,0:T(8,128)(2,1)S(1)} %slice.60), channel_id=1, source_target_pairs={{4,0},{8,4},{12,8},{16,12},{20,16},{24,20},{28,24},{32,28},{36,32}... | collective-permute-start | bytes 442376 | tf_op jit(solution)/shard_map/ppermute | solution.py:425
  12.9 3.7 %copy-start.3 = (bf16[4,6,12,512]{3,0,2,1:T(4,128)(2,1)S(1)}, bf16[4,6,12,512]{3,0,2,1:T(4,128)(2,1)}, u32[]{:S(2)}) copy-start(bf16[4,6,12,512]{3,0,2,1:T(4,128)(2,1)} %param.27) | copy-start | bytes 884740
  12.9 4.4 %copy-start.7 = (bf16[4,3,6,1024]{3,0,2,1:T(4,128)(2,1)S(1)}, bf16[4,3,6,1024]{3,0,2,1:T(4,128)(2,1)}, u32[]{:S(2)}) copy-start(bf16[4,3,6,1024]{3,0,2,1:T(4,128)(2,1)} %param.34) | copy-start | bytes 442372
  17.4 7.1 %copy-start.5 = (bf16[3,24,1024]{2,1,0:T(8,128)(2,1)}, bf16[3,24,1024]{2,1,0:T(8,128)(2,1)S(1)}, u32[]{:S(2)}) copy-start(bf16[3,24,1024]{2,1,0:T(8,128)(2,1)S(1)} %reshape.82) | copy-start | bytes 442372
  17.4 0.7 copy-start.10
  17.4 0.7 copy-start.11
  17.4 0.7 copy-start.9
  24.5 5.4 %collective-permute-start.7 = (bf16[2,12,1024]{2,1,0:T(8,128)(2,1)S(1)}, bf16[2,12,1024]{2,1,0:T(8,128)(2,1)S(1)}, u32[]{:S(2)}, u32[]{:S(2)}) collective-permute-start(bf16[2,12,1024]{2,1,0:T(8,128)(2,1)S(1)} %get-tuple-element.98), channel_id=1, source_target_pairs={{5,0},{6,1},{7,2},{4,3},{9,4},{10,5},{11,6},{8,7},{13,8},{14,9},{1... | collective-permute-start | bytes 147464 | tf_op jit(solution)/shard_map/ppermute | solution.py:515
  24.6 6.0 %collective-permute-start.6 = (bf16[2,12,1024]{2,1,0:T(8,128)(2,1)S(1)}, bf16[2,12,1024]{2,1,0:T(8,128)(2,1)S(1)}, u32[]{:S(2)}, u32[]{:S(2)}) collective-permute-start(bf16[2,12,1024]{2,1,0:T(8,128)(2,1)S(1)} %get-tuple-element.99), channel_id=1, source_target_pairs={{1,0},{2,1},{3,2},{0,3},{5,4},{6,5},{7,6},{4,7},{9,8},{10,9},{11,1... | collective-permute-start | bytes 147464 | tf_op jit(solution)/shard_map/ppermute | solution.py:425
  26.2 5.0 %collective-permute-start.5 = (bf16[2,12,1024]{2,1,0:T(8,128)(2,1)S(1)}, bf16[2,12,1024]{2,1,0:T(8,128)(2,1)S(1)}, u32[]{:S(2)}, u32[]{:S(2)}) collective-permute-start(bf16[2,12,1024]{2,1,0:T(8,128)(2,1)S(1)} %get-tuple-element.100), channel_id=1, source_target_pairs={{4,0},{8,4},{12,8},{16,12},{20,16},{24,20},{28,24},{32,28},{36,32}... | collective-permute-start | bytes 147464 | tf_op jit(solution)/shard_map/ppermute | solution.py:425
  26.7 5.5 %collective-permute-start.3 = (bf16[48,512]{1,0:T(8,128)(2,1)}, bf16[48,512]{1,0:T(8,128)(2,1)S(1)}, u32[]{:S(2)}, u32[]{:S(2)}) collective-permute-start(bf16[48,512]{1,0:T(8,128)(2,1)} %get-tuple-element.58), channel_id=1, source_target_pairs={{3,0},{0,1},{1,2},{2,3},{7,4},{4,5},{5,6},{6,7},{11,8},{8,9},{9,10... | collective-permute-start | bytes 147464 | tf_op jit(solution)/shard_map/ppermute | solution.py:425
  26.7 5.5 %collective-permute-start.4 = (bf16[48,512]{1,0:T(8,128)(2,1)}, bf16[48,512]{1,0:T(8,128)(2,1)S(1)}, u32[]{:S(2)}, u32[]{:S(2)}) collective-permute-start(bf16[48,512]{1,0:T(8,128)(2,1)} %get-tuple-element.59), channel_id=1, source_target_pairs={{1,0},{2,1},{3,2},{0,3},{5,4},{6,5},{7,6},{4,7},{9,8},{10,9},{11,1... | collective-permute-start | bytes 147464 | tf_op jit(solution)/shard_map/ppermute | solution.py:425
  32.2 0.6 copy-start.12
  32.2 0.6 copy-start.13
  36.6 35.7 %all-to-all-start = ((bf16[16,80,768]{2,1,0:T(8,128)(2,1)}), bf16[16,80,768]{2,1,0:T(8,128)(2,1)S(1)}, u32[]{:S(2)}, u32[]{:S(2)}) async-start(bf16[16,80,768]{2,1,0:T(8,128)(2,1)} %get-tuple-element.73), calls=%async_computation | async-start | bytes 3932160 | tf_op jit(solution)/shard_map/all_to_all | solution.py:519
  65.5 2.9 %collective-permute-start.8 = (bf16[8,8,2,32,128]{4,3,2,1,0:T(8,128)(2,1)}, bf16[8,8,2,32,128]{4,3,2,1,0:T(8,128)(2,1)S(1)}, u32[]{:S(2)}, u32[]{:S(2)}) collective-permute-start(bf16[8,8,2,32,128]{4,3,2,1,0:T(8,128)(2,1)} %get-tuple-element.71), channel_id=1, source_target_pairs={{1,0},{0,1},{3,2},{2,3},{5,4},{4,5},{7,6},{6,7},{9,8},{8,9},{11,10... | collective-permute-start | bytes 3145736 | tf_op jit(solution)/shard_map/ppermute | solution.py:510
  65.7 2.8 %collective-permute-start.9 = (f32[80,128]{1,0:T(8,128)}, f32[80,128]{1,0:T(8,128)S(1)}, u32[]{:S(2)}, u32[]{:S(2)}) collective-permute-start(f32[80,128]{1,0:T(8,128)} %get-tuple-element.72.small_ref), channel_id=1, source_target_pairs={{1,0},{0,1},{3,2},{2,3},{5,4},{4,5},{7,6},{6,7},{9,8},{8,9},{11,10... | collective-permute-start | bytes 122888 | tf_op jit(solution)/shard_map/ppermute | solution.py:510
  68.5 1.0 copy-start.4
  72.3 10.7 %copy-start.6 = (bf16[288,512]{1,0:T(8,128)(2,1)S(1)}, bf16[288,512]{1,0:T(8,128)(2,1)}, u32[]{:S(2)}) copy-start(bf16[288,512]{1,0:T(8,128)(2,1)} %get-tuple-element.76) | copy-start | bytes 884740
  72.3 10.8 %copy-start = (bf16[16,80,768]{2,1,0:T(8,128)(2,1)}, bf16[16,80,768]{2,1,0:T(8,128)(2,1)S(1)}, u32[]{:S(2)}) copy-start(bf16[16,80,768]{2,1,0:T(8,128)(2,1)S(1)} %all-to-all-done.early_ref) | copy-start | bytes 5898244
  72.3 28.9 %all-to-all-start.1 = ((bf16[8,592,128]{2,1,0:T(8,128)(2,1)}), bf16[8,592,128]{2,1,0:T(8,128)(2,1)S(1)}, u32[]{:S(2)}, u32[]{:S(2)}) async-start(bf16[8,592,128]{2,1,0:T(8,128)(2,1)} %shard_map.319), calls=%async_computation.1 | async-start | bytes 2424832 | tf_op jit(solution)/shard_map/all_to_all | solution.py:519
  79.1 5.5 %collective-permute-start.13 = (bf16[1,12,1024]{2,1,0:T(8,128)(2,1)S(1)}, bf16[1,12,1024]{2,1,0:T(8,128)(2,1)S(1)}, u32[]{:S(2)}, u32[]{:S(2)}) collective-permute-start(bf16[1,12,1024]{2,1,0:T(8,128)(2,1)S(1)} %get-tuple-element.94), channel_id=1, source_target_pairs={{255,0},{252,1},{253,2},{254,3},{3,4},{0,5},{1,6},{2,7},{7,8},{4,9... | collective-permute-start | bytes 73736 | tf_op jit(solution)/shard_map/ppermute | solution.py:515
  80.3 7.3 %collective-permute-start.14 = (bf16[1,12,1024]{2,1,0:T(8,128)(2,1)S(1)}, bf16[1,12,1024]{2,1,0:T(8,128)(2,1)S(1)}, u32[]{:S(2)}, u32[]{:S(2)}) collective-permute-start(bf16[1,12,1024]{2,1,0:T(8,128)(2,1)S(1)} %get-tuple-element.95), channel_id=1, source_target_pairs={{3,0},{0,1},{1,2},{2,3},{7,4},{4,5},{5,6},{6,7},{11,8},{8,9},{9,10... | collective-permute-start | bytes 73736 | tf_op jit(solution)/shard_map/ppermute | solution.py:425
  82.7 6.9 %collective-permute-start.15 = (bf16[2,12,1024]{2,1,0:T(8,128)(2,1)S(1)}, bf16[2,12,1024]{2,1,0:T(8,128)(2,1)S(1)}, u32[]{:S(2)}, u32[]{:S(2)}) collective-permute-start(bf16[2,12,1024]{2,1,0:T(8,128)(2,1)S(1)} %get-tuple-element.96), channel_id=1, source_target_pairs={{252,0},{0,4},{4,8},{8,12},{12,16},{16,20},{20,24},{24,28},{28,32}... | collective-permute-start | bytes 147464 | tf_op jit(solution)/shard_map/ppermute | solution.py:425
  83.1 7.6 %collective-permute-start.10 = (bf16[3,24,512]{2,1,0:T(8,128)(2,1)S(1)}, bf16[3,24,512]{2,1,0:T(8,128)(2,1)S(1)}, u32[]{:S(2)}, u32[]{:S(2)}) collective-permute-start(bf16[3,24,512]{2,1,0:T(8,128)(2,1)S(1)} %get-tuple-element.88), channel_id=1, source_target_pairs={{255,0},{252,1},{253,2},{254,3},{3,4},{0,5},{1,6},{2,7},{7,8},{4,9... | collective-permute-start | bytes 221192 | tf_op jit(solution)/shard_map/ppermute | solution.py:515
  83.4 9.8 %collective-permute-start.12 = (bf16[3,24,512]{2,1,0:T(8,128)(2,1)S(1)}, bf16[3,24,512]{2,1,0:T(8,128)(2,1)S(1)}, u32[]{:S(2)}, u32[]{:S(2)}) collective-permute-start(bf16[3,24,512]{2,1,0:T(8,128)(2,1)S(1)} %get-tuple-element.90), channel_id=1, source_target_pairs={{252,0},{0,4},{4,8},{8,12},{12,16},{16,20},{20,24},{24,28},{28,32}... | collective-permute-start | bytes 221192 | tf_op jit(solution)/shard_map/ppermute | solution.py:425
  84.6 13.9 %collective-permute-start.11 = (bf16[3,24,512]{2,1,0:T(8,128)(2,1)S(1)}, bf16[3,24,512]{2,1,0:T(8,128)(2,1)S(1)}, u32[]{:S(2)}, u32[]{:S(2)}) collective-permute-start(bf16[3,24,512]{2,1,0:T(8,128)(2,1)S(1)} %get-tuple-element.91), channel_id=1, source_target_pairs={{3,0},{0,1},{1,2},{2,3},{7,4},{4,5},{5,6},{6,7},{11,8},{8,9},{9,10... | collective-permute-start | bytes 221192 | tf_op jit(solution)/shard_map/ppermute | solution.py:425
  101.3 1.0 copy-start.1
  104.7 26.0 %all-to-all-start.2 = ((bf16[16,176,128]{2,1,0:T(8,128)(2,1)}), bf16[16,176,128]{2,1,0:T(8,128)(2,1)S(1)}, u32[]{:S(2)}, u32[]{:S(2)}) async-start(bf16[16,176,128]{2,1,0:T(8,128)(2,1)} %shard_map.321), calls=%async_computation.2 | async-start | bytes 1441792 | tf_op jit(solution)/shard_map/all_to_all | solution.py:519
  130.7 0.9 copy-start.2
  (1 other events, 0.6 us)

commit v2 on v1

--- a/solution.py
+++ b/solution.py
@@ -51,7 +51,8 @@
                         west[t, (i * HALF_LON + j - COLS) * LEV + lev] = 1
                     else:
                         own[t, (i * COLS + j) * LEV + lev] = 1
-                    back[(r * COLS + c) * LEV + lev, t] = 1
+                    part = (r >= 3) * 1 + (c >= 6) * 2
+                    back[part * 72 + ((r % 3) * 6 + c % 6) * LEV + lev, t] = 1
                     dj, pc = c % 2, c // 2
                     if r % 2:
                         di, pr = 0, (r + 1) // 2
@@ -66,8 +67,8 @@
                 dj, pc = c % 2, c // 2
                 quad_prev[(dj * 2 + 0) * 96 + 0 * 24 + s * 6 + pc, s * 12 + c] = 1
                 quad_next[(dj * 2 + 1) * 96 + 3 * 24 + s * 6 + pc, s * 12 + c] = 1
-    cot_own = np.zeros((96, 72)); cot_west = np.zeros((96, 24)); cot_south = np.zeros((96, 24)); cot_corner = np.zeros((96, 24))
-    coarse = np.zeros((72, 96))
+    cot_own = np.zeros((3, 96, 24)); cot_west = np.zeros((2, 96, 12)); cot_south = np.zeros((2, 96, 12)); cot_corner = np.zeros((2, 96, 12))
+    coarse = np.zeros((96, 96))
     for pr in range(4):
         for s in range(LEV):
             lev = (s + 1) % LEV
@@ -75,15 +76,16 @@
                 p = pr * 24 + s * 6 + pc
                 i, j = pr + 1, pc + 3
                 if i >= 3 and j >= 6:
-                    cot_corner[p, ((i - 3) * 3 + j - 6) * LEV + lev] = 1
+                    cot_corner[i - 3, p, (j - 6) * LEV + lev] = 1
                 elif i >= 3:
-                    cot_south[p, ((i - 3) * 3 + pc) * LEV + lev] = 1
+                    cot_south[i - 3, p, pc * LEV + lev] = 1
                 elif j >= 6:
-                    cot_west[p, ((i - 1) * 3 + j - 6) * LEV + lev] = 1
+                    cot_west[i - 1, p, (j - 6) * LEV + lev] = 1
                 else:
-                    cot_own[p, (i * 6 + j) * LEV + lev] = 1
+                    cot_own[i, p, j * LEV + lev] = 1
                 if pr < 3:
-                    coarse[(pr * 6 + pc) * LEV + lev, p] = 1
+                    start = (0 if pc < 3 else 32) if pr < 2 else (64 if pc < 3 else 80)
+                    coarse[start + ((pr % 2) * 3 + pc % 3) * LEV + lev, p] = 1
     place = np.zeros(WIN, np.int64)
     for l in range(2):
         for r in range(ROWS):
@@ -133,7 +135,7 @@
 
 
 def bias_kernel(last_ref, table_ref, spread_ref, level_ref, north_ref, bias_ref, mask_ref, rows_ref, left_ref, right_ref):
-    table = table_ref[...]
+    table = jnp.concatenate([table_ref[...], jnp.zeros((8, 768 - TABLE), F32)], axis=1)
     for q in range(WIN):
         rows_ref[8 * q : 8 * q + 8, :] = pltpu.roll(table, (768 - PLACE[q]) % 768, 1)[:, :SPAN]
     rows = rows_ref[...]
@@ -163,7 +165,7 @@
         scratch_shapes=[pltpu.VMEM((8 * WIN, SPAN), F32)] + [pltpu.VMEM((8 * WIN, 128), F32)] * 2,
         compiler_params=PARAMS,
         cost_estimate=cost(2_000_000_000, 4_000_000),
-    )(last, jnp.pad(table, ((0, 0), (0, 768 - TABLE))), plan("spread"), plan("apart_level"), plan("apart_north"))
+    )(last, table, plan("spread"), plan("apart_level"), plan("apart_north"))
 
 
 def norm_parts(values, width):
@@ -187,7 +189,7 @@
 
 def attend_kernel(
     own_ref, west_ref, south_ref, corner_ref, plan_own, plan_west, plan_south, plan_corner, plan_edge, gain_ref, wqkv_ref, wproj_ref,
-    bias_ref, mask_ref, x_ref, qkv_ref, p_ref, mixed_ref, block_ref, first_ref, last_ref,
+    bias_ref, mask_ref, x_ref, qkv_ref, p_ref, tokens_ref, block_ref, first_ref, last_ref,
 ):
     x = (
         mm(plan_own[...], own_ref[...]) + mm(plan_west[...], west_ref[...])
@@ -196,6 +198,7 @@
     x_ref[...] = x.astype(BF)
     (hat,), _ = norm_parts([x], 512)
     normed = (hat * gain_ref[...]).astype(BF)
+    tokens_ref[:, :512] = normed
     qkv_ref[...] = mm(normed, wqkv_ref[...]).astype(BF)
     lower = lower_half()
     for w in range(2):
@@ -216,8 +219,8 @@
                 weights = (grown / jnp.sum(grown, axis=1, keepdims=True)).astype(BF)
                 p_ref[w * HEADS + h] = weights
                 outs.append(mm(weights, value))
-            mixed_ref[rows, lanes] = jnp.where(lower, outs[0], outs[1]).astype(BF)
-    attended = mm(mixed_ref[...], wproj_ref[...]).astype(BF)
+            tokens_ref[rows, 512 + pair * 128 : 640 + pair * 128] = jnp.where(lower, outs[0], outs[1]).astype(BF)
+    attended = mm(tokens_ref[:, 512:], wproj_ref[...]).astype(BF)
     block = (x + attended.astype(F32)).astype(BF)
     block_ref[...] = block
     edge = mm(plan_edge[...], block).astype(BF)
@@ -226,7 +229,7 @@
 
 
 def attend(own, west, south, corner, gain, wqkv, wproj, bias, mask):
-    shapes = [(TOK, 512), (TOK, 1536), (2 * HEADS, WIN, WIN), (TOK, 512), (TOK, 512), (48, 512), (48, 512)]
+    shapes = [(TOK, 512), (TOK, 1536), (2 * HEADS, WIN, WIN), (TOK, 1024), (TOK, 512), (48, 512), (48, 512)]
     return pl.pallas_call(
         attend_kernel,
         out_shape=[jax.ShapeDtypeStruct(s, BF) for s in shapes],
@@ -249,10 +252,11 @@
     for k in range(4):
         hats_ref[k] = hats[k]
         normed.append((hats[k] * gain_ref[:, 512 * k : 512 * k + 512]).astype(BF))
-    cot = (
-        mm(plan_cot[...], cot_ref[...]) + mm(plan_cot_west[...], cot_west_ref[...])
-        + mm(plan_cot_south[...], cot_south_ref[...]) + mm(plan_cot_corner[...], cot_corner_ref[...])
-    )
+    cot = sum(mm(plan_cot[i], cot_ref[i]) for i in range(1, 3))
+    for some_plan, some_ref in (
+        (plan_cot_west, cot_west_ref), (plan_cot_south, cot_south_ref), (plan_cot_corner, cot_corner_ref),
+    ):
+        cot = cot + mm(some_plan[0], some_ref[0]) + mm(some_plan[1], some_ref[1])
     all_cot_ref[...] = cot.astype(BF)
     counted = lax.broadcasted_iota(jnp.int32, (80, 1024), 0) < 72
     cot_own = jnp.where(counted, cot[:80], 0.0).astype(BF)
@@ -302,7 +306,7 @@
 
 def merge(hats, scale, all_cot, gain, wmerge):
     shapes = [
-        jax.ShapeDtypeStruct((72, 1024), BF), jax.ShapeDtypeStruct((TOK, 512), BF),
+        jax.ShapeDtypeStruct((96, 1024), BF), jax.ShapeDtypeStruct((TOK, 512), BF),
         jax.ShapeDtypeStruct((16, 128), F32),
     ]
     return pl.pallas_call(
@@ -316,70 +320,86 @@
 
 
 def back_kernel(
-    core_ref, cot_ref, x_ref, qkv_ref, p_ref, mixed_ref, wqkv_ref, wproj_ref, gain_ref, merge_gain_ref, spread_t, back_plan,
-    grad_ref, small_ref, mine_ref, theirs_ref, dqkv_ref, left_ref, right_ref, wide_ref,
+    core_ref, cot_ref, x_ref, qkv_ref, p_ref, wqkv_ref, wproj_ref, gain_ref, merged_ref, back_plan,
+    stay_ref, north_ref, east_ref, corner_ref, gain_grad_ref, mine_ref, theirs_ref, left_ref, right_ref, dqkv_ref,
 ):
     cot = cot_ref[...]
     mixed_cot = mm_nt(cot, wproj_ref[...]).astype(BF)
     lower = lower_half()
-    for w in range(2):
-        rows = slice(w * WIN, (w + 1) * WIN)
-        for pair in range(4):
-            lanes = slice(pair * 128, pair * 128 + 128)
+    for pair in range(4):
+        lanes = slice(pair * 128, pair * 128 + 128)
+        score_cots = [0.0, 0.0]
+        for w in range(2):
+            rows = slice(w * WIN, (w + 1) * WIN)
             query = qkv_ref[rows, lanes]
             key = qkv_ref[rows, 512 + pair * 128 : 640 + pair * 128]
             value = qkv_ref[rows, 1024 + pair * 128 : 1152 + pair * 128]
             out_cot = mixed_cot[rows, lanes]
             found = []
             for half in range(2):
-                h = 2 * pair + half
                 keep = lower if half == 0 else jnp.logical_not(lower)
                 part = jnp.where(keep, out_cot, 0.0).astype(BF)
-                weights = p_ref[w * HEADS + h]
+                weights = p_ref[w * HEADS + 2 * pair + half]
                 weight_cot = mm_nt(part, value).astype(BF).astype(F32)
                 wide = weights.astype(F32)
                 product = wide * weight_cot
                 score_cot = product - wide * jnp.sum(product, axis=1, keepdims=True)
-                places = pl.ds(h, WIN, stride=8)
-                right = jnp.concatenate([score_cot[:, 128:], jnp.zeros((WIN, 112), F32)], axis=1)
-                if w == 0:
-                    left_ref[places, :] = score_cot[:, :128]
-                    right_ref[places, :] = right
-                else:
-                    left_ref[places, :] = left_ref[places, :] + score_cot[:, :128]
-                    right_ref[places, :] = right_ref[places, :] + right
+                score_cots[half] = score_cots[half] + score_cot
                 scaled = (score_cot * 0.125).astype(BF)
                 found.append((mm(scaled, key), mm_tn(scaled, query), mm_tn(weights, out_cot)))
             for n in range(3):
                 both = jnp.where(lower, found[0][n], found[1][n]).astype(BF)
                 dqkv_ref[rows, 512 * n + pair * 128 : 512 * n + pair * 128 + 128] = both
+        for half in range(2):
+            places = pl.ds(2 * pair + half, WIN, stride=8)
+            left_ref[places, :] = score_cots[half][:, :128]
+            right_ref[places, :] = jnp.concatenate([score_cots[half][:, 128:], jnp.zeros((WIN, 112), F32)], axis=1)
     dqkv = dqkv_ref[...]
     x = x_ref[...].astype(F32)
     (hat,), scale = norm_parts([x], 512)
     gain = gain_ref[...]
-    normed = (hat * gain).astype(BF)
     normed_cot = mm_nt(dqkv, wqkv_ref[...]).astype(BF).astype(F32)
     gain_grad = jnp.sum(normed_cot * hat, axis=0, keepdims=True)
+    for i in range(4):
+        gain_grad_ref[i : i + 1, :] = gain_grad[:, 128 * i : 128 * i + 128]
+    (pulled,) = norm_back([hat], scale, [normed_cot], [gain], 512)
+    total = (cot.astype(F32) + pulled.astype(BF).astype(F32)).astype(BF)
+    home = mm(back_plan[...], total)
+    stay_ref[...] = home[:72].astype(BF)
+    for out_ref, start, rows, part in ((east_ref, 32, 32, 2), (north_ref, 64, 16, 1), (corner_ref, 80, 16, 3)):
+        out_ref[:rows, :] = merged_ref[start : start + rows, :512]
+        out_ref[rows : 2 * rows, :] = merged_ref[start : start + rows, 512:]
+        out_ref[2 * rows :, :] = home[72 * part : 72 * part + 72].astype(BF)
+    core = core_ref[0]
+    for out_ref, owner in ((theirs_ref, 1 - core), (mine_ref, core)):
+        for yh in range(2):
+            first = pl.multiple_of(768 * yh + 384 * owner, 128)
+            out_ref[:, 384 * yh : 384 * yh + 384] = dqkv_ref[:, pl.ds(first, 384)]
+            first = pl.multiple_of(256 * yh + 128 * owner, 128)
+            out_ref[:, 768 + 128 * yh : 896 + 128 * yh] = cot_ref[:, pl.ds(first, 128)]
+
+
+def attend_back(core, cot, x, qkv, p, wqkv, wproj, gain, merged):
+    shapes = [
+        jax.ShapeDtypeStruct((72, 512), BF), jax.ShapeDtypeStruct((104, 512), BF),
+        jax.ShapeDtypeStruct((136, 512), BF), jax.ShapeDtypeStruct((104, 512), BF),
+        jax.ShapeDtypeStruct((4, 128), F32),
+    ] + [jax.ShapeDtypeStruct((TOK, 1024), BF)] * 2 + [jax.ShapeDtypeStruct((8 * WIN, 128), F32)] * 2
+    return pl.pallas_call(
+        back_kernel,
+        out_shape=shapes,
+        in_specs=[pl.BlockSpec(memory_space=pltpu.SMEM)] + vmem(9),
+        out_specs=vmem(9),
+        scratch_shapes=[pltpu.VMEM((TOK, 1536), BF)],
+        compiler_params=PARAMS,
+        cost_estimate=cost(6_000_000_000, 16_000_000),
+    )(core, cot, x, qkv, p, wqkv, wproj, gain, merged, plan("back"))
+
+
+def small_kernel(left_ref, right_ref, spread_t, merge_gain_ref, norm_gain_ref, small_ref, wide_ref):
     small_ref[48:64, :] = merge_gain_ref[...]
     small_ref[64:80, :] = jnp.zeros((16, 128), F32)
-    for i in range(4):
-        small_ref[64 + i : 65 + i, :] = gain_grad[:, 128 * i : 128 * i + 128]
-    (pulled,) = norm_back([hat], scale, [normed_cot], [gain], 512)
-    total = (cot.astype(F32) + pulled.astype(BF).astype(F32)).astype(BF)
-    grad_ref[...] = mm(back_plan[...], total).astype(BF)
-    mixed = mixed_ref[...]
-    core = core_ref[0]
-    for yh in range(2):
-        for out_ref, owner in ((theirs_ref, 1 - core), (mine_ref, core)):
-            first = pl.multiple_of(768 * yh + 384 * owner, 128)
-            grad = mm_tn(normed, dqkv_ref[:, pl.ds(first, 384)])
-            proj = mm_tn(mixed, cot_ref[:, pl.ds(pl.multiple_of(256 * yh + 128 * owner, 128), 128)])
-            tiles = [grad[:, 128 * t : 128 * t + 128] for t in range(3)] + [proj]
-            for xy in range(8):
-                chunk = [v[64 * xy : 64 * xy + 64].reshape(8, 8, 128) for v in tiles]
-                for t in range(2):
-                    piece = jnp.concatenate([chunk[2 * t], chunk[2 * t + 1]], axis=1).astype(BF)
-                    out_ref[xy, :, yh, 16 * t : 16 * t + 16, :] = piece
+    small_ref[64:68, :] = norm_gain_ref[...]
     wide_ref[...] = mm(left_ref[...].astype(BF), spread_t[:128, :]) + mm(right_ref[...].astype(BF), spread_t[128:, :])
     blank = jnp.zeros((8, 512 - SPAN), F32)
     levels = []
@@ -398,19 +418,48 @@
         small_ref[8 * i : 8 * i + 8, :] = bias_grad[:, 128 * i : 128 * i + 128]
 
 
-def attend_back(core, cot, x, qkv, p, mixed, wqkv, wproj, gain, merge_gain):
-    shapes = [
-        jax.ShapeDtypeStruct((TOK, 512), BF), jax.ShapeDtypeStruct((80, 128), F32),
-    ] + [jax.ShapeDtypeStruct((8, 8, 2, 32, 128), BF)] * 2
-    return pl.pallas_call(
-        back_kernel,
-        out_shape=shapes,
-        in_specs=[pl.BlockSpec(memory_space=pltpu.SMEM)] + vmem(11),
-        out_specs=vmem(4),
-        scratch_shapes=[pltpu.VMEM((TOK, 1536), BF), pltpu.VMEM((8 * WIN, 128), F32), pltpu.VMEM((8 * WIN, 128), F32), pltpu.VMEM((8 * WIN, SPAN), F32)],
-        compiler_params=PARAMS,
-        cost_estimate=cost(8_000_000_000, 16_000_000),
-    )(core, cot, x, qkv, p, mixed, wqkv, wproj, gain, merge_gain, plan("spread_t"), plan("back"))
+def small_grads(left, right, merge_gain, norm_gain):
+    return pl.pallas_call(
+        small_kernel,
+        out_shape=jax.ShapeDtypeStruct((80, 128), F32),
+        in_specs=vmem(5),
+        out_specs=vmem(1)[0],
+        scratch_shapes=[pltpu.VMEM((8 * WIN, SPAN), F32)],
+        compiler_params=PARAMS,
+        cost_estimate=cost(2_000_000_000, 4_000_000),
+    )(left, right, plan("spread_t"), merge_gain, norm_gain)
+
+
+def late_kernel(rows_ref, rows_theirs_ref, columns_ref, columns_theirs_ref, small_ref, small_theirs_ref, out_ref):
+    normed = jnp.concatenate([rows_ref[:, :512], rows_theirs_ref[:, :512]], axis=0)
+    mixed = jnp.concatenate([rows_ref[:, 512:], rows_theirs_ref[:, 512:]], axis=0)
+    columns = jnp.concatenate([columns_ref[...], columns_theirs_ref[...]], axis=0)
+    grad = mm_tn(normed, columns[:, :768])
+    proj = mm_tn(mixed, columns[:, 768:])
+    for yh in range(2):
+        tiles = [grad[:, 384 * yh + 128 * t : 384 * yh + 128 * t + 128] for t in range(3)]
+        tiles.append(proj[:, 128 * yh : 128 * yh + 128])
+        for xy in range(8):
+            chunk = [v[64 * xy : 64 * xy + 64].reshape(8, 8, 128) for v in tiles]
+            for t in range(2):
+                piece = jnp.concatenate([chunk[2 * t], chunk[2 * t + 1]], axis=1).astype(BF)
+                for z in range(8):
+                    start = 64 * z + 32 * yh + 16 * t
+                    out_ref[xy, start : start + 16, :] = piece[z]
+    small = (small_ref[...] + small_theirs_ref[...]).astype(BF)
+    for xy in range(8):
+        out_ref[xy, 512:, :] = small
+
+
+def late_grads(rows, rows_theirs, columns, columns_theirs, small, small_theirs):
+    return pl.pallas_call(
+        late_kernel,
+        out_shape=jax.ShapeDtypeStruct((8, 592, 128), BF),
+        in_specs=vmem(6),
+        out_specs=vmem(1)[0],
+        compiler_params=PARAMS,
+        cost_estimate=cost(2_000_000_000, 4_000_000),
+    )(rows, rows_theirs, columns, columns_theirs, small, small_theirs)
 
 
 def total_of(axes):
@@ -423,23 +472,6 @@
 def moved(block, axes, distance):
     count = total_of(axes)
     return lax.ppermute(block, axes, [((i - distance) % count, i) for i in range(count)])
-
-
-def pack_kernel(mine_ref, theirs_ref, small_ref, small_theirs_ref, out_ref):
-    out_ref[:, :512, :] = (mine_ref[...].astype(F32) + theirs_ref[...].astype(F32)).astype(BF)
-    small = (small_ref[...] + small_theirs_ref[...]).astype(BF)
-    for i in range(8):
-        out_ref[i, 512:, :] = small
-
-
-def pack(mine, theirs, small, small_theirs):
-    return pl.pallas_call(
-        pack_kernel,
-        out_shape=jax.ShapeDtypeStruct((8, 592, 128), BF),
-        in_specs=vmem(4),
-        out_specs=vmem(1)[0],
-        compiler_params=PARAMS,
-    )(mine, theirs, small, small_theirs)
 
 
 def pair_kernel(early_ref, out_ref):
@@ -491,11 +523,11 @@
         width = min(128, TABLE - 128 * t)
         bias_ref[:, 128 * t : 128 * t + width] = total[96 + 8 * t : 104 + 8 * t, :width]
     merge_gain_ref[...] = total[144:160]
-    norm_gain_ref[...] = total[160:168]
+    norm_gain_ref[...] = total[160:164]
 
 
 def unpack(got):
-    shapes = [(8, 384), (8, 128), (32, 256), (8, 128), (16, 128), (8, TABLE)]
+    shapes = [(8, 384), (8, 128), (32, 256), (4, 128), (16, 128), (8, TABLE)]
     return pl.pallas_call(
         unpack_kernel,
         out_shape=[jax.ShapeDtypeStruct(s, F32) for s in shapes],
@@ -519,57 +551,64 @@
     return lax.all_to_all(parts, axes, 0, 0, tiled=True)
 
 
-def home(field, rows, width):
-    north = moved(field[rows:, :width], LAT, 1)
-    east = moved(field[:rows, width:], LON, 1)
-    corner = diagonal(field[rows:, width:], 1)
+def quarters(corner, north, east, stay):
     top = jnp.concatenate([corner, north], axis=1)
-    return jnp.concatenate([top, jnp.concatenate([east, field[:rows, :width]], axis=1)], axis=0)
+    return jnp.concatenate([top, jnp.concatenate([east, stay], axis=1)], axis=0)
 
 
 def on_device(features, norm_gain, qkv_weight, proj_weight, bias_table, merge_gain, merge_weight, merged_cot):
     last = (lax.axis_index(LAT) == total_of(LAT) - 1).astype(jnp.int32).reshape(1)
     gain, wide_gain = norm_gain.reshape(1, 512), merge_gain.reshape(1, 2048)
     own = features.transpose(1, 2, 0, 3).reshape(6, 48, 512)
+    own, merged_cot = lax.optimization_barrier((own, merged_cot))
     cot = merged_cot.transpose(1, 2, 0, 3).reshape(3, 24, 1024)
     west = moved(own[:, :24], LON, -1)
     south = moved(own[:3, 24:], LAT, -1)
     corner = diagonal(own[:3, :24], -1)
+    cot_west = moved(cot[1:, :12], LON, -1)
+    cot_south = moved(cot[:2, 12:], LAT, -1)
+    cot_corner = diagonal(cot[:2, :12], -1)
     bias, mask = bias_of(bias_table, last)
     flat = own.reshape(TOK, 512)
     flat, bias, mask, west, south, corner = lax.optimization_barrier((flat, bias, mask, west, south, corner))
-    x, qkv, p, mixed, block, first, final = attend(
+    x, qkv, p, rows, block, first, final = attend(
         flat, west.reshape(144, 512), south.reshape(72, 512), corner.reshape(72, 512),
         gain, qkv_weight, proj_weight, bias, mask,
     )
     following = moved(first, LAT, -1)
     prev = moved(final, LAT, 1)
-    cot, block = lax.optimization_barrier((cot, block))
-    cot_west = moved(cot[1:, :12], LON, -1)
-    cot_south = moved(cot[:2, 12:], LAT, -1)
-    cot_corner = diagonal(cot[:2, :12], -1)
     core = lax.axis_index("c").astype(jnp.int32).reshape(1)
-    pair, hats, scale, all_cot = stack(
-        block, prev, following, cot.reshape(72, 1024), cot_west.reshape(24, 1024), cot_south.reshape(24, 1024),
-        cot_corner.reshape(24, 1024), wide_gain,
-    )
+    pair, hats, scale, all_cot = stack(block, prev, following, cot, cot_west, cot_south, cot_corner, wide_gain)
     early = spread_over(pair, CLOSE)
     merged, attn_cot, merge_gain_part = merge(hats, scale, all_cot, wide_gain, merge_weight)
-    merged = home(merged.reshape(3, 24, 1024), 2, 12)
-    grad, small, late, late_out = attend_back(
-        core, attn_cot, x, qkv, p, mixed, qkv_weight, proj_weight, gain, merge_gain_part
+    rows_theirs = swapped(rows, "c", 1)
+    stay, north, east, corner, norm_gain_part, columns, columns_out, left, right = attend_back(
+        core, attn_cot, x, qkv, p, qkv_weight, proj_weight, gain, merged
     )
-
-    late_theirs, small_theirs = swapped(late_out, "c", 1), swapped(small, "c", 1)
-    late = pack(late.reshape(8, 512, 128), late_theirs.reshape(8, 512, 128), small, small_theirs)
+    columns_theirs = swapped(columns_out, "c", 1)
+    small = small_grads(left, right, merge_gain_part, norm_gain_part)
+    columns_theirs, small = lax.optimization_barrier((columns_theirs, small))
+    late = late_grads(rows, rows_theirs, columns, columns_theirs, small, swapped(small, "c", 1))
     late, early = lax.optimization_barrier((late, early))
     late = spread_over(late, NEAR)
-    early = pair_grad(early)
-    grad = home(grad.reshape(6, 48, 512), 3, 24)
-    late, early, grad, merged = lax.optimization_barrier((late, early, grad, merged))
-    merged = merged.reshape(3, 6, 4, 1024).transpose(2, 0, 1, 3)
+    north, east, corner = moved(north, LAT, 1), moved(east, LON, 1), diagonal(corner, 1)
+    north, early = lax.optimization_barrier((north, pair_grad(early)))
+    late, early, north, east, corner = lax.optimization_barrier((late, early, north, east, corner))
+    got = spread_over(fold(early, late), FAR)
+    grad = quarters(
+        corner[32:].reshape(3, 24, 512), north[32:].reshape(3, 24, 512), east[64:].reshape(3, 24, 512),
+        stay.reshape(3, 24, 512),
+    )
+
+    def wide(left, right, rows):
+        return jnp.concatenate([left, right], axis=1).reshape(rows, 12, 1024)
+
+    coarse = quarters(
+        wide(corner[:12], corner[16:28], 1), wide(north[:12], north[16:28], 1),
+        wide(east[:24], east[32:56], 2), merged[:24].reshape(2, 12, 1024),
+    )
+    merged = coarse.reshape(3, 6, 4, 1024).transpose(2, 0, 1, 3)
     features_grad = grad.reshape(6, 12, 4, 512).transpose(2, 0, 1, 3)
-    got = spread_over(fold(early, late), FAR)
     qkv_grad, proj_grad, merge_grad, norm_gain_grad, merge_gain_grad, bias_grad = unpack(got)
     return (
         merged,
@@ -577,7 +616,7 @@
         qkv_grad,
         proj_grad,
         merge_grad,
-        norm_gain_grad[:4].reshape(-1),
+        norm_gain_grad.reshape(-1),
         merge_gain_grad.reshape(-1),
         bias_grad,
     )

time: 136 us -> 131 us (0.963)
  local copies, waits for them, and re-layouts: 14 us -> 8.25 us
  starting transfers between devices: 39.7 us -> 36.3 us
  waiting for transfers between devices: 36.9 us -> 39.4 us
  Pallas kernels: 43.2 us -> 45 us
    pallas_call x1 -> x2, Pallas kernels: 2.84 us -> 7.36 us  [the longest x1 3.71 us: small_grads(): pl.pallas_call(small_kernel, out_shape=jax.ShapeDtypeStruct((80, 128), F3...]
    ppermute x10 -> x8, waiting for transfers between devices: 11.5 us -> 15.1 us  [moved(): lax.ppermute(block, axes, [((i - distance) % count, i) for i in range(cou...]
    reshape x5 -> x3, local copies, waits for them, and re-layouts: 3.88 us -> 0.76 us  [the longest x1 0.72 us: on_device(): merged = coarse.reshape(3, 6, 4, 1024).transpose(2, 0, 1, 3)]
    pallas_call x1, Pallas kernels: 13.5 us -> 10.7 us  [attend_back(): pl.pallas_call(back_kernel, out_shape=shapes, in_specs=[pl.BlockSpec(memo...]
    all_to_all x3, waiting for transfers between devices: 20.7 us -> 23 us  [spread_over(): return lax.all_to_all(parts, axes, 0, 0, tiled=True)]
    ppermute x4 -> x3, waiting for transfers between devices: 2.27 us -> 0.01 us  [diagonal(): return lax.ppermute(block, AXES, route)]
    ppermute x10 -> x8, starting transfers between devices: 12.1 us -> 10.6 us  [moved(): lax.ppermute(block, axes, [((i - distance) % count, i) for i in range(cou...]
    ppermute x4 -> x3, starting transfers between devices: 8.09 us -> 6.93 us  [diagonal(): return lax.ppermute(block, AXES, route)]
  transfers between devices with their start and end apart: 19 -> 17, of which waited for: 9 -> 6; matrix products, arithmetic and copies ran while one was open for 6% -> 3% of each run, Pallas kernels for 21% -> 28%
where the time goes in v2:
time: 131 us; the launch traced here: 130 us
  Pallas kernels  45 us (34%)
  waiting for transfers between devices  39.4 us (30%)
  starting transfers between devices  36.3 us (28%)
  local copies, waits for them, and re-layouts  8.25 us (6%)
    all_to_all x3, waiting for transfers between devices, spread_over(): return lax.all_to_all(parts, axes, 0, 0, tiled=True)  23 us
    all_to_all x3, starting transfers between devices, spread_over(): return lax.all_to_all(parts, axes, 0, 0, tiled=True)  18 us
    ppermute x8, waiting for transfers between devices, moved(): lax.ppermute(block, axes, [((i - distance) % count, i) for i in range(cou...  15.1 us
    pallas_call x1, Pallas kernels, attend_back(): pl.pallas_call(back_kernel, out_shape=shapes, in_specs=[pl.BlockSpec(memo...  10.7 us
    ppermute x8, starting transfers between devices, moved(): lax.ppermute(block, axes, [((i - distance) % count, i) for i in range(cou...  10.6 us
    ppermute x3, starting transfers between devices, diagonal(): return lax.ppermute(block, AXES, route)  6.93 us
    pallas_call x1, Pallas kernels, attend(): pl.pallas_call(attend_kernel, out_shape=[jax.ShapeDtypeStruct(s, BF) for...  6.43 us
    pallas_call x1, Pallas kernels, merge(): pl.pallas_call(merge_kernel, out_shape=shapes, in_specs=vmem(7), out_spec...  6.11 us
  transfers between devices with their start and end apart: 17, of which 6 were waited for; matrix products, arithmetic and copies ran while one was open for 3% of the time, Pallas kernels for 28%

profile of v2, /device:TPU:8, one launch (start us, length us, event | category | flops | bytes accessed | tf_op | source)
XLA Modules:
  0.0 129.9 jit_solution(6999223599501106346)
XLA Ops:
  0.6 1.0 reshape.84
  1.7 1.8 %collective-permute-start.1 = (bf16[3,24,512]{2,1,0:T(8,128)(2,1)S(1)}, bf16[3,24,512]{2,1,0:T(8,128)(2,1)S(1)}, u32[]{:S(2)}, u32[]{:S(2)}) collective-permute-start(bf16[3,24,512]{2,1,0:T(8,128)(2,1)S(1)} %get-tuple-element.109), channel_id=1, source_target_pairs={{1,0},{2,1},{3,2},{0,3},{5,4},{6,5},{7,6},{4,7},{9,8},{10,9},{11,1... | collective-permute-start | bytes 221192 | tf_op jit(solution)/shard_map/ppermute | solution.py:474
  3.5 5.2 %collective-permute-start.2 = (bf16[3,24,512]{2,1,0:T(8,128)(2,1)S(1)}, bf16[3,24,512]{2,1,0:T(8,128)(2,1)S(1)}, u32[]{:S(2)}, u32[]{:S(2)}) collective-permute-start(bf16[3,24,512]{2,1,0:T(8,128)(2,1)S(1)} %get-tuple-element.108), channel_id=1, source_target_pairs={{5,0},{6,1},{7,2},{4,3},{9,4},{10,5},{11,6},{8,7},{13,8},{14,9},{1... | collective-permute-start | bytes 221192 | tf_op jit(solution)/shard_map/ppermute | solution.py:547
  8.8 2.6 %collective-permute-start = (bf16[6,24,512]{2,1,0:T(8,128)(2,1)S(1)}, bf16[6,24,512]{2,1,0:T(8,128)(2,1)S(1)}, u32[]{:S(2)}, u32[]{:S(2)}) collective-permute-start(bf16[6,24,512]{2,1,0:T(8,128)(2,1)S(1)} %slice.48), channel_id=1, source_target_pairs={{4,0},{8,4},{12,8},{16,12},{20,16},{24,20},{28,24},{32,28},{36,32}... | collective-permute-start | bytes 442376 | tf_op jit(solution)/shard_map/ppermute | solution.py:474
  11.4 0.9 reshape.93.cot_ref
  12.4 1.1 collective-permute-start.6
  13.4 3.6 %shard_map.314 = (f32[8,144,144]{2,1,0:T(8,128)}, f32[2,144,144]{2,1,0:T(8,128)}) custom-call(s32[1]{0:T(128)} %bitcast.2.last_ref, f32[8,759]{1,0:T(8,128)} %table_ref.1, bf16[384,256]{1,0:T(8,128)(2,1)} %constant.48.clone.spread_ref, bf16[144,144]{1,0:T(8,128)(2,1)} %constant.49.clone.level_ref, bf16[144,144]{1,0:T(8,128)(2,1)} %constant.50.clone.north_ref), custom_call_target="tpu_custom_call" | custom-call | flops 2000000000 | bytes 4000000 | tf_op jit(solution)/shard_map/pallas_call | solution.py:160
  17.9 6.4 %shard_map.315 = (bf16[288,512]{1,0:T(8,128)(2,1)}, bf16[288,1536]{1,0:T(8,128)(2,1)}, bf16[16,144,144]{2,1,0:T(8,128)(2,1)}, bf16[288,1024]{1,0:T(8,128)(2,1)},...) custom-call(bf16[288,512]{1,0:T(8,128)(2,1)} %bitcast.22, bf16[144,512]{1,0:T(8,128)(2,1)} %bitcast.31, ...), custom_call_target="tpu_custom_call" | custom-call | flops 4000000000 | bytes 8000000 | tf_op jit(solution)/shard_map/pallas_call | solution.py:233
  24.3 1.1 collective-permute-start.4
  25.4 2.2 %collective-permute-start.5 = (bf16[48,512]{1,0:T(8,128)(2,1)}, bf16[48,512]{1,0:T(8,128)(2,1)S(1)}, u32[]{:S(2)}, u32[]{:S(2)}) collective-permute-start(bf16[48,512]{1,0:T(8,128)(2,1)} %get-tuple-element.70), channel_id=1, source_target_pairs={{1,0},{2,1},{3,2},{0,3},{5,4},{6,5},{7,6},{4,7},{9,8},{10,9},{11,1... | collective-permute-start | bytes 147464 | tf_op jit(solution)/shard_map/ppermute | solution.py:474
  27.6 1.9 %collective-permute-done.4.prev_ref = bf16[48,512]{1,0:T(8,128)(2,1)S(1)} collective-permute-done((bf16[48,512]{1,0:T(8,128)(2,1)}, bf16[48,512]{1,0:T(8,128)(2,1)S(1)}, u32[]{:S(2)}, u32[]{:S(2)}) %collective-permute-start.4) | collective-permute-done | bytes 49184 | tf_op jit(solution)/shard_map/ppermute | solution.py:474
  30.3 3.8 %shard_map.316 = (bf16[16,80,768]{2,1,0:T(8,128)(2,1)}, f32[4,96,512]{2,1,0:T(8,128)}, f32[96,128]{1,0:T(8,128)}, bf16[96,1024]{1,0:T(8,128)(2,1)}) custom-call(bf16[288,512]{1,0:T(8,128)(2,1)} %get-tuple-element.68.block_ref, bf16[48,512]{1,0:T(8,128)(2,1)} %copy-done.15, bf16[48,512]{1,0:T(8,128)(2,1)} %copy-done.16, bf16[3,24,1024]{2,1,0:T(8,128)(2,1)} %copy-done.4, ...), custom_call_target="tpu_custom_call" | custom-call | flops 2000000000 | bytes 8000000 | tf_op jit(solution)/shard_map/pallas_call | solution.py:278
  34.1 8.6 %all-to-all-start = ((bf16[16,80,768]{2,1,0:T(8,128)(2,1)}), bf16[16,80,768]{2,1,0:T(8,128)(2,1)S(1)}, u32[]{:S(2)}, u32[]{:S(2)}) async-start(bf16[16,80,768]{2,1,0:T(8,128)(2,1)} %get-tuple-element.88), calls=%async_computation | async-start | bytes 3932160 | tf_op jit(solution)/shard_map/all_to_all | solution.py:551
  42.7 6.1 %shard_map.317 = (bf16[96,1024]{1,0:T(8,128)(2,1)}, bf16[288,512]{1,0:T(8,128)(2,1)}, f32[16,128]{1,0:T(8,128)}) custom-call(f32[4,96,512]{2,1,0:T(8,128)} %get-tuple-element.72.hats_ref, f32[96,128]{1,0:T(8,128)} %get-tuple-element.73.scale_ref, bf16[96,1024]{1,0:T(8,128)(2,1)} %get-tuple-element.74.all_cot_ref, bf16[288,384]{1,0:T(8,128)(2,1)} %constant.63.clone.quad_t, ...), custom_call_target="tpu_custom_call" | custom-call | flops 4000000000 | bytes 16000000 | tf_op jit(solution)/shard_map/pallas_call | solution.py:312
  48.8 10.7 %shard_map.318 = (bf16[72,512]{1,0:T(8,128)(2,1)}, bf16[104,512]{1,0:T(8,128)(2,1)}, bf16[136,512]{1,0:T(8,128)(2,1)}, bf16[104,512]{1,0:T(8,128)(2,1)}, f32[4,1...) custom-call(s32[1]{0:T(128)} %bitcast.7.core_ref, ...), custom_call_target="tpu_custom_call" | custom-call | flops 6000000000 | bytes 16000000 | tf_op jit(solution)/shard_map/pallas_call | solution.py:388
  60.0 3.7 %shard_map.319.small_ref = f32[80,128]{1,0:T(8,128)} custom-call(f32[1152,128]{1,0:T(8,128)} %get-tuple-element.82.left_ref, f32[1152,128]{1,0:T(8,128)} %get-tuple-element.83.right_ref, bf16[256,384]{1,0:T(8,128)(2,1)} %constant.66.clone.spread_t, f32[16,128]{1,0:T(8,128)} %get-tuple-element.84.merge_gain_ref, f32[4,128]{1,0:T(4,128)} %get-tuple-element.85.norm_gain_ref), custom_call_target="tpu_custom_call" | custom-call | flops 2000000000 | bytes 4000000 | tf_op jit(solution)/shard_map/pallas_call | solution.py:422
  63.9 1.3 collective-permute-done.10.small_theirs_ref
  65.8 3.7 %shard_map.320 = bf16[8,592,128]{2,1,0:T(8,128)(2,1)} custom-call(bf16[288,1024]{1,0:T(8,128)(2,1)} %get-tuple-element.67.rows_ref, bf16[288,1024]{1,0:T(8,128)(2,1)} %copy-done.8, bf16[288,1024]{1,0:T(8,128)(2,1)} %get-tuple-element.80.columns_ref, bf16[288,1024]{1,0:T(8,128)(2,1)} %copy-done.7, f32[80,128]{1,0:T(8,128)} %shard_map.319.small_ref, ...), custom_call_target="tpu_custom_call" | custom-call | flops 2000000000 | bytes 4000000 | tf_op jit(solution)/shard_map/pallas_call | solution.py:455
  69.4 5.7 %all-to-all-start.1 = ((bf16[8,592,128]{2,1,0:T(8,128)(2,1)}), bf16[8,592,128]{2,1,0:T(8,128)(2,1)S(1)}, u32[]{:S(2)}, u32[]{:S(2)}) async-start(bf16[8,592,128]{2,1,0:T(8,128)(2,1)} %shard_map.320), calls=%async_computation.1 | async-start | bytes 2424832 | tf_op jit(solution)/shard_map/all_to_all | solution.py:551
  75.1 1.9 %collective-permute-start.12 = (bf16[136,512]{1,0:T(8,128)(2,1)}, bf16[136,512]{1,0:T(8,128)(2,1)S(1)}, u32[]{:S(2)}, u32[]{:S(2)}) collective-permute-start(bf16[136,512]{1,0:T(8,128)(2,1)} %get-tuple-element.94), channel_id=1, source_target_pairs={{252,0},{0,4},{4,8},{8,12},{12,16},{16,20},{20,24},{24,28},{28,32}... | collective-permute-start | bytes 417800 | tf_op jit(solution)/shard_map/ppermute | solution.py:474
  77.0 1.6 %collective-permute-start.13 = (bf16[104,512]{1,0:T(8,128)(2,1)}, bf16[104,512]{1,0:T(8,128)(2,1)S(1)}, u32[]{:S(2)}, u32[]{:S(2)}) collective-permute-start(bf16[104,512]{1,0:T(8,128)(2,1)} %get-tuple-element.95), channel_id=1, source_target_pairs={{255,0},{252,1},{253,2},{254,3},{3,4},{0,5},{1,6},{2,7},{7,8},{4,9... | collective-permute-start | bytes 319496 | tf_op jit(solution)/shard_map/ppermute | solution.py:547
  78.6 2.8 %shard_map.321.early_ref = bf16[16,64,128]{2,1,0:T(8,128)(2,1)} custom-call(bf16[16,80,768]{2,1,0:T(8,128)(2,1)} %copy-done), custom_call_target="tpu_custom_call" | custom-call | tf_op jit(solution)/shard_map/pallas_call | solution.py:488
  81.4 13.1 %collective-permute-done.11 = bf16[104,512]{1,0:T(8,128)(2,1)S(1)} collective-permute-done((bf16[104,512]{1,0:T(8,128)(2,1)}, bf16[104,512]{1,0:T(8,128)(2,1)S(1)}, u32[]{:S(2)}, u32[]{:S(2)}) %collective-permute-start.11) | collective-permute-done | bytes 106528 | tf_op jit(solution)/shard_map/ppermute | solution.py:474
  94.5 2.6 %all-to-all-done.1.late_ref = bf16[8,592,128]{2,1,0:T(8,128)(2,1)S(1)} async-done(((bf16[8,592,128]{2,1,0:T(8,128)(2,1)}), bf16[8,592,128]{2,1,0:T(8,128)(2,1)S(1)}, u32[]{:S(2)}, u32[]{:S(2)}) %all-to-all-start.1) | async-done | bytes 1212448 | tf_op jit(solution)/shard_map/all_to_all | solution.py:551
  97.0 1.1 copy-done.1
  98.1 2.4 %shard_map.322 = bf16[16,176,128]{2,1,0:T(8,128)(2,1)} custom-call(bf16[16,64,128]{2,1,0:T(8,128)(2,1)} %shard_map.321.early_ref, bf16[8,592,128]{2,1,0:T(8,128)(2,1)} %copy-done.1), custom_call_target="tpu_custom_call" | custom-call | tf_op jit(solution)/shard_map/pallas_call | solution.py:506
  100.5 3.7 %all-to-all-start.2 = ((bf16[16,176,128]{2,1,0:T(8,128)(2,1)}), bf16[16,176,128]{2,1,0:T(8,128)(2,1)S(1)}, u32[]{:S(2)}, u32[]{:S(2)}) async-start(bf16[16,176,128]{2,1,0:T(8,128)(2,1)} %shard_map.322), calls=%async_computation.2 | async-start | bytes 1441792 | tf_op jit(solution)/shard_map/all_to_all | solution.py:551
  104.3 0.8 slice.60
  105.2 0.8 reshape.104
  106.8 20.4 %all-to-all-done.2.got_ref = bf16[16,176,128]{2,1,0:T(8,128)(2,1)S(1)} async-done(((bf16[16,176,128]{2,1,0:T(8,128)(2,1)}), bf16[16,176,128]{2,1,0:T(8,128)(2,1)S(1)}, u32[]{:S(2)}, u32[]{:S(2)}) %all-to-all-start.2) | async-done | bytes 720928 | tf_op jit(solution)/shard_map/all_to_all | solution.py:551
  127.2 0.9 copy-done.2
  128.1 1.8 %shard_map.323 = (f32[8,384]{1,0:T(8,128)}, f32[8,128]{1,0:T(8,128)}, f32[32,256]{1,0:T(8,128)}, f32[4,128]{1,0:T(4,128)}, f32[16,128]{1,0:T(8,128)}, /*index=5*/f32[8,759]{1,0:T(8,128)}) custom-call(bf16[16,176,128]{2,1,0:T(8,128)(2,1)} %copy-done.2), custom_call_target="tpu_custom_call" | custom-call | tf_op jit(solution)/shard_map/pallas_call | solution.py:531
  (68 shorter events, 3.8 us)
Async XLA Ops:
  1.7 15.4 %copy-start.3 = (bf16[6,48,512]{2,1,0:T(8,128)(2,1)}, bf16[6,48,512]{2,1,0:T(8,128)(2,1)S(1)}, u32[]{:S(2)}) copy-start(bf16[6,48,512]{2,1,0:T(8,128)(2,1)S(1)} %reshape.84) | copy-start | bytes 884740
  1.7 15.4 %collective-permute-start.1 = (bf16[3,24,512]{2,1,0:T(8,128)(2,1)S(1)}, bf16[3,24,512]{2,1,0:T(8,128)(2,1)S(1)}, u32[]{:S(2)}, u32[]{:S(2)}) collective-permute-start(bf16[3,24,512]{2,1,0:T(8,128)(2,1)S(1)} %get-tuple-element.109), channel_id=1, source_target_pairs={{1,0},{2,1},{3,2},{0,3},{5,4},{6,5},{7,6},{4,7},{9,8},{10,9},{11,1... | collective-permute-start | bytes 221192 | tf_op jit(solution)/shard_map/ppermute | solution.py:474
  3.5 13.7 %collective-permute-start.2 = (bf16[3,24,512]{2,1,0:T(8,128)(2,1)S(1)}, bf16[3,24,512]{2,1,0:T(8,128)(2,1)S(1)}, u32[]{:S(2)}, u32[]{:S(2)}) collective-permute-start(bf16[3,24,512]{2,1,0:T(8,128)(2,1)S(1)} %get-tuple-element.108), channel_id=1, source_target_pairs={{5,0},{6,1},{7,2},{4,3},{9,4},{10,5},{11,6},{8,7},{13,8},{14,9},{1... | collective-permute-start | bytes 221192 | tf_op jit(solution)/shard_map/ppermute | solution.py:547
  8.8 8.4 %collective-permute-start = (bf16[6,24,512]{2,1,0:T(8,128)(2,1)S(1)}, bf16[6,24,512]{2,1,0:T(8,128)(2,1)S(1)}, u32[]{:S(2)}, u32[]{:S(2)}) collective-permute-start(bf16[6,24,512]{2,1,0:T(8,128)(2,1)S(1)} %slice.48), channel_id=1, source_target_pairs={{4,0},{8,4},{12,8},{16,12},{20,16},{24,20},{28,24},{32,28},{36,32}... | collective-permute-start | bytes 442376 | tf_op jit(solution)/shard_map/ppermute | solution.py:474
  12.3 4.8 %copy-start.4 = (bf16[3,24,1024]{2,1,0:T(8,128)(2,1)}, bf16[3,24,1024]{2,1,0:T(8,128)(2,1)S(1)}, u32[]{:S(2)}) copy-start(bf16[3,24,1024]{2,1,0:T(8,128)(2,1)S(1)} %reshape.93.cot_ref) | copy-start | bytes 442372
  12.4 15.2 %collective-permute-start.6 = (bf16[2,12,1024]{2,1,0:T(8,128)(2,1)S(1)}, bf16[2,12,1024]{2,1,0:T(8,128)(2,1)S(1)}, u32[]{:S(2)}, u32[]{:S(2)}) collective-permute-start(bf16[2,12,1024]{2,1,0:T(8,128)(2,1)S(1)} %get-tuple-element.112), channel_id=1, source_target_pairs={{4,0},{8,4},{12,8},{16,12},{20,16},{24,20},{28,24},{32,28},{36,32}... | collective-permute-start | bytes 147464 | tf_op jit(solution)/shard_map/ppermute | solution.py:474
  13.4 14.1 %collective-permute-start.7 = (bf16[2,12,1024]{2,1,0:T(8,128)(2,1)S(1)}, bf16[2,12,1024]{2,1,0:T(8,128)(2,1)S(1)}, u32[]{:S(2)}, u32[]{:S(2)}) collective-permute-start(bf16[2,12,1024]{2,1,0:T(8,128)(2,1)S(1)} %get-tuple-element.111), channel_id=1, source_target_pairs={{1,0},{2,1},{3,2},{0,3},{5,4},{6,5},{7,6},{4,7},{9,8},{10,9},{11,1... | collective-permute-start | bytes 147464 | tf_op jit(solution)/shard_map/ppermute | solution.py:474
  17.1 0.6 copy-start.10
  17.1 10.5 %collective-permute-start.8 = (bf16[2,12,1024]{2,1,0:T(8,128)(2,1)S(1)}, bf16[2,12,1024]{2,1,0:T(8,128)(2,1)S(1)}, u32[]{:S(2)}, u32[]{:S(2)}) collective-permute-start(bf16[2,12,1024]{2,1,0:T(8,128)(2,1)S(1)} %get-tuple-element.110), channel_id=1, source_target_pairs={{5,0},{6,1},{7,2},{4,3},{9,4},{10,5},{11,6},{8,7},{13,8},{14,9},{1... | collective-permute-start | bytes 147464 | tf_op jit(solution)/shard_map/ppermute | solution.py:547
  17.2 0.6 copy-start.11
  17.2 0.7 copy-start.9
  24.3 5.2 %collective-permute-start.4 = (bf16[48,512]{1,0:T(8,128)(2,1)}, bf16[48,512]{1,0:T(8,128)(2,1)S(1)}, u32[]{:S(2)}, u32[]{:S(2)}) collective-permute-start(bf16[48,512]{1,0:T(8,128)(2,1)} %get-tuple-element.69), channel_id=1, source_target_pairs={{3,0},{0,1},{1,2},{2,3},{7,4},{4,5},{5,6},{6,7},{11,8},{8,9},{9,10... | collective-permute-start | bytes 147464 | tf_op jit(solution)/shard_map/ppermute | solution.py:474
  25.4 4.2 %collective-permute-start.5 = (bf16[48,512]{1,0:T(8,128)(2,1)}, bf16[48,512]{1,0:T(8,128)(2,1)S(1)}, u32[]{:S(2)}, u32[]{:S(2)}) collective-permute-start(bf16[48,512]{1,0:T(8,128)(2,1)} %get-tuple-element.70), channel_id=1, source_target_pairs={{1,0},{2,1},{3,2},{0,3},{5,4},{6,5},{7,6},{4,7},{9,8},{10,9},{11,1... | collective-permute-start | bytes 147464 | tf_op jit(solution)/shard_map/ppermute | solution.py:474
  27.6 2.1 %copy-start.12 = (bf16[2,12,1024]{2,1,0:T(8,128)(2,1)}, bf16[2,12,1024]{2,1,0:T(8,128)(2,1)S(1)}, u32[]{:S(2)}) copy-start(bf16[2,12,1024]{2,1,0:T(8,128)(2,1)S(1)} %collective-permute-done.6.cot_west_ref) | copy-start | bytes 147460
  27.6 2.1 %copy-start.13 = (bf16[2,12,1024]{2,1,0:T(8,128)(2,1)}, bf16[2,12,1024]{2,1,0:T(8,128)(2,1)S(1)}, u32[]{:S(2)}) copy-start(bf16[2,12,1024]{2,1,0:T(8,128)(2,1)S(1)} %collective-permute-done.7.cot_south_ref) | copy-start | bytes 147460
  27.6 2.0 %copy-start.14 = (bf16[2,12,1024]{2,1,0:T(8,128)(2,1)}, bf16[2,12,1024]{2,1,0:T(8,128)(2,1)S(1)}, u32[]{:S(2)}) copy-start(bf16[2,12,1024]{2,1,0:T(8,128)(2,1)S(1)} %collective-permute-done.8.cot_corner_ref) | copy-start | bytes 147460
  34.1 35.3 %all-to-all-start = ((bf16[16,80,768]{2,1,0:T(8,128)(2,1)}), bf16[16,80,768]{2,1,0:T(8,128)(2,1)S(1)}, u32[]{:S(2)}, u32[]{:S(2)}) async-start(bf16[16,80,768]{2,1,0:T(8,128)(2,1)} %get-tuple-element.88), calls=%async_computation | async-start | bytes 3932160 | tf_op jit(solution)/shard_map/all_to_all | solution.py:551
  48.8 10.9 %copy-start.6 = (bf16[288,1024]{1,0:T(8,128)(2,1)S(1)}, bf16[288,1024]{1,0:T(8,128)(2,1)}, u32[]{:S(2)}) copy-start(bf16[288,1024]{1,0:T(8,128)(2,1)} %get-tuple-element.67.rows_ref) | copy-start | bytes 1769476
  59.4 4.3 %collective-permute-start.9 = (bf16[288,1024]{1,0:T(8,128)(2,1)}, bf16[288,1024]{1,0:T(8,128)(2,1)S(1)}, u32[]{:S(2)}, u32[]{:S(2)}) collective-permute-start(bf16[288,1024]{1,0:T(8,128)(2,1)} %get-tuple-element.81), channel_id=1, source_target_pairs={{1,0},{0,1},{3,2},{2,3},{5,4},{4,5},{7,6},{6,7},{9,8},{8,9},{11,10... | collective-permute-start | bytes 1769480 | tf_op jit(solution)/shard_map/ppermute | solution.py:542
  59.6 4.2 %collective-permute-start.3 = (bf16[288,1024]{1,0:T(8,128)(2,1)S(1)}, bf16[288,1024]{1,0:T(8,128)(2,1)S(1)}, u32[]{:S(2)}, u32[]{:S(2)}) collective-permute-start(bf16[288,1024]{1,0:T(8,128)(2,1)S(1)} %copy-done.6), channel_id=1, source_target_pairs={{1,0},{0,1},{3,2},{2,3},{5,4},{4,5},{7,6},{6,7},{9,8},{8,9},{11,10... | collective-permute-start | bytes 1769480 | tf_op jit(solution)/shard_map/ppermute | solution.py:542
  63.7 1.4 %copy-start.7 = (bf16[288,1024]{1,0:T(8,128)(2,1)}, bf16[288,1024]{1,0:T(8,128)(2,1)S(1)}, u32[]{:S(2)}) copy-start(bf16[288,1024]{1,0:T(8,128)(2,1)S(1)} %collective-permute-done.9.columns_theirs_ref) | copy-start | bytes 1769476
  63.7 1.4 %collective-permute-start.10 = (f32[80,128]{1,0:T(8,128)}, f32[80,128]{1,0:T(8,128)S(1)}, u32[]{:S(2)}, u32[]{:S(2)}) collective-permute-start(f32[80,128]{1,0:T(8,128)} %shard_map.319.small_ref), channel_id=1, source_target_pairs={{1,0},{0,1},{3,2},{2,3},{5,4},{4,5},{7,6},{6,7},{9,8},{8,9},{11,10... | collective-permute-start | bytes 122888 | tf_op jit(solution)/shard_map/ppermute | solution.py:542
  63.9 1.3 copy-start.8
  69.4 9.2 %copy-start = (bf16[16,80,768]{2,1,0:T(8,128)(2,1)}, bf16[16,80,768]{2,1,0:T(8,128)(2,1)S(1)}, u32[]{:S(2)}) copy-start(bf16[16,80,768]{2,1,0:T(8,128)(2,1)S(1)} %all-to-all-done.early_ref) | copy-start | bytes 5898244
  69.4 27.6 %all-to-all-start.1 = ((bf16[8,592,128]{2,1,0:T(8,128)(2,1)}), bf16[8,592,128]{2,1,0:T(8,128)(2,1)S(1)}, u32[]{:S(2)}, u32[]{:S(2)}) async-start(bf16[8,592,128]{2,1,0:T(8,128)(2,1)} %shard_map.320), calls=%async_computation.1 | async-start | bytes 2424832 | tf_op jit(solution)/shard_map/all_to_all | solution.py:551
  75.1 19.4 %collective-permute-start.12 = (bf16[136,512]{1,0:T(8,128)(2,1)}, bf16[136,512]{1,0:T(8,128)(2,1)S(1)}, u32[]{:S(2)}, u32[]{:S(2)}) collective-permute-start(bf16[136,512]{1,0:T(8,128)(2,1)} %get-tuple-element.94), channel_id=1, source_target_pairs={{252,0},{0,4},{4,8},{8,12},{12,16},{16,20},{20,24},{24,28},{28,32}... | collective-permute-start | bytes 417800 | tf_op jit(solution)/shard_map/ppermute | solution.py:474
  77.0 17.5 %collective-permute-start.11 = (bf16[104,512]{1,0:T(8,128)(2,1)}, bf16[104,512]{1,0:T(8,128)(2,1)S(1)}, u32[]{:S(2)}, u32[]{:S(2)}) collective-permute-start(bf16[104,512]{1,0:T(8,128)(2,1)} %get-tuple-element.90), channel_id=1, source_target_pairs={{3,0},{0,1},{1,2},{2,3},{7,4},{4,5},{5,6},{6,7},{11,8},{8,9},{9,10... | collective-permute-start | bytes 319496 | tf_op jit(solution)/shard_map/ppermute | solution.py:474
  77.0 17.5 %collective-permute-start.13 = (bf16[104,512]{1,0:T(8,128)(2,1)}, bf16[104,512]{1,0:T(8,128)(2,1)S(1)}, u32[]{:S(2)}, u32[]{:S(2)}) collective-permute-start(bf16[104,512]{1,0:T(8,128)(2,1)} %get-tuple-element.95), channel_id=1, source_target_pairs={{255,0},{252,1},{253,2},{254,3},{3,4},{0,5},{1,6},{2,7},{7,8},{4,9... | collective-permute-start | bytes 319496 | tf_op jit(solution)/shard_map/ppermute | solution.py:547
  97.0 1.1 copy-start.1
  100.5 4.6 %copy-start.5 = (bf16[72,512]{1,0:T(8,128)(2,1)S(1)}, bf16[72,512]{1,0:T(8,128)(2,1)}, u32[]{:S(2)}) copy-start(bf16[72,512]{1,0:T(8,128)(2,1)} %get-tuple-element.99) | copy-start | bytes 221188
  100.5 26.7 %all-to-all-start.2 = ((bf16[16,176,128]{2,1,0:T(8,128)(2,1)}), bf16[16,176,128]{2,1,0:T(8,128)(2,1)S(1)}, u32[]{:S(2)}, u32[]{:S(2)}) async-start(bf16[16,176,128]{2,1,0:T(8,128)(2,1)} %shard_map.322), calls=%async_computation.2 | async-start | bytes 1441792 | tf_op jit(solution)/shard_map/all_to_all | solution.py:551
  127.2 0.9 copy-start.2
  (3 other events, 1.8 us)

commit v3 on v2

--- a/solution.py
+++ b/solution.py
@@ -19,7 +19,7 @@
 TABLE = 759
 AXES = ("x", "yl", "z", "yh", "c")
 LON, LAT = ("x", "yl", "z"), ("yh", "c")
-NEAR, FAR, CLOSE = ("x", "yl"), ("z", "yh"), ("x", "yl", "c")
+NEAR, FAR, CLOSE = ("yl", "x"), ("yh", "z"), ("x", "yl", "c")
 BF, F32 = jnp.bfloat16, jnp.float32
 
 
@@ -286,7 +286,7 @@
 
 
 def merge_kernel(
-    hats_ref, scale_ref, all_cot_ref, quad_t, coarse, gain_ref, wmerge_ref, merged_ref, back_ref, gain_grad_ref,
+    hats_ref, scale_ref, all_cot_ref, quad_t, gain_ref, wmerge_ref, back_ref, gain_grad_ref,
 ):
     gains = [gain_ref[:, 512 * k : 512 * k + 512] for k in range(4)]
     hats = [hats_ref[k] for k in range(4)]
@@ -295,9 +295,6 @@
     cots = [mm_nt(cot_all, wmerge_ref[512 * k : 512 * k + 512, :]).astype(BF).astype(F32) for k in range(4)]
     pulled = norm_back(hats, scale, cots, gains, 2048)
     back_ref[...] = mm(quad_t[...], jnp.concatenate(pulled, axis=0).astype(BF)).astype(BF)
-    normed = [(h * g).astype(BF) for h, g in zip(hats, gains)]
-    merged = sum(mm(normed[k], wmerge_ref[512 * k : 512 * k + 512, :]) for k in range(4)).astype(BF)
-    merged_ref[...] = mm(coarse[...], merged).astype(BF)
     for k in range(4):
         summed = jnp.sum((cots[k] * hats[k])[:72], axis=0, keepdims=True)
         for i in range(4):
@@ -306,22 +303,21 @@
 
 def merge(hats, scale, all_cot, gain, wmerge):
     shapes = [
-        jax.ShapeDtypeStruct((96, 1024), BF), jax.ShapeDtypeStruct((TOK, 512), BF),
-        jax.ShapeDtypeStruct((16, 128), F32),
+        jax.ShapeDtypeStruct((TOK, 512), BF), jax.ShapeDtypeStruct((16, 128), F32),
     ]
     return pl.pallas_call(
         merge_kernel,
         out_shape=shapes,
-        in_specs=vmem(7),
-        out_specs=vmem(3),
+        in_specs=vmem(6),
+        out_specs=vmem(2),
         compiler_params=PARAMS,
         cost_estimate=cost(4_000_000_000, 16_000_000),
-    )(hats, scale, all_cot, plan("quad_t"), plan("coarse"), gain, wmerge)
+    )(hats, scale, all_cot, plan("quad_t"), gain, wmerge)
 
 
 def back_kernel(
-    core_ref, cot_ref, x_ref, qkv_ref, p_ref, wqkv_ref, wproj_ref, gain_ref, merged_ref, back_plan,
-    stay_ref, north_ref, east_ref, corner_ref, gain_grad_ref, mine_ref, theirs_ref, left_ref, right_ref, dqkv_ref,
+    core_ref, cot_ref, x_ref, qkv_ref, p_ref, wqkv_ref, wproj_ref, gain_ref, back_plan,
+    home_ref, gain_grad_ref, mine_ref, theirs_ref, left_ref, right_ref, dqkv_ref,
 ):
     cot = cot_ref[...]
     mixed_cot = mm_nt(cot, wproj_ref[...]).astype(BF)
@@ -364,12 +360,7 @@
         gain_grad_ref[i : i + 1, :] = gain_grad[:, 128 * i : 128 * i + 128]
     (pulled,) = norm_back([hat], scale, [normed_cot], [gain], 512)
     total = (cot.astype(F32) + pulled.astype(BF).astype(F32)).astype(BF)
-    home = mm(back_plan[...], total)
-    stay_ref[...] = home[:72].astype(BF)
-    for out_ref, start, rows, part in ((east_ref, 32, 32, 2), (north_ref, 64, 16, 1), (corner_ref, 80, 16, 3)):
-        out_ref[:rows, :] = merged_ref[start : start + rows, :512]
-        out_ref[rows : 2 * rows, :] = merged_ref[start : start + rows, 512:]
-        out_ref[2 * rows :, :] = home[72 * part : 72 * part + 72].astype(BF)
+    home_ref[...] = mm(back_plan[...], total).astype(BF)
     core = core_ref[0]
     for out_ref, owner in ((theirs_ref, 1 - core), (mine_ref, core)):
         for yh in range(2):
@@ -379,21 +370,48 @@
             out_ref[:, 768 + 128 * yh : 896 + 128 * yh] = cot_ref[:, pl.ds(first, 128)]
 
 
-def attend_back(core, cot, x, qkv, p, wqkv, wproj, gain, merged):
+def attend_back(core, cot, x, qkv, p, wqkv, wproj, gain):
     shapes = [
-        jax.ShapeDtypeStruct((72, 512), BF), jax.ShapeDtypeStruct((104, 512), BF),
-        jax.ShapeDtypeStruct((136, 512), BF), jax.ShapeDtypeStruct((104, 512), BF),
-        jax.ShapeDtypeStruct((4, 128), F32),
+        jax.ShapeDtypeStruct((TOK, 512), BF), jax.ShapeDtypeStruct((4, 128), F32),
     ] + [jax.ShapeDtypeStruct((TOK, 1024), BF)] * 2 + [jax.ShapeDtypeStruct((8 * WIN, 128), F32)] * 2
     return pl.pallas_call(
         back_kernel,
         out_shape=shapes,
-        in_specs=[pl.BlockSpec(memory_space=pltpu.SMEM)] + vmem(9),
-        out_specs=vmem(9),
+        in_specs=[pl.BlockSpec(memory_space=pltpu.SMEM)] + vmem(8),
+        out_specs=vmem(6),
         scratch_shapes=[pltpu.VMEM((TOK, 1536), BF)],
         compiler_params=PARAMS,
         cost_estimate=cost(6_000_000_000, 16_000_000),
-    )(core, cot, x, qkv, p, wqkv, wproj, gain, merged, plan("back"))
+    )(core, cot, x, qkv, p, wqkv, wproj, gain, plan("back"))
+
+
+def home_kernel(
+    hats_ref, gain_ref, wmerge_ref, coarse, home_ref, stay_ref, merged_ref, north_ref, east_ref, corner_ref,
+):
+    merged = 0.0
+    for k in range(4):
+        normed = (hats_ref[k] * gain_ref[:, 512 * k : 512 * k + 512]).astype(BF)
+        merged = merged + mm(normed, wmerge_ref[512 * k : 512 * k + 512, :])
+    merged = mm(coarse[...], merged.astype(BF))
+    home = home_ref[...].astype(F32)
+    stay_ref[...] = home[:72].astype(BF)
+    merged_ref[...] = merged[:32].astype(BF)
+    for out_ref, start, rows, part in ((east_ref, 32, 32, 2), (north_ref, 64, 16, 1), (corner_ref, 80, 16, 3)):
+        out_ref[:rows, :] = merged[start : start + rows, :512].astype(BF)
+        out_ref[rows : 2 * rows, :] = merged[start : start + rows, 512:].astype(BF)
+        out_ref[2 * rows :, :] = home[72 * part : 72 * part + 72].astype(BF)
+
+
+def home_parts(hats, gain, wmerge, home):
+    shapes = [(72, 512), (32, 1024), (104, 512), (136, 512), (104, 512)]
+    return pl.pallas_call(
+        home_kernel,
+        out_shape=[jax.ShapeDtypeStruct(s, BF) for s in shapes],
+        in_specs=vmem(5),
+        out_specs=vmem(5),
+        compiler_params=PARAMS,
+        cost_estimate=cost(1_000_000_000, 8_000_000),
+    )(hats, gain, wmerge, plan("coarse"), home)
 
 
 def small_kernel(left_ref, right_ref, spread_t, merge_gain_ref, norm_gain_ref, small_ref, wide_ref):
@@ -444,8 +462,8 @@
             for t in range(2):
                 piece = jnp.concatenate([chunk[2 * t], chunk[2 * t + 1]], axis=1).astype(BF)
                 for z in range(8):
-                    start = 64 * z + 32 * yh + 16 * t
-                    out_ref[xy, start : start + 16, :] = piece[z]
+                    start = 256 * yh + 32 * z + 16 * t
+                    out_ref[4 * (xy % 2) + xy // 2, start : start + 16, :] = piece[z]
     small = (small_ref[...] + small_theirs_ref[...]).astype(BF)
     for xy in range(8):
         out_ref[xy, 512:, :] = small
@@ -481,7 +499,7 @@
         for yh in range(2):
             for t in range(2):
                 piece = grad[32 * z : 32 * z + 32, 256 * yh + 128 * t : 256 * yh + 128 * t + 128]
-                out_ref[2 * z + yh, 32 * t : 32 * t + 32, :] = piece.astype(BF)
+                out_ref[8 * yh + z, 32 * t : 32 * t + 32, :] = piece.astype(BF)
 
 
 def pair_grad(early):
@@ -580,21 +598,22 @@
     core = lax.axis_index("c").astype(jnp.int32).reshape(1)
     pair, hats, scale, all_cot = stack(block, prev, following, cot, cot_west, cot_south, cot_corner, wide_gain)
     early = spread_over(pair, CLOSE)
-    merged, attn_cot, merge_gain_part = merge(hats, scale, all_cot, wide_gain, merge_weight)
+    attn_cot, merge_gain_part = merge(hats, scale, all_cot, wide_gain, merge_weight)
     rows_theirs = swapped(rows, "c", 1)
-    stay, north, east, corner, norm_gain_part, columns, columns_out, left, right = attend_back(
-        core, attn_cot, x, qkv, p, qkv_weight, proj_weight, gain, merged
+    home, norm_gain_part, columns, columns_out, left, right = attend_back(
+        core, attn_cot, x, qkv, p, qkv_weight, proj_weight, gain
     )
     columns_theirs = swapped(columns_out, "c", 1)
     small = small_grads(left, right, merge_gain_part, norm_gain_part)
     columns_theirs, small = lax.optimization_barrier((columns_theirs, small))
     late = late_grads(rows, rows_theirs, columns, columns_theirs, small, swapped(small, "c", 1))
-    late, early = lax.optimization_barrier((late, early))
+    late, early, home = lax.optimization_barrier((late, early, home))
     late = spread_over(late, NEAR)
+    stay, merged, north, east, corner = home_parts(hats, wide_gain, merge_weight, home)
     north, east, corner = moved(north, LAT, 1), moved(east, LON, 1), diagonal(corner, 1)
-    north, early = lax.optimization_barrier((north, pair_grad(early)))
-    late, early, north, east, corner = lax.optimization_barrier((late, early, north, east, corner))
-    got = spread_over(fold(early, late), FAR)
+    last = fold(pair_grad(early), late)
+    last, north, east, corner = lax.optimization_barrier((last, north, east, corner))
+    got = spread_over(last, FAR)
     grad = quarters(
         corner[32:].reshape(3, 24, 512), north[32:].reshape(3, 24, 512), east[64:].reshape(3, 24, 512),
         stay.reshape(3, 24, 512),

time: 131 us -> 128 us (0.977)
  waiting for transfers between devices: 39.4 us -> 33.6 us
  Pallas kernels: 45 us -> 48.2 us
    ppermute x8, waiting for transfers between devices: 15.1 us -> 2.04 us  [moved(): lax.ppermute(block, axes, [((i - distance) % count, i) for i in range(cou...]
    all_to_all x3, waiting for transfers between devices: 23 us -> 30.3 us  [spread_over(): return lax.all_to_all(parts, axes, 0, 0, tiled=True)]
    pallas_call x1 -> x2, Pallas kernels: 6.11 us -> 9.43 us  [the longest x1 5.28 us: merge(): pl.pallas_call(merge_kernel, out_shape=shapes, in_specs=vmem(6), out_spec...]
    unnamed x36 -> x38, local copies, waits for them, and re-layouts: 3.85 us -> 3.88 us
  transfers between devices with their start and end apart: 17 -> 17, of which waited for: 6 -> 6; matrix products, arithmetic and copies ran while one was open for 3% -> 2% of each run, Pallas kernels for 28% -> 34%
where the time goes in v3:
time: 128 us; the launch traced here: 126 us
  Pallas kernels  48.2 us (38%)
  starting transfers between devices  35.7 us (28%)
  waiting for transfers between devices  33.6 us (26%)
  local copies, waits for them, and re-layouts  7.49 us (6%)
    all_to_all x3, waiting for transfers between devices, spread_over(): return lax.all_to_all(parts, axes, 0, 0, tiled=True)  30.3 us
    all_to_all x3, starting transfers between devices, spread_over(): return lax.all_to_all(parts, axes, 0, 0, tiled=True)  17.5 us
    ppermute x8, starting transfers between devices, moved(): lax.ppermute(block, axes, [((i - distance) % count, i) for i in range(cou...  10.7 us
    pallas_call x1, Pallas kernels, attend_back(): pl.pallas_call(back_kernel, out_shape=shapes, in_specs=[pl.BlockSpec(memo...  10.6 us
    ppermute x3, starting transfers between devices, diagonal(): return lax.ppermute(block, AXES, route)  6.87 us
    pallas_call x1, Pallas kernels, attend(): pl.pallas_call(attend_kernel, out_shape=[jax.ShapeDtypeStruct(s, BF) for...  6.42 us
    pallas_call x1, Pallas kernels, merge(): pl.pallas_call(merge_kernel, out_shape=shapes, in_specs=vmem(6), out_spec...  5.28 us
    pallas_call x1, Pallas kernels, home_parts(): pl.pallas_call(home_kernel, out_shape=[jax.ShapeDtypeStruct(s, BF) for s...  4.16 us
  transfers between devices with their start and end apart: 17, of which 6 were waited for; matrix products, arithmetic and copies ran while one was open for 2% of the time, Pallas kernels for 34%

profile of v3, /device:TPU:8, one launch (start us, length us, event | category | flops | bytes accessed | tf_op | source)
XLA Modules:
  0.0 126.0 jit_solution(2171569041010384659)
XLA Ops:
  0.6 1.0 reshape.84
  1.7 1.8 %collective-permute-start.1 = (bf16[3,24,512]{2,1,0:T(8,128)(2,1)S(1)}, bf16[3,24,512]{2,1,0:T(8,128)(2,1)S(1)}, u32[]{:S(2)}, u32[]{:S(2)}) collective-permute-start(bf16[3,24,512]{2,1,0:T(8,128)(2,1)S(1)} %get-tuple-element.107), channel_id=1, source_target_pairs={{1,0},{2,1},{3,2},{0,3},{5,4},{6,5},{7,6},{4,7},{9,8},{10,9},{11,1... | collective-permute-start | bytes 221192 | tf_op jit(solution)/shard_map/ppermute | solution.py:492
  3.5 5.2 %collective-permute-start.2 = (bf16[3,24,512]{2,1,0:T(8,128)(2,1)S(1)}, bf16[3,24,512]{2,1,0:T(8,128)(2,1)S(1)}, u32[]{:S(2)}, u32[]{:S(2)}) collective-permute-start(bf16[3,24,512]{2,1,0:T(8,128)(2,1)S(1)} %get-tuple-element.106), channel_id=1, source_target_pairs={{5,0},{6,1},{7,2},{4,3},{9,4},{10,5},{11,6},{8,7},{13,8},{14,9},{1... | collective-permute-start | bytes 221192 | tf_op jit(solution)/shard_map/ppermute | solution.py:565
  8.8 2.6 %collective-permute-start = (bf16[6,24,512]{2,1,0:T(8,128)(2,1)S(1)}, bf16[6,24,512]{2,1,0:T(8,128)(2,1)S(1)}, u32[]{:S(2)}, u32[]{:S(2)}) collective-permute-start(bf16[6,24,512]{2,1,0:T(8,128)(2,1)S(1)} %slice.48), channel_id=1, source_target_pairs={{4,0},{8,4},{12,8},{16,12},{20,16},{24,20},{28,24},{32,28},{36,32}... | collective-permute-start | bytes 442376 | tf_op jit(solution)/shard_map/ppermute | solution.py:492
  11.4 0.9 reshape.93.cot_ref
  12.4 1.1 collective-permute-start.6
  13.4 3.6 %shard_map.314 = (f32[8,144,144]{2,1,0:T(8,128)}, f32[2,144,144]{2,1,0:T(8,128)}) custom-call(s32[1]{0:T(128)} %bitcast.2.last_ref, f32[8,759]{1,0:T(8,128)} %table_ref.1, bf16[384,256]{1,0:T(8,128)(2,1)} %constant.48.clone.spread_ref, bf16[144,144]{1,0:T(8,128)(2,1)} %constant.49.clone.level_ref, bf16[144,144]{1,0:T(8,128)(2,1)} %constant.50.clone.north_ref), custom_call_target="tpu_custom_call" | custom-call | flops 2000000000 | bytes 4000000 | tf_op jit(solution)/shard_map/pallas_call | solution.py:160
  17.9 6.4 %shard_map.315 = (bf16[288,512]{1,0:T(8,128)(2,1)}, bf16[288,1536]{1,0:T(8,128)(2,1)}, bf16[16,144,144]{2,1,0:T(8,128)(2,1)}, bf16[288,1024]{1,0:T(8,128)(2,1)},...) custom-call(bf16[288,512]{1,0:T(8,128)(2,1)} %bitcast.22, bf16[144,512]{1,0:T(8,128)(2,1)} %bitcast.34, ...), custom_call_target="tpu_custom_call" | custom-call | flops 4000000000 | bytes 8000000 | tf_op jit(solution)/shard_map/pallas_call | solution.py:233
  24.3 1.1 collective-permute-start.4
  25.4 2.2 %collective-permute-start.5 = (bf16[48,512]{1,0:T(8,128)(2,1)}, bf16[48,512]{1,0:T(8,128)(2,1)S(1)}, u32[]{:S(2)}, u32[]{:S(2)}) collective-permute-start(bf16[48,512]{1,0:T(8,128)(2,1)} %get-tuple-element.69), channel_id=1, source_target_pairs={{1,0},{2,1},{3,2},{0,3},{5,4},{6,5},{7,6},{4,7},{9,8},{10,9},{11,1... | collective-permute-start | bytes 147464 | tf_op jit(solution)/shard_map/ppermute | solution.py:492
  27.6 1.9 %collective-permute-done.4.prev_ref = bf16[48,512]{1,0:T(8,128)(2,1)S(1)} collective-permute-done((bf16[48,512]{1,0:T(8,128)(2,1)}, bf16[48,512]{1,0:T(8,128)(2,1)S(1)}, u32[]{:S(2)}, u32[]{:S(2)}) %collective-permute-start.4) | collective-permute-done | bytes 49184 | tf_op jit(solution)/shard_map/ppermute | solution.py:492
  30.2 3.8 %shard_map.316 = (bf16[16,80,768]{2,1,0:T(8,128)(2,1)}, f32[4,96,512]{2,1,0:T(8,128)}, f32[96,128]{1,0:T(8,128)}, bf16[96,1024]{1,0:T(8,128)(2,1)}) custom-call(bf16[288,512]{1,0:T(8,128)(2,1)} %get-tuple-element.67.block_ref, bf16[48,512]{1,0:T(8,128)(2,1)} %copy-done.16, bf16[48,512]{1,0:T(8,128)(2,1)} %copy-done.17, bf16[3,24,1024]{2,1,0:T(8,128)(2,1)} %copy-done.4, ...), custom_call_target="tpu_custom_call" | custom-call | flops 2000000000 | bytes 8000000 | tf_op jit(solution)/shard_map/pallas_call | solution.py:278
  34.1 8.6 %all-to-all-start = ((bf16[16,80,768]{2,1,0:T(8,128)(2,1)}), bf16[16,80,768]{2,1,0:T(8,128)(2,1)S(1)}, u32[]{:S(2)}, u32[]{:S(2)}) async-start(bf16[16,80,768]{2,1,0:T(8,128)(2,1)} %get-tuple-element.86), calls=%async_computation | async-start | bytes 3932160 | tf_op jit(solution)/shard_map/all_to_all | solution.py:569
  42.6 5.3 %shard_map.317 = (bf16[288,512]{1,0:T(8,128)(2,1)}, f32[16,128]{1,0:T(8,128)}) custom-call(f32[4,96,512]{2,1,0:T(8,128)} %get-tuple-element.71.hats_ref, f32[96,128]{1,0:T(8,128)} %get-tuple-element.72.scale_ref, bf16[96,1024]{1,0:T(8,128)(2,1)} %get-tuple-element.73.all_cot_ref, bf16[288,384]{1,0:T(8,128)(2,1)} %constant.63.clone.quad_t, ...), custom_call_target="tpu_custom_call" | custom-call | flops 4000000000 | bytes 16000000 | tf_op jit(solution)/shard_map/pallas_call | solution.py:308
  47.9 10.6 %shard_map.318 = (bf16[288,512]{1,0:T(8,128)(2,1)}, f32[4,128]{1,0:T(4,128)}, bf16[288,1024]{1,0:T(8,128)(2,1)}, bf16[288,1024]{1,0:T(8,128)(2,1)}, f32[1152,128]{1,0:T(8,128)}, /*index=5*/f32[1152,128]{1,0:T(8,128)}) custom-call(s32[1]{0:T(128)} %bitcast.7.core_ref, bf16[288,512]{1,0:T(8,128)(2,1)} %get-tuple-element.74.cot_ref, ...), custom_call_target="tpu_custom_call" | custom-call | flops 6000000000 | bytes 16000000 | tf_op jit(solution)/shard_map/pallas_call | solution.py:377
  59.0 3.7 %shard_map.319.small_ref = f32[80,128]{1,0:T(8,128)} custom-call(f32[1152,128]{1,0:T(8,128)} %get-tuple-element.80.left_ref, f32[1152,128]{1,0:T(8,128)} %get-tuple-element.81.right_ref, bf16[256,384]{1,0:T(8,128)(2,1)} %constant.65.clone.spread_t, f32[16,128]{1,0:T(8,128)} %get-tuple-element.82.merge_gain_ref, f32[4,128]{1,0:T(4,128)} %get-tuple-element.83.norm_gain_ref), custom_call_target="tpu_custom_call" | custom-call | flops 2000000000 | bytes 4000000 | tf_op jit(solution)/shard_map/pallas_call | solution.py:440
  62.9 1.3 %collective-permute-done.10.small_theirs_ref = f32[80,128]{1,0:T(8,128)S(1)} collective-permute-done((f32[80,128]{1,0:T(8,128)}, f32[80,128]{1,0:T(8,128)S(1)}, u32[]{:S(2)}, u32[]{:S(2)}) %collective-permute-start.10) | collective-permute-done | bytes 40992 | tf_op jit(solution)/shard_map/ppermute | solution.py:560
  64.8 3.6 %shard_map.320 = bf16[8,592,128]{2,1,0:T(8,128)(2,1)} custom-call(bf16[288,1024]{1,0:T(8,128)(2,1)} %get-tuple-element.66.rows_ref, bf16[288,1024]{1,0:T(8,128)(2,1)} %copy-done.9, bf16[288,1024]{1,0:T(8,128)(2,1)} %get-tuple-element.78.columns_ref, bf16[288,1024]{1,0:T(8,128)(2,1)} %copy-done.8, f32[80,128]{1,0:T(8,128)} %shard_map.319.small_ref, ...), custom_call_target="tpu_custom_call" | custom-call | flops 2000000000 | bytes 4000000 | tf_op jit(solution)/shard_map/pallas_call | solution.py:473
  68.9 5.2 %all-to-all-start.1 = ((bf16[8,592,128]{2,1,0:T(8,128)(2,1)}), bf16[8,592,128]{2,1,0:T(8,128)(2,1)S(1)}, u32[]{:S(2)}, u32[]{:S(2)}) async-start(bf16[8,592,128]{2,1,0:T(8,128)(2,1)} %shard_map.320), calls=%async_computation.1 | async-start | bytes 2424832 | tf_op jit(solution)/shard_map/all_to_all | solution.py:569
  74.1 4.2 %shard_map.323 = (bf16[72,512]{1,0:T(8,128)(2,1)}, bf16[32,1024]{1,0:T(8,128)(2,1)}, bf16[104,512]{1,0:T(8,128)(2,1)}, bf16[136,512]{1,0:T(8,128)(2,1)}, bf16[104,512]{1,0:T(8,128)(2,1)}) custom-call(f32[4,96,512]{2,1,0:T(8,128)} %get-tuple-element.71.hats_ref, f32[1,2048]{1,0:T(1,128)} %bitcast.33, bf16[2048,1024]{1,0:T(8,128)(2,1)} %wmerge_ref.3, ...), custom_call_target="tpu_custom_call" | custom-call | flops 1000000000 | bytes 8000000 | tf_op jit(solution)/shard_map/pallas_call | solution.py:407
  78.3 1.9 %collective-permute-start.12 = (bf16[136,512]{1,0:T(8,128)(2,1)}, bf16[136,512]{1,0:T(8,128)(2,1)S(1)}, u32[]{:S(2)}, u32[]{:S(2)}) collective-permute-start(bf16[136,512]{1,0:T(8,128)(2,1)} %get-tuple-element.92), channel_id=1, source_target_pairs={{252,0},{0,4},{4,8},{8,12},{12,16},{16,20},{20,24},{24,28},{28,32}... | collective-permute-start | bytes 417800 | tf_op jit(solution)/shard_map/ppermute | solution.py:492
  80.2 1.5 %collective-permute-start.13 = (bf16[104,512]{1,0:T(8,128)(2,1)}, bf16[104,512]{1,0:T(8,128)(2,1)S(1)}, u32[]{:S(2)}, u32[]{:S(2)}) collective-permute-start(bf16[104,512]{1,0:T(8,128)(2,1)} %get-tuple-element.93), channel_id=1, source_target_pairs={{255,0},{252,1},{253,2},{254,3},{3,4},{0,5},{1,6},{2,7},{7,8},{4,9... | collective-permute-start | bytes 319496 | tf_op jit(solution)/shard_map/ppermute | solution.py:565
  81.7 2.8 %shard_map.321.early_ref = bf16[16,64,128]{2,1,0:T(8,128)(2,1)} custom-call(bf16[16,80,768]{2,1,0:T(8,128)(2,1)} %copy-done), custom_call_target="tpu_custom_call" | custom-call | tf_op jit(solution)/shard_map/pallas_call | solution.py:506
  84.5 10.8 %all-to-all-done.1.late_ref = bf16[8,592,128]{2,1,0:T(8,128)(2,1)S(1)} async-done(((bf16[8,592,128]{2,1,0:T(8,128)(2,1)}), bf16[8,592,128]{2,1,0:T(8,128)(2,1)S(1)}, u32[]{:S(2)}, u32[]{:S(2)}) %all-to-all-start.1) | async-done | bytes 1212448 | tf_op jit(solution)/shard_map/all_to_all | solution.py:569
  95.3 1.1 copy-done.1
  96.4 2.4 %shard_map.322 = bf16[16,176,128]{2,1,0:T(8,128)(2,1)} custom-call(bf16[16,64,128]{2,1,0:T(8,128)(2,1)} %shard_map.321.early_ref, bf16[8,592,128]{2,1,0:T(8,128)(2,1)} %copy-done.1), custom_call_target="tpu_custom_call" | custom-call | tf_op jit(solution)/shard_map/pallas_call | solution.py:524
  98.8 3.7 %all-to-all-start.2 = ((bf16[16,176,128]{2,1,0:T(8,128)(2,1)}), bf16[16,176,128]{2,1,0:T(8,128)(2,1)S(1)}, u32[]{:S(2)}, u32[]{:S(2)}) async-start(bf16[16,176,128]{2,1,0:T(8,128)(2,1)} %shard_map.322), calls=%async_computation.2 | async-start | bytes 1441792 | tf_op jit(solution)/shard_map/all_to_all | solution.py:569
  102.7 0.8 reshape.104
  103.6 0.7 reshape.99
  104.3 19.0 %all-to-all-done.2.got_ref = bf16[16,176,128]{2,1,0:T(8,128)(2,1)S(1)} async-done(((bf16[16,176,128]{2,1,0:T(8,128)(2,1)}), bf16[16,176,128]{2,1,0:T(8,128)(2,1)S(1)}, u32[]{:S(2)}, u32[]{:S(2)}) %all-to-all-start.2) | async-done | bytes 720928 | tf_op jit(solution)/shard_map/all_to_all | solution.py:569
  123.4 0.9 copy-done.2
  124.2 1.8 %shard_map.324 = (f32[8,384]{1,0:T(8,128)}, f32[8,128]{1,0:T(8,128)}, f32[32,256]{1,0:T(8,128)}, f32[4,128]{1,0:T(4,128)}, f32[16,128]{1,0:T(8,128)}, /*index=5*/f32[8,759]{1,0:T(8,128)}) custom-call(bf16[16,176,128]{2,1,0:T(8,128)(2,1)} %copy-done.2), custom_call_target="tpu_custom_call" | custom-call | tf_op jit(solution)/shard_map/pallas_call | solution.py:549
  (71 shorter events, 3.5 us)
Async XLA Ops:
  1.7 15.4 %copy-start.3 = (bf16[6,48,512]{2,1,0:T(8,128)(2,1)}, bf16[6,48,512]{2,1,0:T(8,128)(2,1)S(1)}, u32[]{:S(2)}) copy-start(bf16[6,48,512]{2,1,0:T(8,128)(2,1)S(1)} %reshape.84) | copy-start | bytes 884740
  1.7 15.4 %collective-permute-start.1 = (bf16[3,24,512]{2,1,0:T(8,128)(2,1)S(1)}, bf16[3,24,512]{2,1,0:T(8,128)(2,1)S(1)}, u32[]{:S(2)}, u32[]{:S(2)}) collective-permute-start(bf16[3,24,512]{2,1,0:T(8,128)(2,1)S(1)} %get-tuple-element.107), channel_id=1, source_target_pairs={{1,0},{2,1},{3,2},{0,3},{5,4},{6,5},{7,6},{4,7},{9,8},{10,9},{11,1... | collective-permute-start | bytes 221192 | tf_op jit(solution)/shard_map/ppermute | solution.py:492
  3.5 13.7 %collective-permute-start.2 = (bf16[3,24,512]{2,1,0:T(8,128)(2,1)S(1)}, bf16[3,24,512]{2,1,0:T(8,128)(2,1)S(1)}, u32[]{:S(2)}, u32[]{:S(2)}) collective-permute-start(bf16[3,24,512]{2,1,0:T(8,128)(2,1)S(1)} %get-tuple-element.106), channel_id=1, source_target_pairs={{5,0},{6,1},{7,2},{4,3},{9,4},{10,5},{11,6},{8,7},{13,8},{14,9},{1... | collective-permute-start | bytes 221192 | tf_op jit(solution)/shard_map/ppermute | solution.py:565
  8.8 8.4 %collective-permute-start = (bf16[6,24,512]{2,1,0:T(8,128)(2,1)S(1)}, bf16[6,24,512]{2,1,0:T(8,128)(2,1)S(1)}, u32[]{:S(2)}, u32[]{:S(2)}) collective-permute-start(bf16[6,24,512]{2,1,0:T(8,128)(2,1)S(1)} %slice.48), channel_id=1, source_target_pairs={{4,0},{8,4},{12,8},{16,12},{20,16},{24,20},{28,24},{32,28},{36,32}... | collective-permute-start | bytes 442376 | tf_op jit(solution)/shard_map/ppermute | solution.py:492
  12.3 4.8 %copy-start.4 = (bf16[3,24,1024]{2,1,0:T(8,128)(2,1)}, bf16[3,24,1024]{2,1,0:T(8,128)(2,1)S(1)}, u32[]{:S(2)}) copy-start(bf16[3,24,1024]{2,1,0:T(8,128)(2,1)S(1)} %reshape.93.cot_ref) | copy-start | bytes 442372
  12.4 15.2 %collective-permute-start.6 = (bf16[2,12,1024]{2,1,0:T(8,128)(2,1)S(1)}, bf16[2,12,1024]{2,1,0:T(8,128)(2,1)S(1)}, u32[]{:S(2)}, u32[]{:S(2)}) collective-permute-start(bf16[2,12,1024]{2,1,0:T(8,128)(2,1)S(1)} %get-tuple-element.110), channel_id=1, source_target_pairs={{4,0},{8,4},{12,8},{16,12},{20,16},{24,20},{28,24},{32,28},{36,32}... | collective-permute-start | bytes 147464 | tf_op jit(solution)/shard_map/ppermute | solution.py:492
  13.4 14.1 %collective-permute-start.7 = (bf16[2,12,1024]{2,1,0:T(8,128)(2,1)S(1)}, bf16[2,12,1024]{2,1,0:T(8,128)(2,1)S(1)}, u32[]{:S(2)}, u32[]{:S(2)}) collective-permute-start(bf16[2,12,1024]{2,1,0:T(8,128)(2,1)S(1)} %get-tuple-element.109), channel_id=1, source_target_pairs={{1,0},{2,1},{3,2},{0,3},{5,4},{6,5},{7,6},{4,7},{9,8},{10,9},{11,1... | collective-permute-start | bytes 147464 | tf_op jit(solution)/shard_map/ppermute | solution.py:492
  17.1 10.5 %collective-permute-start.8 = (bf16[2,12,1024]{2,1,0:T(8,128)(2,1)S(1)}, bf16[2,12,1024]{2,1,0:T(8,128)(2,1)S(1)}, u32[]{:S(2)}, u32[]{:S(2)}) collective-permute-start(bf16[2,12,1024]{2,1,0:T(8,128)(2,1)S(1)} %get-tuple-element.108), channel_id=1, source_target_pairs={{5,0},{6,1},{7,2},{4,3},{9,4},{10,5},{11,6},{8,7},{13,8},{14,9},{1... | collective-permute-start | bytes 147464 | tf_op jit(solution)/shard_map/ppermute | solution.py:565
  17.2 0.6 copy-start.12
  17.2 0.7 copy-start.10
  24.3 5.2 %collective-permute-start.4 = (bf16[48,512]{1,0:T(8,128)(2,1)}, bf16[48,512]{1,0:T(8,128)(2,1)S(1)}, u32[]{:S(2)}, u32[]{:S(2)}) collective-permute-start(bf16[48,512]{1,0:T(8,128)(2,1)} %get-tuple-element.68), channel_id=1, source_target_pairs={{3,0},{0,1},{1,2},{2,3},{7,4},{4,5},{5,6},{6,7},{11,8},{8,9},{9,10... | collective-permute-start | bytes 147464 | tf_op jit(solution)/shard_map/ppermute | solution.py:492
  25.4 4.2 %collective-permute-start.5 = (bf16[48,512]{1,0:T(8,128)(2,1)}, bf16[48,512]{1,0:T(8,128)(2,1)S(1)}, u32[]{:S(2)}, u32[]{:S(2)}) collective-permute-start(bf16[48,512]{1,0:T(8,128)(2,1)} %get-tuple-element.69), channel_id=1, source_target_pairs={{1,0},{2,1},{3,2},{0,3},{5,4},{6,5},{7,6},{4,7},{9,8},{10,9},{11,1... | collective-permute-start | bytes 147464 | tf_op jit(solution)/shard_map/ppermute | solution.py:492
  27.6 2.1 %copy-start.13 = (bf16[2,12,1024]{2,1,0:T(8,128)(2,1)}, bf16[2,12,1024]{2,1,0:T(8,128)(2,1)S(1)}, u32[]{:S(2)}) copy-start(bf16[2,12,1024]{2,1,0:T(8,128)(2,1)S(1)} %collective-permute-done.6.cot_west_ref) | copy-start | bytes 147460
  27.6 2.1 %copy-start.14 = (bf16[2,12,1024]{2,1,0:T(8,128)(2,1)}, bf16[2,12,1024]{2,1,0:T(8,128)(2,1)S(1)}, u32[]{:S(2)}) copy-start(bf16[2,12,1024]{2,1,0:T(8,128)(2,1)S(1)} %collective-permute-done.7.cot_south_ref) | copy-start | bytes 147460
  27.6 2.0 %copy-start.15 = (bf16[2,12,1024]{2,1,0:T(8,128)(2,1)}, bf16[2,12,1024]{2,1,0:T(8,128)(2,1)S(1)}, u32[]{:S(2)}) copy-start(bf16[2,12,1024]{2,1,0:T(8,128)(2,1)S(1)} %collective-permute-done.8.cot_corner_ref) | copy-start | bytes 147460
  34.1 34.9 %all-to-all-start = ((bf16[16,80,768]{2,1,0:T(8,128)(2,1)}), bf16[16,80,768]{2,1,0:T(8,128)(2,1)S(1)}, u32[]{:S(2)}, u32[]{:S(2)}) async-start(bf16[16,80,768]{2,1,0:T(8,128)(2,1)} %get-tuple-element.86), calls=%async_computation | async-start | bytes 3932160 | tf_op jit(solution)/shard_map/all_to_all | solution.py:569
  47.9 10.7 %copy-start.7 = (bf16[288,1024]{1,0:T(8,128)(2,1)S(1)}, bf16[288,1024]{1,0:T(8,128)(2,1)}, u32[]{:S(2)}) copy-start(bf16[288,1024]{1,0:T(8,128)(2,1)} %get-tuple-element.66.rows_ref) | copy-start | bytes 1769476
  58.5 4.2 %collective-permute-start.9 = (bf16[288,1024]{1,0:T(8,128)(2,1)}, bf16[288,1024]{1,0:T(8,128)(2,1)S(1)}, u32[]{:S(2)}, u32[]{:S(2)}) collective-permute-start(bf16[288,1024]{1,0:T(8,128)(2,1)} %get-tuple-element.79), channel_id=1, source_target_pairs={{1,0},{0,1},{3,2},{2,3},{5,4},{4,5},{7,6},{6,7},{9,8},{8,9},{11,10... | collective-permute-start | bytes 1769480 | tf_op jit(solution)/shard_map/ppermute | solution.py:560
  58.7 4.2 %collective-permute-start.3 = (bf16[288,1024]{1,0:T(8,128)(2,1)S(1)}, bf16[288,1024]{1,0:T(8,128)(2,1)S(1)}, u32[]{:S(2)}, u32[]{:S(2)}) collective-permute-start(bf16[288,1024]{1,0:T(8,128)(2,1)S(1)} %copy-done.7), channel_id=1, source_target_pairs={{1,0},{0,1},{3,2},{2,3},{5,4},{4,5},{7,6},{6,7},{9,8},{8,9},{11,10... | collective-permute-start | bytes 1769480 | tf_op jit(solution)/shard_map/ppermute | solution.py:560
  62.7 1.4 %copy-start.8 = (bf16[288,1024]{1,0:T(8,128)(2,1)}, bf16[288,1024]{1,0:T(8,128)(2,1)S(1)}, u32[]{:S(2)}) copy-start(bf16[288,1024]{1,0:T(8,128)(2,1)S(1)} %collective-permute-done.9.columns_theirs_ref) | copy-start | bytes 1769476
  62.7 1.4 %collective-permute-start.10 = (f32[80,128]{1,0:T(8,128)}, f32[80,128]{1,0:T(8,128)S(1)}, u32[]{:S(2)}, u32[]{:S(2)}) collective-permute-start(f32[80,128]{1,0:T(8,128)} %shard_map.319.small_ref), channel_id=1, source_target_pairs={{1,0},{0,1},{3,2},{2,3},{5,4},{4,5},{7,6},{6,7},{9,8},{8,9},{11,10... | collective-permute-start | bytes 122888 | tf_op jit(solution)/shard_map/ppermute | solution.py:560
  62.9 1.3 %copy-start.9 = (bf16[288,1024]{1,0:T(8,128)(2,1)}, bf16[288,1024]{1,0:T(8,128)(2,1)S(1)}, u32[]{:S(2)}) copy-start(bf16[288,1024]{1,0:T(8,128)(2,1)S(1)} %collective-permute-done.3.rows_theirs_ref) | copy-start | bytes 1769476
  68.9 9.4 %copy-start = (bf16[16,80,768]{2,1,0:T(8,128)(2,1)}, bf16[16,80,768]{2,1,0:T(8,128)(2,1)S(1)}, u32[]{:S(2)}) copy-start(bf16[16,80,768]{2,1,0:T(8,128)(2,1)S(1)} %all-to-all-done.early_ref) | copy-start | bytes 5898244
  68.9 26.4 %all-to-all-start.1 = ((bf16[8,592,128]{2,1,0:T(8,128)(2,1)}), bf16[8,592,128]{2,1,0:T(8,128)(2,1)S(1)}, u32[]{:S(2)}, u32[]{:S(2)}) async-start(bf16[8,592,128]{2,1,0:T(8,128)(2,1)} %shard_map.320), calls=%async_computation.1 | async-start | bytes 2424832 | tf_op jit(solution)/shard_map/all_to_all | solution.py:569
  78.3 20.5 %collective-permute-start.12 = (bf16[136,512]{1,0:T(8,128)(2,1)}, bf16[136,512]{1,0:T(8,128)(2,1)S(1)}, u32[]{:S(2)}, u32[]{:S(2)}) collective-permute-start(bf16[136,512]{1,0:T(8,128)(2,1)} %get-tuple-element.92), channel_id=1, source_target_pairs={{252,0},{0,4},{4,8},{8,12},{12,16},{16,20},{20,24},{24,28},{28,32}... | collective-permute-start | bytes 417800 | tf_op jit(solution)/shard_map/ppermute | solution.py:492
  80.2 18.6 %collective-permute-start.11 = (bf16[104,512]{1,0:T(8,128)(2,1)}, bf16[104,512]{1,0:T(8,128)(2,1)S(1)}, u32[]{:S(2)}, u32[]{:S(2)}) collective-permute-start(bf16[104,512]{1,0:T(8,128)(2,1)} %get-tuple-element.91), channel_id=1, source_target_pairs={{3,0},{0,1},{1,2},{2,3},{7,4},{4,5},{5,6},{6,7},{11,8},{8,9},{9,10... | collective-permute-start | bytes 319496 | tf_op jit(solution)/shard_map/ppermute | solution.py:492
  80.2 18.6 %collective-permute-start.13 = (bf16[104,512]{1,0:T(8,128)(2,1)}, bf16[104,512]{1,0:T(8,128)(2,1)S(1)}, u32[]{:S(2)}, u32[]{:S(2)}) collective-permute-start(bf16[104,512]{1,0:T(8,128)(2,1)} %get-tuple-element.93), channel_id=1, source_target_pairs={{255,0},{252,1},{253,2},{254,3},{3,4},{0,5},{1,6},{2,7},{7,8},{4,9... | collective-permute-start | bytes 319496 | tf_op jit(solution)/shard_map/ppermute | solution.py:565
  84.5 18.1 %copy-start.6 = (bf16[32,1024]{1,0:T(8,128)(2,1)S(1)}, bf16[32,1024]{1,0:T(8,128)(2,1)}, u32[]{:S(2)}) copy-start(bf16[32,1024]{1,0:T(8,128)(2,1)} %get-tuple-element.97) | copy-start | bytes 196612
  95.3 1.1 copy-start.1
  98.8 3.9 %copy-start.5 = (bf16[72,512]{1,0:T(8,128)(2,1)S(1)}, bf16[72,512]{1,0:T(8,128)(2,1)}, u32[]{:S(2)}) copy-start(bf16[72,512]{1,0:T(8,128)(2,1)} %get-tuple-element.98) | copy-start | bytes 221188
  98.8 24.5 %all-to-all-start.2 = ((bf16[16,176,128]{2,1,0:T(8,128)(2,1)}), bf16[16,176,128]{2,1,0:T(8,128)(2,1)S(1)}, u32[]{:S(2)}, u32[]{:S(2)}) async-start(bf16[16,176,128]{2,1,0:T(8,128)(2,1)} %shard_map.322), calls=%async_computation.2 | async-start | bytes 1441792 | tf_op jit(solution)/shard_map/all_to_all | solution.py:569
  123.4 0.9 copy-start.2
  (4 other events, 2.5 us)

commit v4 on v3

--- a/solution.py
+++ b/solution.py
@@ -145,8 +145,8 @@
     low = (rest - middle.astype(F32)).astype(BF)
     spread = spread_ref[...]
     wide = mm(high, spread) + mm(middle, spread) + mm(low, spread)
-    left_ref[...] = wide[:, :128]
-    right_ref[...] = wide[:, 128:]
+    left_ref[: 8 * WIN, :] = wide[:, :128]
+    right_ref[: 8 * WIN, :] = wide[:, 128:]
     for h in range(HEADS):
         bias_ref[h, :, :128] = left_ref[pl.ds(h, WIN, stride=8), :]
         bias_ref[h, :, 128:] = right_ref[pl.ds(h, WIN, stride=8), :][:, :16]
@@ -162,7 +162,7 @@
         out_shape=shapes,
         in_specs=[pl.BlockSpec(memory_space=pltpu.SMEM)] + vmem(4),
         out_specs=vmem(2),
-        scratch_shapes=[pltpu.VMEM((8 * WIN, SPAN), F32)] + [pltpu.VMEM((8 * WIN, 128), F32)] * 2,
+        scratch_shapes=[pltpu.VMEM((8 * WIN, SPAN), F32)] + [pltpu.VMEM((8 * WIN + 8, 128), F32)] * 2,
         compiler_params=PARAMS,
         cost_estimate=cost(2_000_000_000, 4_000_000),
     )(last, table, plan("spread"), plan("apart_level"), plan("apart_north"))
@@ -373,7 +373,7 @@
 def attend_back(core, cot, x, qkv, p, wqkv, wproj, gain):
     shapes = [
         jax.ShapeDtypeStruct((TOK, 512), BF), jax.ShapeDtypeStruct((4, 128), F32),
-    ] + [jax.ShapeDtypeStruct((TOK, 1024), BF)] * 2 + [jax.ShapeDtypeStruct((8 * WIN, 128), F32)] * 2
+    ] + [jax.ShapeDtypeStruct((TOK, 1024), BF)] * 2 + [jax.ShapeDtypeStruct((8 * WIN + 8, 128), F32)] * 2
     return pl.pallas_call(
         back_kernel,
         out_shape=shapes,
@@ -418,7 +418,8 @@
     small_ref[48:64, :] = merge_gain_ref[...]
     small_ref[64:80, :] = jnp.zeros((16, 128), F32)
     small_ref[64:68, :] = norm_gain_ref[...]
-    wide_ref[...] = mm(left_ref[...].astype(BF), spread_t[:128, :]) + mm(right_ref[...].astype(BF), spread_t[128:, :])
+    left, right = left_ref[: 8 * WIN, :].astype(BF), right_ref[: 8 * WIN, :].astype(BF)
+    wide_ref[...] = mm(left, spread_t[:128, :]) + mm(right, spread_t[128:, :])
     blank = jnp.zeros((8, 512 - SPAN), F32)
     levels = []
     for l in range(2):

time: 128 us -> 128 us (level)
  no operation moved by 1% of the time
where the time goes in v4:
time: 128 us; the launch traced here: 126 us
  Pallas kernels  48.2 us (38%)
  starting transfers between devices  35.7 us (28%)
  waiting for transfers between devices  33.6 us (26%)
  local copies, waits for them, and re-layouts  7.47 us (6%)
    all_to_all x3, waiting for transfers between devices, spread_over(): return lax.all_to_all(parts, axes, 0, 0, tiled=True)  30.3 us
    all_to_all x3, starting transfers between devices, spread_over(): return lax.all_to_all(parts, axes, 0, 0, tiled=True)  17.5 us
    ppermute x8, starting transfers between devices, moved(): lax.ppermute(block, axes, [((i - distance) % count, i) for i in range(cou...  10.6 us
    pallas_call x1, Pallas kernels, attend_back(): pl.pallas_call(back_kernel, out_shape=shapes, in_specs=[pl.BlockSpec(memo...  10.6 us
    ppermute x3, starting transfers between devices, diagonal(): return lax.ppermute(block, AXES, route)  6.88 us
    pallas_call x1, Pallas kernels, attend(): pl.pallas_call(attend_kernel, out_shape=[jax.ShapeDtypeStruct(s, BF) for...  6.38 us
    pallas_call x1, Pallas kernels, merge(): pl.pallas_call(merge_kernel, out_shape=shapes, in_specs=vmem(6), out_spec...  5.28 us
    pallas_call x1, Pallas kernels, home_parts(): pl.pallas_call(home_kernel, out_shape=[jax.ShapeDtypeStruct(s, BF) for s...  4.15 us
  transfers between devices with their start and end apart: 17, of which 6 were waited for; matrix products, arithmetic and copies ran while one was open for 2% of the time, Pallas kernels for 34%

profile of v4, /device:TPU:8, one launch (start us, length us, event | category | flops | bytes accessed | tf_op | source)
XLA Modules:
  0.0 126.0 jit_solution(2816193680985764130)
XLA Ops:
  0.6 1.0 reshape.84
  1.7 1.8 %collective-permute-start.1 = (bf16[3,24,512]{2,1,0:T(8,128)(2,1)S(1)}, bf16[3,24,512]{2,1,0:T(8,128)(2,1)S(1)}, u32[]{:S(2)}, u32[]{:S(2)}) collective-permute-start(bf16[3,24,512]{2,1,0:T(8,128)(2,1)S(1)} %get-tuple-element.107), channel_id=1, source_target_pairs={{1,0},{2,1},{3,2},{0,3},{5,4},{6,5},{7,6},{4,7},{9,8},{10,9},{11,1... | collective-permute-start | bytes 221192 | tf_op jit(solution)/shard_map/ppermute | solution.py:493
  3.5 5.2 %collective-permute-start.2 = (bf16[3,24,512]{2,1,0:T(8,128)(2,1)S(1)}, bf16[3,24,512]{2,1,0:T(8,128)(2,1)S(1)}, u32[]{:S(2)}, u32[]{:S(2)}) collective-permute-start(bf16[3,24,512]{2,1,0:T(8,128)(2,1)S(1)} %get-tuple-element.106), channel_id=1, source_target_pairs={{5,0},{6,1},{7,2},{4,3},{9,4},{10,5},{11,6},{8,7},{13,8},{14,9},{1... | collective-permute-start | bytes 221192 | tf_op jit(solution)/shard_map/ppermute | solution.py:566
  8.8 2.6 %collective-permute-start = (bf16[6,24,512]{2,1,0:T(8,128)(2,1)S(1)}, bf16[6,24,512]{2,1,0:T(8,128)(2,1)S(1)}, u32[]{:S(2)}, u32[]{:S(2)}) collective-permute-start(bf16[6,24,512]{2,1,0:T(8,128)(2,1)S(1)} %slice.48), channel_id=1, source_target_pairs={{4,0},{8,4},{12,8},{16,12},{20,16},{24,20},{28,24},{32,28},{36,32}... | collective-permute-start | bytes 442376 | tf_op jit(solution)/shard_map/ppermute | solution.py:493
  11.4 0.9 reshape.93.cot_ref
  12.4 1.1 collective-permute-start.6
  13.4 3.6 %shard_map.314 = (f32[8,144,144]{2,1,0:T(8,128)}, f32[2,144,144]{2,1,0:T(8,128)}) custom-call(s32[1]{0:T(128)} %bitcast.2.last_ref, f32[8,759]{1,0:T(8,128)} %table_ref.1, bf16[384,256]{1,0:T(8,128)(2,1)} %constant.48.clone.spread_ref, bf16[144,144]{1,0:T(8,128)(2,1)} %constant.49.clone.level_ref, bf16[144,144]{1,0:T(8,128)(2,1)} %constant.50.clone.north_ref), custom_call_target="tpu_custom_call" | custom-call | flops 2000000000 | bytes 4000000 | tf_op jit(solution)/shard_map/pallas_call | solution.py:160
  17.9 6.4 %shard_map.315 = (bf16[288,512]{1,0:T(8,128)(2,1)}, bf16[288,1536]{1,0:T(8,128)(2,1)}, bf16[16,144,144]{2,1,0:T(8,128)(2,1)}, bf16[288,1024]{1,0:T(8,128)(2,1)},...) custom-call(bf16[288,512]{1,0:T(8,128)(2,1)} %bitcast.22, bf16[144,512]{1,0:T(8,128)(2,1)} %bitcast.34, ...), custom_call_target="tpu_custom_call" | custom-call | flops 4000000000 | bytes 8000000 | tf_op jit(solution)/shard_map/pallas_call | solution.py:233
  24.3 1.1 collective-permute-start.4
  25.4 2.1 %collective-permute-start.5 = (bf16[48,512]{1,0:T(8,128)(2,1)}, bf16[48,512]{1,0:T(8,128)(2,1)S(1)}, u32[]{:S(2)}, u32[]{:S(2)}) collective-permute-start(bf16[48,512]{1,0:T(8,128)(2,1)} %get-tuple-element.69), channel_id=1, source_target_pairs={{1,0},{2,1},{3,2},{0,3},{5,4},{6,5},{7,6},{4,7},{9,8},{10,9},{11,1... | collective-permute-start | bytes 147464 | tf_op jit(solution)/shard_map/ppermute | solution.py:493
  27.6 1.9 %collective-permute-done.4.prev_ref = bf16[48,512]{1,0:T(8,128)(2,1)S(1)} collective-permute-done((bf16[48,512]{1,0:T(8,128)(2,1)}, bf16[48,512]{1,0:T(8,128)(2,1)S(1)}, u32[]{:S(2)}, u32[]{:S(2)}) %collective-permute-start.4) | collective-permute-done | bytes 49184 | tf_op jit(solution)/shard_map/ppermute | solution.py:493
  30.2 3.8 %shard_map.316 = (bf16[16,80,768]{2,1,0:T(8,128)(2,1)}, f32[4,96,512]{2,1,0:T(8,128)}, f32[96,128]{1,0:T(8,128)}, bf16[96,1024]{1,0:T(8,128)(2,1)}) custom-call(bf16[288,512]{1,0:T(8,128)(2,1)} %get-tuple-element.67.block_ref, bf16[48,512]{1,0:T(8,128)(2,1)} %copy-done.16, bf16[48,512]{1,0:T(8,128)(2,1)} %copy-done.17, bf16[3,24,1024]{2,1,0:T(8,128)(2,1)} %copy-done.4, ...), custom_call_target="tpu_custom_call" | custom-call | flops 2000000000 | bytes 8000000 | tf_op jit(solution)/shard_map/pallas_call | solution.py:278
  34.0 8.6 %all-to-all-start = ((bf16[16,80,768]{2,1,0:T(8,128)(2,1)}), bf16[16,80,768]{2,1,0:T(8,128)(2,1)S(1)}, u32[]{:S(2)}, u32[]{:S(2)}) async-start(bf16[16,80,768]{2,1,0:T(8,128)(2,1)} %get-tuple-element.86), calls=%async_computation | async-start | bytes 3932160 | tf_op jit(solution)/shard_map/all_to_all | solution.py:570
  42.6 5.3 %shard_map.317 = (bf16[288,512]{1,0:T(8,128)(2,1)}, f32[16,128]{1,0:T(8,128)}) custom-call(f32[4,96,512]{2,1,0:T(8,128)} %get-tuple-element.71.hats_ref, f32[96,128]{1,0:T(8,128)} %get-tuple-element.72.scale_ref, bf16[96,1024]{1,0:T(8,128)(2,1)} %get-tuple-element.73.all_cot_ref, bf16[288,384]{1,0:T(8,128)(2,1)} %constant.63.clone.quad_t, ...), custom_call_target="tpu_custom_call" | custom-call | flops 4000000000 | bytes 16000000 | tf_op jit(solution)/shard_map/pallas_call | solution.py:308
  47.9 10.6 %shard_map.318 = (bf16[288,512]{1,0:T(8,128)(2,1)}, f32[4,128]{1,0:T(4,128)}, bf16[288,1024]{1,0:T(8,128)(2,1)}, bf16[288,1024]{1,0:T(8,128)(2,1)}, f32[1160,128]{1,0:T(8,128)}, /*index=5*/f32[1160,128]{1,0:T(8,128)}) custom-call(s32[1]{0:T(128)} %bitcast.7.core_ref, bf16[288,512]{1,0:T(8,128)(2,1)} %get-tuple-element.74.cot_ref, ...), custom_call_target="tpu_custom_call" | custom-call | flops 6000000000 | bytes 16000000 | tf_op jit(solution)/shard_map/pallas_call | solution.py:377
  59.0 3.7 %shard_map.319.small_ref = f32[80,128]{1,0:T(8,128)} custom-call(f32[1160,128]{1,0:T(8,128)} %get-tuple-element.80.left_ref, f32[1160,128]{1,0:T(8,128)} %get-tuple-element.81.right_ref, bf16[256,384]{1,0:T(8,128)(2,1)} %constant.65.clone.spread_t, f32[16,128]{1,0:T(8,128)} %get-tuple-element.82.merge_gain_ref, f32[4,128]{1,0:T(4,128)} %get-tuple-element.83.norm_gain_ref), custom_call_target="tpu_custom_call" | custom-call | flops 2000000000 | bytes 4000000 | tf_op jit(solution)/shard_map/pallas_call | solution.py:441
  62.9 1.3 %collective-permute-done.10.small_theirs_ref = f32[80,128]{1,0:T(8,128)S(1)} collective-permute-done((f32[80,128]{1,0:T(8,128)}, f32[80,128]{1,0:T(8,128)S(1)}, u32[]{:S(2)}, u32[]{:S(2)}) %collective-permute-start.10) | collective-permute-done | bytes 40992 | tf_op jit(solution)/shard_map/ppermute | solution.py:561
  64.8 3.6 %shard_map.320 = bf16[8,592,128]{2,1,0:T(8,128)(2,1)} custom-call(bf16[288,1024]{1,0:T(8,128)(2,1)} %get-tuple-element.66.rows_ref, bf16[288,1024]{1,0:T(8,128)(2,1)} %copy-done.9, bf16[288,1024]{1,0:T(8,128)(2,1)} %get-tuple-element.78.columns_ref, bf16[288,1024]{1,0:T(8,128)(2,1)} %copy-done.8, f32[80,128]{1,0:T(8,128)} %shard_map.319.small_ref, ...), custom_call_target="tpu_custom_call" | custom-call | flops 2000000000 | bytes 4000000 | tf_op jit(solution)/shard_map/pallas_call | solution.py:474
  68.9 5.2 %all-to-all-start.1 = ((bf16[8,592,128]{2,1,0:T(8,128)(2,1)}), bf16[8,592,128]{2,1,0:T(8,128)(2,1)S(1)}, u32[]{:S(2)}, u32[]{:S(2)}) async-start(bf16[8,592,128]{2,1,0:T(8,128)(2,1)} %shard_map.320), calls=%async_computation.1 | async-start | bytes 2424832 | tf_op jit(solution)/shard_map/all_to_all | solution.py:570
  74.1 4.2 %shard_map.323 = (bf16[72,512]{1,0:T(8,128)(2,1)}, bf16[32,1024]{1,0:T(8,128)(2,1)}, bf16[104,512]{1,0:T(8,128)(2,1)}, bf16[136,512]{1,0:T(8,128)(2,1)}, bf16[104,512]{1,0:T(8,128)(2,1)}) custom-call(f32[4,96,512]{2,1,0:T(8,128)} %get-tuple-element.71.hats_ref, f32[1,2048]{1,0:T(1,128)} %bitcast.33, bf16[2048,1024]{1,0:T(8,128)(2,1)} %wmerge_ref.3, ...), custom_call_target="tpu_custom_call" | custom-call | flops 1000000000 | bytes 8000000 | tf_op jit(solution)/shard_map/pallas_call | solution.py:407
  78.3 1.9 %collective-permute-start.12 = (bf16[136,512]{1,0:T(8,128)(2,1)}, bf16[136,512]{1,0:T(8,128)(2,1)S(1)}, u32[]{:S(2)}, u32[]{:S(2)}) collective-permute-start(bf16[136,512]{1,0:T(8,128)(2,1)} %get-tuple-element.92), channel_id=1, source_target_pairs={{252,0},{0,4},{4,8},{8,12},{12,16},{16,20},{20,24},{24,28},{28,32}... | collective-permute-start | bytes 417800 | tf_op jit(solution)/shard_map/ppermute | solution.py:493
  80.2 1.5 %collective-permute-start.13 = (bf16[104,512]{1,0:T(8,128)(2,1)}, bf16[104,512]{1,0:T(8,128)(2,1)S(1)}, u32[]{:S(2)}, u32[]{:S(2)}) collective-permute-start(bf16[104,512]{1,0:T(8,128)(2,1)} %get-tuple-element.93), channel_id=1, source_target_pairs={{255,0},{252,1},{253,2},{254,3},{3,4},{0,5},{1,6},{2,7},{7,8},{4,9... | collective-permute-start | bytes 319496 | tf_op jit(solution)/shard_map/ppermute | solution.py:566
  81.7 2.8 %shard_map.321.early_ref = bf16[16,64,128]{2,1,0:T(8,128)(2,1)} custom-call(bf16[16,80,768]{2,1,0:T(8,128)(2,1)} %copy-done), custom_call_target="tpu_custom_call" | custom-call | tf_op jit(solution)/shard_map/pallas_call | solution.py:507
  84.5 10.8 %all-to-all-done.1.late_ref = bf16[8,592,128]{2,1,0:T(8,128)(2,1)S(1)} async-done(((bf16[8,592,128]{2,1,0:T(8,128)(2,1)}), bf16[8,592,128]{2,1,0:T(8,128)(2,1)S(1)}, u32[]{:S(2)}, u32[]{:S(2)}) %all-to-all-start.1) | async-done | bytes 1212448 | tf_op jit(solution)/shard_map/all_to_all | solution.py:570
  95.3 1.1 copy-done.1
  96.4 2.4 %shard_map.322 = bf16[16,176,128]{2,1,0:T(8,128)(2,1)} custom-call(bf16[16,64,128]{2,1,0:T(8,128)(2,1)} %shard_map.321.early_ref, bf16[8,592,128]{2,1,0:T(8,128)(2,1)} %copy-done.1), custom_call_target="tpu_custom_call" | custom-call | tf_op jit(solution)/shard_map/pallas_call | solution.py:525
  98.8 3.7 %all-to-all-start.2 = ((bf16[16,176,128]{2,1,0:T(8,128)(2,1)}), bf16[16,176,128]{2,1,0:T(8,128)(2,1)S(1)}, u32[]{:S(2)}, u32[]{:S(2)}) async-start(bf16[16,176,128]{2,1,0:T(8,128)(2,1)} %shard_map.322), calls=%async_computation.2 | async-start | bytes 1441792 | tf_op jit(solution)/shard_map/all_to_all | solution.py:570
  102.7 0.8 reshape.104
  103.6 0.7 reshape.99
  104.3 19.0 %all-to-all-done.2.got_ref = bf16[16,176,128]{2,1,0:T(8,128)(2,1)S(1)} async-done(((bf16[16,176,128]{2,1,0:T(8,128)(2,1)}), bf16[16,176,128]{2,1,0:T(8,128)(2,1)S(1)}, u32[]{:S(2)}, u32[]{:S(2)}) %all-to-all-start.2) | async-done | bytes 720928 | tf_op jit(solution)/shard_map/all_to_all | solution.py:570
  123.3 0.9 copy-done.2
  124.2 1.8 %shard_map.324 = (f32[8,384]{1,0:T(8,128)}, f32[8,128]{1,0:T(8,128)}, f32[32,256]{1,0:T(8,128)}, f32[4,128]{1,0:T(4,128)}, f32[16,128]{1,0:T(8,128)}, /*index=5*/f32[8,759]{1,0:T(8,128)}) custom-call(bf16[16,176,128]{2,1,0:T(8,128)(2,1)} %copy-done.2), custom_call_target="tpu_custom_call" | custom-call | tf_op jit(solution)/shard_map/pallas_call | solution.py:550
  (71 shorter events, 3.5 us)
Async XLA Ops:
  1.7 15.4 %copy-start.3 = (bf16[6,48,512]{2,1,0:T(8,128)(2,1)}, bf16[6,48,512]{2,1,0:T(8,128)(2,1)S(1)}, u32[]{:S(2)}) copy-start(bf16[6,48,512]{2,1,0:T(8,128)(2,1)S(1)} %reshape.84) | copy-start | bytes 884740
  1.7 15.4 %collective-permute-start.1 = (bf16[3,24,512]{2,1,0:T(8,128)(2,1)S(1)}, bf16[3,24,512]{2,1,0:T(8,128)(2,1)S(1)}, u32[]{:S(2)}, u32[]{:S(2)}) collective-permute-start(bf16[3,24,512]{2,1,0:T(8,128)(2,1)S(1)} %get-tuple-element.107), channel_id=1, source_target_pairs={{1,0},{2,1},{3,2},{0,3},{5,4},{6,5},{7,6},{4,7},{9,8},{10,9},{11,1... | collective-permute-start | bytes 221192 | tf_op jit(solution)/shard_map/ppermute | solution.py:493
  3.5 13.7 %collective-permute-start.2 = (bf16[3,24,512]{2,1,0:T(8,128)(2,1)S(1)}, bf16[3,24,512]{2,1,0:T(8,128)(2,1)S(1)}, u32[]{:S(2)}, u32[]{:S(2)}) collective-permute-start(bf16[3,24,512]{2,1,0:T(8,128)(2,1)S(1)} %get-tuple-element.106), channel_id=1, source_target_pairs={{5,0},{6,1},{7,2},{4,3},{9,4},{10,5},{11,6},{8,7},{13,8},{14,9},{1... | collective-permute-start | bytes 221192 | tf_op jit(solution)/shard_map/ppermute | solution.py:566
  8.8 8.4 %collective-permute-start = (bf16[6,24,512]{2,1,0:T(8,128)(2,1)S(1)}, bf16[6,24,512]{2,1,0:T(8,128)(2,1)S(1)}, u32[]{:S(2)}, u32[]{:S(2)}) collective-permute-start(bf16[6,24,512]{2,1,0:T(8,128)(2,1)S(1)} %slice.48), channel_id=1, source_target_pairs={{4,0},{8,4},{12,8},{16,12},{20,16},{24,20},{28,24},{32,28},{36,32}... | collective-permute-start | bytes 442376 | tf_op jit(solution)/shard_map/ppermute | solution.py:493
  12.3 4.8 %copy-start.4 = (bf16[3,24,1024]{2,1,0:T(8,128)(2,1)}, bf16[3,24,1024]{2,1,0:T(8,128)(2,1)S(1)}, u32[]{:S(2)}) copy-start(bf16[3,24,1024]{2,1,0:T(8,128)(2,1)S(1)} %reshape.93.cot_ref) | copy-start | bytes 442372
  12.4 15.2 %collective-permute-start.6 = (bf16[2,12,1024]{2,1,0:T(8,128)(2,1)S(1)}, bf16[2,12,1024]{2,1,0:T(8,128)(2,1)S(1)}, u32[]{:S(2)}, u32[]{:S(2)}) collective-permute-start(bf16[2,12,1024]{2,1,0:T(8,128)(2,1)S(1)} %get-tuple-element.110), channel_id=1, source_target_pairs={{4,0},{8,4},{12,8},{16,12},{20,16},{24,20},{28,24},{32,28},{36,32}... | collective-permute-start | bytes 147464 | tf_op jit(solution)/shard_map/ppermute | solution.py:493
  13.4 14.1 %collective-permute-start.7 = (bf16[2,12,1024]{2,1,0:T(8,128)(2,1)S(1)}, bf16[2,12,1024]{2,1,0:T(8,128)(2,1)S(1)}, u32[]{:S(2)}, u32[]{:S(2)}) collective-permute-start(bf16[2,12,1024]{2,1,0:T(8,128)(2,1)S(1)} %get-tuple-element.109), channel_id=1, source_target_pairs={{1,0},{2,1},{3,2},{0,3},{5,4},{6,5},{7,6},{4,7},{9,8},{10,9},{11,1... | collective-permute-start | bytes 147464 | tf_op jit(solution)/shard_map/ppermute | solution.py:493
  17.1 0.6 copy-start.11
  17.1 10.4 %collective-permute-start.8 = (bf16[2,12,1024]{2,1,0:T(8,128)(2,1)S(1)}, bf16[2,12,1024]{2,1,0:T(8,128)(2,1)S(1)}, u32[]{:S(2)}, u32[]{:S(2)}) collective-permute-start(bf16[2,12,1024]{2,1,0:T(8,128)(2,1)S(1)} %get-tuple-element.108), channel_id=1, source_target_pairs={{5,0},{6,1},{7,2},{4,3},{9,4},{10,5},{11,6},{8,7},{13,8},{14,9},{1... | collective-permute-start | bytes 147464 | tf_op jit(solution)/shard_map/ppermute | solution.py:566
  17.2 0.7 copy-start.10
  24.3 5.2 %collective-permute-start.4 = (bf16[48,512]{1,0:T(8,128)(2,1)}, bf16[48,512]{1,0:T(8,128)(2,1)S(1)}, u32[]{:S(2)}, u32[]{:S(2)}) collective-permute-start(bf16[48,512]{1,0:T(8,128)(2,1)} %get-tuple-element.68), channel_id=1, source_target_pairs={{3,0},{0,1},{1,2},{2,3},{7,4},{4,5},{5,6},{6,7},{11,8},{8,9},{9,10... | collective-permute-start | bytes 147464 | tf_op jit(solution)/shard_map/ppermute | solution.py:493
  25.4 4.2 %collective-permute-start.5 = (bf16[48,512]{1,0:T(8,128)(2,1)}, bf16[48,512]{1,0:T(8,128)(2,1)S(1)}, u32[]{:S(2)}, u32[]{:S(2)}) collective-permute-start(bf16[48,512]{1,0:T(8,128)(2,1)} %get-tuple-element.69), channel_id=1, source_target_pairs={{1,0},{2,1},{3,2},{0,3},{5,4},{6,5},{7,6},{4,7},{9,8},{10,9},{11,1... | collective-permute-start | bytes 147464 | tf_op jit(solution)/shard_map/ppermute | solution.py:493
  27.5 2.1 %copy-start.13 = (bf16[2,12,1024]{2,1,0:T(8,128)(2,1)}, bf16[2,12,1024]{2,1,0:T(8,128)(2,1)S(1)}, u32[]{:S(2)}) copy-start(bf16[2,12,1024]{2,1,0:T(8,128)(2,1)S(1)} %collective-permute-done.6.cot_west_ref) | copy-start | bytes 147460
  27.5 2.1 %copy-start.14 = (bf16[2,12,1024]{2,1,0:T(8,128)(2,1)}, bf16[2,12,1024]{2,1,0:T(8,128)(2,1)S(1)}, u32[]{:S(2)}) copy-start(bf16[2,12,1024]{2,1,0:T(8,128)(2,1)S(1)} %collective-permute-done.7.cot_south_ref) | copy-start | bytes 147460
  27.6 2.0 %copy-start.15 = (bf16[2,12,1024]{2,1,0:T(8,128)(2,1)}, bf16[2,12,1024]{2,1,0:T(8,128)(2,1)S(1)}, u32[]{:S(2)}) copy-start(bf16[2,12,1024]{2,1,0:T(8,128)(2,1)S(1)} %collective-permute-done.8.cot_corner_ref) | copy-start | bytes 147460
  34.0 34.9 %all-to-all-start = ((bf16[16,80,768]{2,1,0:T(8,128)(2,1)}), bf16[16,80,768]{2,1,0:T(8,128)(2,1)S(1)}, u32[]{:S(2)}, u32[]{:S(2)}) async-start(bf16[16,80,768]{2,1,0:T(8,128)(2,1)} %get-tuple-element.86), calls=%async_computation | async-start | bytes 3932160 | tf_op jit(solution)/shard_map/all_to_all | solution.py:570
  47.9 10.8 %copy-start.7 = (bf16[288,1024]{1,0:T(8,128)(2,1)S(1)}, bf16[288,1024]{1,0:T(8,128)(2,1)}, u32[]{:S(2)}) copy-start(bf16[288,1024]{1,0:T(8,128)(2,1)} %get-tuple-element.66.rows_ref) | copy-start | bytes 1769476
  58.5 4.2 %collective-permute-start.9 = (bf16[288,1024]{1,0:T(8,128)(2,1)}, bf16[288,1024]{1,0:T(8,128)(2,1)S(1)}, u32[]{:S(2)}, u32[]{:S(2)}) collective-permute-start(bf16[288,1024]{1,0:T(8,128)(2,1)} %get-tuple-element.79), channel_id=1, source_target_pairs={{1,0},{0,1},{3,2},{2,3},{5,4},{4,5},{7,6},{6,7},{9,8},{8,9},{11,10... | collective-permute-start | bytes 1769480 | tf_op jit(solution)/shard_map/ppermute | solution.py:561
  58.6 4.2 %collective-permute-start.3 = (bf16[288,1024]{1,0:T(8,128)(2,1)S(1)}, bf16[288,1024]{1,0:T(8,128)(2,1)S(1)}, u32[]{:S(2)}, u32[]{:S(2)}) collective-permute-start(bf16[288,1024]{1,0:T(8,128)(2,1)S(1)} %copy-done.7), channel_id=1, source_target_pairs={{1,0},{0,1},{3,2},{2,3},{5,4},{4,5},{7,6},{6,7},{9,8},{8,9},{11,10... | collective-permute-start | bytes 1769480 | tf_op jit(solution)/shard_map/ppermute | solution.py:561
  62.7 1.4 %copy-start.8 = (bf16[288,1024]{1,0:T(8,128)(2,1)}, bf16[288,1024]{1,0:T(8,128)(2,1)S(1)}, u32[]{:S(2)}) copy-start(bf16[288,1024]{1,0:T(8,128)(2,1)S(1)} %collective-permute-done.9.columns_theirs_ref) | copy-start | bytes 1769476
  62.7 1.4 %collective-permute-start.10 = (f32[80,128]{1,0:T(8,128)}, f32[80,128]{1,0:T(8,128)S(1)}, u32[]{:S(2)}, u32[]{:S(2)}) collective-permute-start(f32[80,128]{1,0:T(8,128)} %shard_map.319.small_ref), channel_id=1, source_target_pairs={{1,0},{0,1},{3,2},{2,3},{5,4},{4,5},{7,6},{6,7},{9,8},{8,9},{11,10... | collective-permute-start | bytes 122888 | tf_op jit(solution)/shard_map/ppermute | solution.py:561
  62.9 1.3 %copy-start.9 = (bf16[288,1024]{1,0:T(8,128)(2,1)}, bf16[288,1024]{1,0:T(8,128)(2,1)S(1)}, u32[]{:S(2)}) copy-start(bf16[288,1024]{1,0:T(8,128)(2,1)S(1)} %collective-permute-done.3.rows_theirs_ref) | copy-start | bytes 1769476
  68.9 9.4 %copy-start = (bf16[16,80,768]{2,1,0:T(8,128)(2,1)}, bf16[16,80,768]{2,1,0:T(8,128)(2,1)S(1)}, u32[]{:S(2)}) copy-start(bf16[16,80,768]{2,1,0:T(8,128)(2,1)S(1)} %all-to-all-done.early_ref) | copy-start | bytes 5898244
  68.9 26.4 %all-to-all-start.1 = ((bf16[8,592,128]{2,1,0:T(8,128)(2,1)}), bf16[8,592,128]{2,1,0:T(8,128)(2,1)S(1)}, u32[]{:S(2)}, u32[]{:S(2)}) async-start(bf16[8,592,128]{2,1,0:T(8,128)(2,1)} %shard_map.320), calls=%async_computation.1 | async-start | bytes 2424832 | tf_op jit(solution)/shard_map/all_to_all | solution.py:570
  78.3 20.5 %collective-permute-start.12 = (bf16[136,512]{1,0:T(8,128)(2,1)}, bf16[136,512]{1,0:T(8,128)(2,1)S(1)}, u32[]{:S(2)}, u32[]{:S(2)}) collective-permute-start(bf16[136,512]{1,0:T(8,128)(2,1)} %get-tuple-element.92), channel_id=1, source_target_pairs={{252,0},{0,4},{4,8},{8,12},{12,16},{16,20},{20,24},{24,28},{28,32}... | collective-permute-start | bytes 417800 | tf_op jit(solution)/shard_map/ppermute | solution.py:493
  80.2 18.6 %collective-permute-start.11 = (bf16[104,512]{1,0:T(8,128)(2,1)}, bf16[104,512]{1,0:T(8,128)(2,1)S(1)}, u32[]{:S(2)}, u32[]{:S(2)}) collective-permute-start(bf16[104,512]{1,0:T(8,128)(2,1)} %get-tuple-element.91), channel_id=1, source_target_pairs={{3,0},{0,1},{1,2},{2,3},{7,4},{4,5},{5,6},{6,7},{11,8},{8,9},{9,10... | collective-permute-start | bytes 319496 | tf_op jit(solution)/shard_map/ppermute | solution.py:493
  80.2 18.6 %collective-permute-start.13 = (bf16[104,512]{1,0:T(8,128)(2,1)}, bf16[104,512]{1,0:T(8,128)(2,1)S(1)}, u32[]{:S(2)}, u32[]{:S(2)}) collective-permute-start(bf16[104,512]{1,0:T(8,128)(2,1)} %get-tuple-element.93), channel_id=1, source_target_pairs={{255,0},{252,1},{253,2},{254,3},{3,4},{0,5},{1,6},{2,7},{7,8},{4,9... | collective-permute-start | bytes 319496 | tf_op jit(solution)/shard_map/ppermute | solution.py:566
  84.5 18.1 %copy-start.6 = (bf16[32,1024]{1,0:T(8,128)(2,1)S(1)}, bf16[32,1024]{1,0:T(8,128)(2,1)}, u32[]{:S(2)}) copy-start(bf16[32,1024]{1,0:T(8,128)(2,1)} %get-tuple-element.97) | copy-start | bytes 196612
  95.3 1.1 copy-start.1
  98.8 3.9 %copy-start.5 = (bf16[72,512]{1,0:T(8,128)(2,1)S(1)}, bf16[72,512]{1,0:T(8,128)(2,1)}, u32[]{:S(2)}) copy-start(bf16[72,512]{1,0:T(8,128)(2,1)} %get-tuple-element.98) | copy-start | bytes 221188
  98.8 24.5 %all-to-all-start.2 = ((bf16[16,176,128]{2,1,0:T(8,128)(2,1)}), bf16[16,176,128]{2,1,0:T(8,128)(2,1)S(1)}, u32[]{:S(2)}, u32[]{:S(2)}) async-start(bf16[16,176,128]{2,1,0:T(8,128)(2,1)} %shard_map.322), calls=%async_computation.2 | async-start | bytes 1441792 | tf_op jit(solution)/shard_map/all_to_all | solution.py:570
  123.3 0.9 copy-start.2
  (4 other events, 2.5 us)
